TPU v7x, 256 devices: a whole 4x4x8 slice. The times are simulated.
256 devices in a mesh: narrow: 2 (over core), wide: 128 (over y, z, x).
Axes of the slice: x: 4, y: 4, z: 8, core: 2. Of those that a mesh axis runs over, the one named last changes fastest.
Arguments:
- embeddings: bfloat16 [196608, 4096], P(('narrow', 'wide')), may hold values from -32 to 32
- sketch_seed: int32 [4096, 256], replicated, may hold values from -1 to 1
- list_ids: int32 [196608], P(('narrow', 'wide')), may hold values from 0 to 262143, as said below
- owner_map: int32 [262144], replicated, may hold values from 0 to 255, as said below
Outputs:
- received: bfloat16 [256, 256, 12, 256], P(('narrow', 'wide'))
- received_lists: int32 [256, 256, 12], P(('narrow', 'wide'))
Inputs may be any that keep to these rules, and one draw needn't show every extreme that they name: `owner_map`: each device owns exactly 1024 lists. `list_ids`: among the rows of one device at most 12 have lists owned by one device; in every draw some owners get exactly 12 rows from every device.
All inputs are finite; a program needn't handle non-finite values.
Results may differ from a plain program's by a relative error of at most 0.0029.
The roundings to bfloat16 on the way count: a program that leaves them out, or rounds other values in their place, can miss the bound.
Values may be sent and summed in bfloat16 or wider, within the bound.
No kernel may reach another device: no remote copies, remote signals or barrier semaphores. Data moves between devices by JAX's collectives and lax.ppermute only.
A program may use at most 128 MiB of HBM per device.

v0:
```python
import functools

import jax
import jax.numpy as jnp
from jax import lax
from jax.experimental import pallas as pl
from jax.experimental.pallas import tpu as pltpu
from jax.sharding import Mesh
from jax.sharding import PartitionSpec as P

NS_STEPS = 6
BLOCK = 32
TILE = 8
ALL = ("narrow", "y", "z", "x")
PLANE = ("y", "z")
HIGHEST = lax.Precision.HIGHEST
ROW_DIMS = (((0,), (0,)), ((), ()))


def dot_f32(a, b, dims=(((1,), (0,)), ((), ()))):
    return lax.dot_general(a, b, dims, precision=HIGHEST, preferred_element_type=jnp.float32)


def invert_kernel(spot_ref, *refs):
    parts, inverse_ref, work_ref = refs[:-2], refs[-2], refs[-1]
    rank = inverse_ref.shape[0]
    height = rank // len(parts)
    row_ids = lax.broadcasted_iota(jnp.int32, (rank, rank), 0)
    col_ids = lax.broadcasted_iota(jnp.int32, (rank, rank), 1)
    for step, part_ref in enumerate(parts):
        place = lax.rem(spot_ref[0] + len(parts) - step, len(parts))
        work_ref[pl.ds(pl.multiple_of(place * height, height), height), :rank] = part_ref[...]
    work_ref[:, rank:] = (row_ids == col_ids).astype(jnp.float32)
    lane = lax.broadcasted_iota(jnp.int32, (BLOCK, 128), 1)
    row = lax.broadcasted_iota(jnp.int32, (BLOCK, 128), 0)
    panel_lane = lax.broadcasted_iota(jnp.int32, (BLOCK, rank), 1)

    def block_step(step, carry):
        start = pl.multiple_of(step * BLOCK, BLOCK)
        panel = work_ref[pl.ds(start, BLOCK), :]
        shifted = pltpu.roll(panel[:, :rank], rank - start, 1)[:, :128]
        rest = jnp.where(lane < BLOCK, shifted, (lane - BLOCK == row).astype(jnp.float32))
        done = []
        for tile in range(BLOCK // TILE):
            height = BLOCK - tile * TILE
            sub = lax.broadcasted_iota(jnp.int32, (height, 128), 0)
            columns = [
                jnp.broadcast_to(rest[:, tile * TILE + j : tile * TILE + j + 1], (height, 128))
                for j in range(TILE)
            ]
            for j in range(TILE):
                pivot = columns[j][j : j + 1, :]
                scale = lax.rsqrt(pivot)
                scale = scale * (1.5 - 0.5 * (pivot * scale) * scale)
                below = jnp.where(sub > j, columns[j] * scale, 0.0)
                lead = rest[j : j + 1, :] * scale
                done.append(lead)
                rest = rest - below * lead
                for m in range(j + 1, TILE):
                    columns[m] = columns[m] - below * (columns[m][j : j + 1, :] * scale)
            rest = rest[TILE:, :]
        solved = jnp.concatenate(done, axis=0)
        small = pltpu.roll(solved, 128 - BLOCK, 1)[:, :BLOCK]
        panel = dot_f32(small, panel)
        inverse_ref[pl.ds(start, BLOCK), :] = panel[:, rank:]
        later = jnp.where(panel_lane >= start + BLOCK, panel[:, :rank], 0.0)
        work_ref[...] -= dot_f32(later, panel, (((0,), (0,)), ((), ())))
        return carry

    lax.fori_loop(0, rank // BLOCK, block_step, 0)


def invert_factor(spot, parts):
    rank = parts[0].shape[1]
    return pl.pallas_call(
        invert_kernel,
        in_specs=[pl.BlockSpec(memory_space=pltpu.SMEM)]
        + [pl.BlockSpec(memory_space=pltpu.VMEM)] * len(parts),
        out_shape=jax.ShapeDtypeStruct((rank, rank), jnp.float32),
        scratch_shapes=[pltpu.VMEM((rank, 2 * rank), jnp.float32)],
        cost_estimate=pl.CostEstimate(flops=20_000_000_000, bytes_accessed=524288, transcendentals=0),
        name="invert_factor",
    )(spot, *parts)


def moment_kernel(*refs):
    total = None
    for part_ref in refs[:-1]:
        part = part_ref[...]
        term = dot_f32(part, part, ROW_DIMS)
        total = term if total is None else total + term
    refs[-1][...] = total


def moment_of(parts):
    rank = parts[0].shape[1]
    return pl.pallas_call(
        moment_kernel,
        out_shape=jax.ShapeDtypeStruct((rank, rank), jnp.float32),
        cost_estimate=pl.CostEstimate(flops=4_000_000_000, bytes_accessed=2359296, transcendentals=0),
        name="moment_of",
    )(*parts)


def whiten_kernel(spot_ref, inverse_ref, moment_ref, other_ref, *refs):
    parts, out_ref = refs[:-1], refs[-1]
    inverse = inverse_ref[...]
    rank = inverse.shape[0]
    moment = moment_ref[...] + other_ref[...]
    cov_total = dot_f32(dot_f32(inverse, moment), inverse, (((1,), (1,)), ((), ())))
    row_ids = lax.broadcasted_iota(jnp.int32, (rank, rank), 0)
    col_ids = lax.broadcasted_iota(jnp.int32, (rank, rank), 1)
    eye_matrix = (row_ids == col_ids).astype(jnp.float32)
    trace_value = jnp.sum(cov_total * eye_matrix, axis=(0, 1), keepdims=True)
    left_iter = cov_total / trace_value
    right_iter = 1.5 * eye_matrix - 0.5 * left_iter
    left_iter = dot_f32(left_iter, right_iter)
    for step_index in range(1, NS_STEPS):
        middle = 1.5 * eye_matrix - 0.5 * dot_f32(right_iter, left_iter)
        if step_index < NS_STEPS - 1:
            left_iter = dot_f32(left_iter, middle)
        right_iter = dot_f32(middle, right_iter)
    factor = right_iter / jnp.sqrt(trace_value)
    weight = dot_f32(inverse, factor, ROW_DIMS)
    height = out_ref.shape[0] // len(parts)
    for step, part_ref in enumerate(parts):
        place = lax.rem(spot_ref[0] + len(parts) - step, len(parts))
        rows = pl.ds(pl.multiple_of(place * height, height), height)
        out_ref[rows, :] = dot_f32(part_ref[...], weight).astype(jnp.bfloat16)


def project_half(spot, inverse, moment, other, parts):
    chunk, rank = parts[0].shape
    return pl.pallas_call(
        whiten_kernel,
        in_specs=[pl.BlockSpec(memory_space=pltpu.SMEM)]
        + [pl.BlockSpec(memory_space=pltpu.VMEM)] * (3 + len(parts)),
        out_shape=jax.ShapeDtypeStruct((chunk * len(parts), rank), jnp.bfloat16),
        cost_estimate=pl.CostEstimate(flops=12_000_000_000, bytes_accessed=4194304, transcendentals=0),
        name="project_half",
    )(spot, inverse, moment, other, *parts)


def cross_kernel(half_ref, rows_ref, sketch_ref, cross_ref, *rest):
    sketch = sketch_ref[...]
    cross_ref[...] = lax.dot_general(
        rows_ref[...], sketch, ROW_DIMS, preferred_element_type=jnp.float32
    )
    if rest:

        @pl.when(pl.program_id(0) == 0)
        def _():
            rest[0][...] = lax.dot_general(
                sketch, sketch, ROW_DIMS, preferred_element_type=jnp.float32
            )


def cross_of_half(half, embeddings, sketch, with_gram):
    depth, dim = embeddings.shape
    rank = sketch.shape[1]
    width, steps = 512, dim // 2 // 512
    out_shape = [jax.ShapeDtypeStruct((dim // 2, rank), jnp.float32)]
    out_specs = [pl.BlockSpec((width, rank), lambda i, half: (i, 0))]
    if with_gram:
        out_shape.append(jax.ShapeDtypeStruct((rank, rank), jnp.float32))
        out_specs.append(pl.BlockSpec((rank, rank), lambda i, half: (0, 0)))
    return pl.pallas_call(
        cross_kernel,
        grid_spec=pltpu.PrefetchScalarGridSpec(
            num_scalar_prefetch=1,
            grid=(steps,),
            in_specs=[
                pl.BlockSpec((depth, width), lambda i, half: (0, half[0] * steps + i)),
                pl.BlockSpec((depth, rank), lambda i, half: (0, 0)),
            ],
            out_specs=out_specs,
        ),
        out_shape=out_shape,
        cost_estimate=pl.CostEstimate(
            flops=depth * dim * rank, bytes_accessed=depth * dim + dim * rank * 2, transcendentals=0
        ),
        name="cross_of_half",
    )(half, embeddings, sketch)


def product_kernel(half_ref, rows_ref, basis_ref, *refs):
    begin_ref, out_ref, sum_ref = (None,) * (3 - len(refs)) + refs
    step = pl.program_id(0)
    term = jnp.dot(rows_ref[...], basis_ref[...], preferred_element_type=jnp.float32)

    @pl.when(step == 0)
    def _():
        sum_ref[...] = term if begin_ref is None else term + begin_ref[...]

    @pl.when(step > 0)
    def _():
        sum_ref[...] += term

    @pl.when(step == pl.num_programs(0) - 1)
    def _():
        out_ref[...] = sum_ref[...].astype(out_ref.dtype)


def product_of_half(half, embeddings, basis, begin, out_type):
    depth, dim = embeddings.shape
    rank = basis.shape[1]
    width, steps = 512, dim // 2 // 512
    whole = pl.BlockSpec((depth, rank), lambda i, half: (0, 0))
    extra = [] if begin is None else [begin]
    return pl.pallas_call(
        product_kernel,
        grid_spec=pltpu.PrefetchScalarGridSpec(
            num_scalar_prefetch=1,
            grid=(steps,),
            in_specs=[
                pl.BlockSpec((depth, width), lambda i, half: (0, half[0] * steps + i)),
                pl.BlockSpec((width, rank), lambda i, half: (i, 0)),
            ]
            + [whole] * len(extra),
            out_specs=whole,
            scratch_shapes=[pltpu.VMEM((depth, rank), jnp.float32)],
        ),
        out_shape=jax.ShapeDtypeStruct((depth, rank), out_type),
        cost_estimate=pl.CostEstimate(
            flops=depth * dim * rank, bytes_accessed=depth * dim + dim * rank, transcendentals=0
        ),
        name="product_of_half",
    )(half, embeddings, basis, *extra)


def pack_kernel(keep_ref, got_ref, gram_ref, gram_got_ref, out_ref):
    count, _, rank = out_ref.shape
    cross = keep_ref[...] + got_ref[...]
    gram = gram_ref[...] + gram_got_ref[...]
    pieces = [cross.reshape(count, -1, rank)]
    for term in range(3):
        short = gram.astype(jnp.bfloat16).astype(jnp.float32)
        pieces.append(short.reshape(count, -1, rank))
        gram = gram - short
    filled = sum(p.shape[1] for p in pieces)
    pieces.append(jnp.zeros((count, out_ref.shape[1] - filled, rank), jnp.float32))
    out_ref[...] = jnp.concatenate(pieces, axis=1).astype(jnp.bfloat16)


def pack_partials(keep, got, gram, gram_got, chips):
    half, rank = keep.shape
    steps = 8
    rows = half // chips + 3 * rank // chips
    rows += -rows % 8
    return pl.pallas_call(
        pack_kernel,
        grid=(steps,),
        in_specs=[pl.BlockSpec((half // steps, rank), lambda i: (i, 0))] * 2
        + [pl.BlockSpec((rank // steps, rank), lambda i: (i, 0))] * 2,
        out_specs=pl.BlockSpec((chips // steps, rows, rank), lambda i: (i, 0, 0)),
        out_shape=jax.ShapeDtypeStruct((chips, rows, rank), jnp.bfloat16),
        cost_estimate=pl.CostEstimate(flops=4000000, bytes_accessed=6000000, transcendentals=0),
        name="pack_partials",
    )(keep, got, gram, gram_got)


def total_kernel(piece, gram_piece, parts_ref, out_ref):
    total = jnp.sum(parts_ref[...].astype(jnp.float32), axis=0)
    gram = sum(total[piece + t * gram_piece : piece + (t + 1) * gram_piece] for t in range(3))
    fill = jnp.zeros((out_ref.shape[1] - piece - gram_piece, total.shape[1]), jnp.float32)
    mine = jnp.concatenate([total[:piece], gram, fill], axis=0)
    out_ref[...] = jnp.broadcast_to(mine[None], out_ref.shape)


def total_partials(parts, piece, gram_piece, copies):
    rows = piece + gram_piece
    rows += -rows % 8
    return pl.pallas_call(
        functools.partial(total_kernel, piece, gram_piece),
        out_shape=jax.ShapeDtypeStruct((copies, rows, parts.shape[2]), jnp.float32),
        cost_estimate=pl.CostEstimate(flops=1000000, bytes_accessed=1600000, transcendentals=0),
        name="total_partials",
    )(parts)


def place_kernel(target_ref, first_ref, second_ref, out_ref):
    tile = out_ref.shape[0]
    base = pl.program_id(0) * tile
    depth = first_ref.shape[0]
    slots = base + lax.broadcasted_iota(jnp.int32, (tile, depth), 0)
    total = None
    for part, rows_ref in enumerate((first_ref, second_ref)):
        onehot = (slots == target_ref[part : part + 1, :]).astype(jnp.bfloat16)
        term = jnp.dot(onehot, rows_ref[...], preferred_element_type=jnp.float32)
        total = term if total is None else total + term
    out_ref[...] = total.astype(jnp.bfloat16)


def place_rows(target, first, second, count):
    tile = 512
    depth, width = first.shape
    return pl.pallas_call(
        place_kernel,
        grid=(count // tile,),
        in_specs=[pl.BlockSpec((2, depth), lambda i: (0, 0))]
        + [pl.BlockSpec((depth, width), lambda i: (0, 0))] * 2,
        out_specs=pl.BlockSpec((tile, width), lambda i: (i, 0)),
        out_shape=jax.ShapeDtypeStruct((count, width), jnp.bfloat16),
        cost_estimate=pl.CostEstimate(
            flops=4 * count * depth * width, bytes_accessed=4 * count * width, transcendentals=0
        ),
        name="place_rows",
    )(target, first, second)


def shift(value, axis, step):
    size = lax.axis_size(axis)
    return lax.ppermute(value, axis, [(i, (i + step) % size) for i in range(size)])


def local(embeddings, sketch_seed, list_ids, owner_map):
    row_count, dim = embeddings.shape
    rank = sketch_seed.shape[1]
    cores, line = lax.axis_size("narrow"), lax.axis_size("x")
    plane = lax.axis_size("y") * lax.axis_size("z")
    chips = plane * line
    dev_count = cores * chips
    core = lax.axis_index("narrow")
    spot = lax.axis_index("x").reshape(1)
    own_half, other_half = core.reshape(1), (1 - core).reshape(1)
    piece, gram_piece = dim // dev_count, rank // chips
    seed_matrix = sketch_seed.astype(jnp.bfloat16)
    sketch = jnp.dot(embeddings, seed_matrix, preferred_element_type=jnp.float32).astype(
        jnp.bfloat16
    )

    give, gram_part = cross_of_half(other_half, embeddings, sketch, True)
    got, gram_got = shift(give, "narrow", 1), shift(gram_part, "narrow", 1)
    (keep,) = cross_of_half(own_half, embeddings, sketch, False)
    packed = pack_partials(keep, got, gram_part, gram_got, chips)
    packed = lax.all_to_all(packed, ("x", "y", "z"), 0, 0, tiled=True)

    packed = total_partials(packed, piece, gram_piece, plane)
    packed = lax.all_to_all(packed, PLANE, 0, 0, tiled=True)
    gram_line = packed[:, piece : piece + gram_piece].reshape(-1, rank)
    gram_parts = [gram_line] + [shift(gram_line, "x", step) for step in range(1, line)]
    packed, gram_parts[1] = lax.optimization_barrier((packed, gram_parts[1]))
    cross_line = packed[:, :piece].reshape(-1, rank)
    cross_parts = [cross_line] + [shift(cross_line, "x", step) for step in range(1, line)]

    capacity = 4 * row_count // dev_count
    owners = owner_map[list_ids]
    onehot = owners[:, None] == jnp.arange(dev_count, dtype=jnp.int32)[None, :]
    ids = jnp.arange(row_count, dtype=jnp.int32)
    earlier = (ids[:, None] > ids[None, :]).astype(jnp.bfloat16)
    before = jnp.dot(earlier, onehot.astype(jnp.bfloat16), preferred_element_type=jnp.float32)
    slot_index = jnp.sum(jnp.where(onehot, before, 0.0), axis=1).astype(jnp.int32)
    dest_index = owners * capacity + slot_index

    labels = jnp.full((dev_count * capacity,), -1, jnp.int32).at[dest_index].set(list_ids)
    labels = labels.reshape(dev_count, capacity)
    arrived_labels = lax.all_to_all(labels, ALL, 0, 0, tiled=True)

    both_dest = jnp.stack([dest_index, shift(dest_index, "narrow", 1)])
    both_owner = both_dest // capacity
    source = jnp.stack([core, 1 - core])[:, None]
    target = ((both_owner % chips) * cores + source) * capacity + both_dest % capacity
    target = jnp.where(both_owner // chips == core, target, -1)

    inverse = invert_factor(spot, gram_parts)
    moment = moment_of(cross_parts)
    basis = project_half(spot, inverse, moment, shift(moment, "narrow", 1), cross_parts)
    other_basis = shift(basis, "narrow", 1)
    begun = product_of_half(own_half, embeddings, basis, None, jnp.float32)
    reduced = product_of_half(other_half, embeddings, other_basis, begun, jnp.bfloat16)
    send_rows = place_rows(
        target, reduced, shift(reduced, "narrow", 1), chips * cores * capacity
    )
    send_rows = send_rows.reshape(chips, cores * capacity, rank)
    arrived = lax.all_to_all(send_rows, ("y", "z", "x"), 0, 0, tiled=True)
    arrived = arrived.reshape(chips, cores, capacity, rank).transpose(1, 0, 2, 3)
    return (
        arrived.reshape(1, dev_count, capacity, rank),
        arrived_labels.reshape(1, dev_count, capacity),
    )


def solution(mesh):
    grid = Mesh(mesh.devices.reshape(2, 4, 8, 4), ALL)
    in_specs = (P(ALL, None), P(), P(ALL), P())
    out_specs = (P(ALL, None, None, None), P(ALL, None, None))
    return jax.shard_map(local, mesh=grid, in_specs=in_specs, out_specs=out_specs, check_vma=False)
```

profile of v0, /device:TPU:32, one launch (start us, length us, event | category | flops | bytes accessed | tf_op | source)
XLA Modules:
  0.0 271.1 jit_solution(10407960804139370400)
XLA Ops:
  0.7 6.6 %fusion.4.sketch_ref = bf16[768,256]{1,0:T(8,128)(2,1)} fusion(bf16[768,4096]{1,0:T(8,128)(2,1)} %rows_ref.7, s32[4096,256]{1,0:T(8,128)} %param.5), kind=kOutput, calls=%fused_computation.7 | convolution fusion | flops 1611857920 | bytes 10878976 | tf_op jit(solution)/shard_map/dot_general | solution.py:328
  7.3 5.3 %cross_of_half.3 = (f32[2048,256]{1,0:T(8,128)}, f32[256,256]{1,0:T(8,128)}) custom-call(s32[1]{0:T(128)} %bitcast.1.half_ref, bf16[768,4096]{1,0:T(8,128)(2,1)} %rows_ref.7, bf16[768,256]{1,0:T(8,128)(2,1)} %fusion.4.sketch_ref), custom_call_target="tpu_custom_call" | custom-call | flops 805306368 | bytes 5242880 | tf_op jit(solution)/shard_map/cross_of_half/pallas_call | solution.py:167
  13.1 4.9 %cross_of_half.2.keep_ref = f32[2048,256]{1,0:T(8,128)} custom-call(s32[1]{0:T(128)} %bitcast.half_ref, bf16[768,4096]{1,0:T(8,128)(2,1)} %rows_ref.7, bf16[768,256]{1,0:T(8,128)(2,1)} %fusion.4.sketch_ref), custom_call_target="tpu_custom_call" | custom-call | flops 805306368 | bytes 5242880 | tf_op jit(solution)/shard_map/cross_of_half/pallas_call | solution.py:167
  18.7 1.3 copy-done.1
  20.0 6.1 %pack_partials.1 = bf16[128,24,256]{2,1,0:T(8,128)(2,1)} custom-call(f32[2048,256]{1,0:T(8,128)} %cross_of_half.2.keep_ref, f32[2048,256]{1,0:T(8,128)} %copy-done.1, f32[256,256]{1,0:T(8,128)} %get-tuple-element.7.gram_ref, f32[256,256]{1,0:T(8,128)} %copy-done.4), custom_call_target="tpu_custom_call" | custom-call | flops 4000000 | bytes 6000000 | tf_op jit(solution)/shard_map/pack_partials/pallas_call | solution.py:250
  26.1 57.9 %all_to_all.24.parts_ref = bf16[128,24,256]{2,1,0:T(8,128)(2,1)} all-to-all(bf16[128,24,256]{2,1,0:T(8,128)(2,1)} %pack_partials.1), channel_id=1, replica_groups=mesh['narrow'=2,'y'=4,'z'=8,'x'=4] {'x','y','z'}, dimensions={0} | all-to-all | bytes 3145728 | tf_op jit(solution)/shard_map/all_to_all | solution.py:336
  84.0 2.6 total_partials.1
  86.6 27.0 %all_to_all.25 = f32[32,24,256]{2,1,0:T(8,128)S(1)} all-to-all(f32[32,24,256]{2,1,0:T(8,128)} %total_partials.1), channel_id=1, replica_groups=mesh['narrow'=2,'y'=4,'z'=8,'x'=4] {'y','z'}, dimensions={0} | all-to-all | bytes 1572864 | tf_op jit(solution)/shard_map/all_to_all | solution.py:339
  113.8 6.1 %collective-permute-done.3.refs_1_ = f32[64,256]{1,0:T(8,128)S(1)} collective-permute-done((f32[64,256]{1,0:T(8,128)S(1)}, f32[64,256]{1,0:T(8,128)S(1)}, u32[]{:S(2)}, u32[]{:S(2)}) %collective-permute-start.3) | collective-permute-done | bytes 65568 | tf_op jit(solution)/shard_map/ppermute | solution.py:313
  121.1 2.2 collective-permute-start.8
  123.3 2.9 %collective-permute-start.4 = (f32[64,256]{1,0:T(8,128)S(1)}, f32[64,256]{1,0:T(8,128)S(1)}, u32[]{:S(2)}, u32[]{:S(2)}) collective-permute-start(f32[64,256]{1,0:T(8,128)S(1)} %reshape.86.refs_0_), channel_id=1, source_target_pairs={{0,2},{1,3},{2,0},{3,1},{4,6},{5,7},{6,4},{7,5},{8,10},{9,11},{10,... | collective-permute-start | bytes 196616 | tf_op jit(solution)/shard_map/ppermute | solution.py:313
  126.8 15.7 %collective-permute-done.6.refs_1_ = f32[512,256]{1,0:T(8,128)S(1)} collective-permute-done((f32[512,256]{1,0:T(8,128)S(1)}, f32[512,256]{1,0:T(8,128)S(1)}, u32[]{:S(2)}, u32[]{:S(2)}) %collective-permute-start.6) | collective-permute-done | bytes 524320 | tf_op jit(solution)/shard_map/ppermute | solution.py:313
  144.3 4.3 %moment_of.1.moment_ref = f32[256,256]{1,0:T(8,128)} custom-call(f32[512,256]{1,0:T(8,128)} %bitcast.18, f32[512,256]{1,0:T(8,128)} %copy-done.7, f32[512,256]{1,0:T(8,128)} %copy-done.8, f32[512,256]{1,0:T(8,128)} %copy-done.9), custom_call_target="tpu_custom_call" | custom-call | flops 4000000000 | bytes 2359296 | tf_op jit(solution)/shard_map/moment_of/pallas_call | solution.py:97
  149.3 15.8 %invert_factor.1.inverse_ref = f32[256,256]{1,0:T(8,128)} custom-call(s32[1]{0:T(128)} %bitcast.2.spot_ref, f32[64,256]{1,0:T(8,128)} %copy-done.5, f32[64,256]{1,0:T(8,128)} %copy-done.12, f32[64,256]{1,0:T(8,128)} %copy-done.13, f32[64,256]{1,0:T(8,128)} %copy-done.14), custom_call_target="tpu_custom_call" | custom-call | flops 20000000000 | bytes 524288 | tf_op jit(solution)/shard_map/invert_factor/pallas_call | solution.py:75
  165.8 12.2 %project_half.1.basis_ref = bf16[2048,256]{1,0:T(8,128)(2,1)} custom-call(s32[1]{0:T(128)} %bitcast.2.spot_ref, f32[256,256]{1,0:T(8,128)} %invert_factor.1.inverse_ref, f32[256,256]{1,0:T(8,128)} %moment_of.1.moment_ref, f32[256,256]{1,0:T(8,128)} %copy-done.11, f32[512,256]{1,0:T(8,128)} %bitcast.19, f32[512,256]{1,0:T(8,128)} %copy-done.7, ...), custom_call_target="tpu_custom_call" | custom-call | flops 12000000000 | bytes 4194304 | tf_op jit(solution)/shard_map/project_half/pallas_call | solution.py:134
  178.6 4.5 %gather_fusion = s32[768]{0:T(1024)S(1)} fusion(s32[262144]{0:T(1024)S(1)} %copy-done, s32[1024]{0:T(1024)S(1)} %pad_clamp_fusion), kind=kCustom, calls=%fused_computation | custom fusion | bytes 9216 | tf_op jit(solution)/shard_map/gather | solution.py:347
  183.5 4.7 %product_of_half.2.refs_0_ = f32[768,256]{1,0:T(8,128)} custom-call(s32[1]{0:T(128)} %bitcast.half_ref, bf16[768,4096]{1,0:T(8,128)(2,1)} %rows_ref.7, bf16[2048,256]{1,0:T(8,128)(2,1)} %project_half.1.basis_ref), custom_call_target="tpu_custom_call" | custom-call | flops 805306368 | bytes 4194304 | tf_op jit(solution)/shard_map/product_of_half/pallas_call | solution.py:210
  189.2 4.9 %product_of_half.3.first_ref = bf16[768,256]{1,0:T(8,128)(2,1)} custom-call(s32[1]{0:T(128)} %bitcast.1.half_ref, bf16[768,4096]{1,0:T(8,128)(2,1)} %rows_ref.7, bf16[2048,256]{1,0:T(8,128)(2,1)} %copy-done.2, f32[768,256]{1,0:T(8,128)} %product_of_half.2.refs_0_), custom_call_target="tpu_custom_call" | custom-call | flops 805306368 | bytes 4194304 | tf_op jit(solution)/shard_map/product_of_half/pallas_call | solution.py:210
  194.7 3.4 %scatter_custom_fusion = s32[3072]{0:T(1024)S(1)} fusion(s32[768]{0:T(1024)S(1)} %fusion.13, s32[768]{0:T(1024)S(1)} %copy-done.6, s32[]{:T(128)} %constant.55.clone.1), kind=kCustom, calls=%fused_computation.24 | custom fusion | bytes 12292 | tf_op jit(solution)/shard_map/scatter | solution.py:355
  198.9 7.5 %all-to-all-start.3 = ((s32[256,1,12]{2,1,0:T(1,128)}), s32[256,1,12]{2,1,0:T(1,128)S(1)}, u32[]{:S(2)}, u32[]{:S(2)}) async-start(s32[256,1,12]{2,1,0:T(1,128)} %bitcast.8), calls=%async_computation.3 | async-start | bytes 262144 | tf_op jit(solution)/shard_map/all_to_all | solution.py:357
  207.9 5.6 %place_rows.1 = bf16[3072,256]{1,0:T(8,128)(2,1)} custom-call(s32[2,768]{1,0:T(2,128)} %compare_select_fusion.1.target_ref, bf16[768,256]{1,0:T(8,128)(2,1)} %product_of_half.3.first_ref, bf16[768,256]{1,0:T(8,128)(2,1)} %copy-done.10), custom_call_target="tpu_custom_call" | custom-call | flops 2415919104 | bytes 3145728 | tf_op jit(solution)/shard_map/place_rows/pallas_call | solution.py:297
  213.5 5.7 %all-to-all-done.3 = s32[256,1,12]{2,1,0:T(1,128)S(1)} async-done(((s32[256,1,12]{2,1,0:T(1,128)}), s32[256,1,12]{2,1,0:T(1,128)S(1)}, u32[]{:S(2)}, u32[]{:S(2)}) %all-to-all-start.3) | async-done | bytes 12320 | tf_op jit(solution)/shard_map/all_to_all | solution.py:357
  219.2 8.6 %all-to-all-start.2 = ((bf16[128,24,256]{2,1,0:T(8,128)(2,1)}), bf16[128,24,256]{2,1,0:T(8,128)(2,1)S(1)}, u32[]{:S(2)}, u32[]{:S(2)}) async-start(bf16[128,24,256]{2,1,0:T(8,128)(2,1)} %bitcast.13), calls=%async_computation.2 | async-start | bytes 3145728 | tf_op jit(solution)/shard_map/all_to_all | solution.py:375
  228.5 41.0 %all-to-all-done.2 = bf16[128,24,256]{2,1,0:T(8,128)(2,1)S(1)} async-done(((bf16[128,24,256]{2,1,0:T(8,128)(2,1)}), bf16[128,24,256]{2,1,0:T(8,128)(2,1)S(1)}, u32[]{:S(2)}, u32[]{:S(2)}) %all-to-all-start.2) | async-done | bytes 1572896 | tf_op jit(solution)/shard_map/all_to_all | solution.py:375
  (65 shorter events, 13.4 us)
Async XLA Ops:
  0.6 177.9 %copy-start = (s32[262144]{0:T(1024)S(1)}, s32[262144]{0:T(1024)}, u32[]{:S(2)}) copy-start(s32[262144]{0:T(1024)} %param.7) | copy-start | bytes 3145732
  12.5 5.4 %collective-permute-start.1 = (f32[2048,256]{1,0:T(8,128)}, f32[2048,256]{1,0:T(8,128)S(1)}, u32[]{:S(2)}, u32[]{:S(2)}) collective-permute-start(f32[2048,256]{1,0:T(8,128)} %get-tuple-element.6), channel_id=1, source_target_pairs={{0,128},{128,0},{1,129},{129,1},{2,130},{130,2},{3,131},{131,3},{4... | collective-permute-start | bytes 6291464 | tf_op jit(solution)/shard_map/ppermute | solution.py:313
  12.6 5.4 %collective-permute-start.2 = (f32[256,256]{1,0:T(8,128)}, f32[256,256]{1,0:T(8,128)S(1)}, u32[]{:S(2)}, u32[]{:S(2)}) collective-permute-start(f32[256,256]{1,0:T(8,128)} %get-tuple-element.7.gram_ref), channel_id=1, source_target_pairs={{0,128},{128,0},{1,129},{129,1},{2,130},{130,2},{3,131},{131,3},{4... | collective-permute-start | bytes 786440 | tf_op jit(solution)/shard_map/ppermute | solution.py:313
  18.7 1.3 copy-start.1
  113.7 35.0 %copy-start.5 = (f32[64,256]{1,0:T(8,128)}, f32[64,256]{1,0:T(8,128)S(1)}, u32[]{:S(2)}) copy-start(f32[64,256]{1,0:T(8,128)S(1)} %reshape.86.refs_0_) | copy-start | bytes 196612
  113.7 6.2 %collective-permute-start.3 = (f32[64,256]{1,0:T(8,128)S(1)}, f32[64,256]{1,0:T(8,128)S(1)}, u32[]{:S(2)}, u32[]{:S(2)}) collective-permute-start(f32[64,256]{1,0:T(8,128)S(1)} %reshape.86.refs_0_), channel_id=1, source_target_pairs={{0,1},{1,2},{2,3},{3,0},{4,5},{5,6},{6,7},{7,4},{8,9},{9,10},{10,1... | collective-permute-start | bytes 196616 | tf_op jit(solution)/shard_map/ppermute | solution.py:313
  119.9 28.8 %copy-start.12 = (f32[64,256]{1,0:T(8,128)}, f32[64,256]{1,0:T(8,128)S(1)}, u32[]{:S(2)}) copy-start(f32[64,256]{1,0:T(8,128)S(1)} %collective-permute-done.3.refs_1_) | copy-start | bytes 196612
  120.0 22.6 %copy-start.3 = (f32[32,16,256]{2,1,0:T(8,128)}, f32[32,16,256]{2,1,0:T(8,128)S(1)}, u32[]{:S(2)}) copy-start(f32[32,16,256]{2,1,0:T(8,128)S(1)} %slice.7) | copy-start | bytes 1572868
  120.0 22.5 %collective-permute-start.6 = (f32[512,256]{1,0:T(8,128)S(1)}, f32[512,256]{1,0:T(8,128)S(1)}, u32[]{:S(2)}, u32[]{:S(2)}) collective-permute-start(f32[512,256]{1,0:T(8,128)S(1)} %bitcast.15), channel_id=1, source_target_pairs={{0,1},{1,2},{2,3},{3,0},{4,5},{5,6},{6,7},{7,4},{8,9},{9,10},{10,1... | collective-permute-start | bytes 1572872 | tf_op jit(solution)/shard_map/ppermute | solution.py:313
  120.1 22.5 %collective-permute-start.7 = (f32[512,256]{1,0:T(8,128)S(1)}, f32[512,256]{1,0:T(8,128)S(1)}, u32[]{:S(2)}, u32[]{:S(2)}) collective-permute-start(f32[512,256]{1,0:T(8,128)S(1)} %bitcast.16), channel_id=1, source_target_pairs={{0,2},{1,3},{2,0},{3,1},{4,6},{5,7},{6,4},{7,5},{8,10},{9,11},{10,... | collective-permute-start | bytes 1572872 | tf_op jit(solution)/shard_map/ppermute | solution.py:313
  121.1 21.5 %collective-permute-start.8 = (f32[512,256]{1,0:T(8,128)S(1)}, f32[512,256]{1,0:T(8,128)S(1)}, u32[]{:S(2)}, u32[]{:S(2)}) collective-permute-start(f32[512,256]{1,0:T(8,128)S(1)} %bitcast.17), channel_id=1, source_target_pairs={{0,3},{1,0},{2,1},{3,2},{4,7},{5,4},{6,5},{7,6},{8,11},{9,8},{10,9... | collective-permute-start | bytes 1572872 | tf_op jit(solution)/shard_map/ppermute | solution.py:313
  123.3 25.4 %collective-permute-start.4 = (f32[64,256]{1,0:T(8,128)S(1)}, f32[64,256]{1,0:T(8,128)S(1)}, u32[]{:S(2)}, u32[]{:S(2)}) collective-permute-start(f32[64,256]{1,0:T(8,128)S(1)} %reshape.86.refs_0_), channel_id=1, source_target_pairs={{0,2},{1,3},{2,0},{3,1},{4,6},{5,7},{6,4},{7,5},{8,10},{9,11},{10,... | collective-permute-start | bytes 196616 | tf_op jit(solution)/shard_map/ppermute | solution.py:313
  126.2 22.5 %collective-permute-start.5 = (f32[64,256]{1,0:T(8,128)S(1)}, f32[64,256]{1,0:T(8,128)S(1)}, u32[]{:S(2)}, u32[]{:S(2)}) collective-permute-start(f32[64,256]{1,0:T(8,128)S(1)} %reshape.86.refs_0_), channel_id=1, source_target_pairs={{0,3},{1,0},{2,1},{3,2},{4,7},{5,4},{6,5},{7,6},{8,11},{9,8},{10,9... | collective-permute-start | bytes 196616 | tf_op jit(solution)/shard_map/ppermute | solution.py:313
  142.5 0.8 copy-start.7
  142.5 1.0 copy-start.8
  143.5 0.8 copy-start.9
  148.7 16.5 %collective-permute-start.9 = (f32[256,256]{1,0:T(8,128)}, f32[256,256]{1,0:T(8,128)S(1)}, u32[]{:S(2)}, u32[]{:S(2)}) collective-permute-start(f32[256,256]{1,0:T(8,128)} %moment_of.1.moment_ref), channel_id=1, source_target_pairs={{0,128},{128,0},{1,129},{129,1},{2,130},{130,2},{3,131},{131,3},{4... | collective-permute-start | bytes 786440 | tf_op jit(solution)/shard_map/ppermute | solution.py:313
  165.1 13.4 %copy-start.6 = (s32[768]{0:T(1024)S(1)}, s32[768]{0:T(1024)}, u32[]{:S(2)}) copy-start(s32[768]{0:T(1024)} %param.6) | copy-start | bytes 9220
  178.1 10.2 %collective-permute-start.10 = (bf16[2048,256]{1,0:T(8,128)(2,1)}, bf16[2048,256]{1,0:T(8,128)(2,1)S(1)}, u32[]{:S(2)}, u32[]{:S(2)}) collective-permute-start(bf16[2048,256]{1,0:T(8,128)(2,1)} %project_half.1.basis_ref), channel_id=1, source_target_pairs={{0,128},{128,0},{1,129},{129,1},{2,130},{130,2},{3,131},{131,3},{4... | collective-permute-start | bytes 3145736 | tf_op jit(solution)/shard_map/ppermute | solution.py:313
  188.3 1.0 copy-start.2
  194.1 13.0 %collective-permute-start.11 = (bf16[768,256]{1,0:T(8,128)(2,1)}, bf16[768,256]{1,0:T(8,128)(2,1)S(1)}, u32[]{:S(2)}, u32[]{:S(2)}) collective-permute-start(bf16[768,256]{1,0:T(8,128)(2,1)} %product_of_half.3.first_ref), channel_id=1, source_target_pairs={{0,128},{128,0},{1,129},{129,1},{2,130},{130,2},{3,131},{131,3},{4... | collective-permute-start | bytes 1179656 | tf_op jit(solution)/shard_map/ppermute | solution.py:313
  194.2 12.3 %collective-permute-start = (s32[768]{0:T(1024)S(1)}, s32[768]{0:T(1024)S(1)}, u32[]{:S(2)}, u32[]{:S(2)}) collective-permute-start(s32[768]{0:T(1024)S(1)} %convert_add_fusion), channel_id=1, source_target_pairs={{0,128},{128,0},{1,129},{129,1},{2,130},{130,2},{3,131},{131,3},{4... | collective-permute-start | bytes 9224 | tf_op jit(solution)/shard_map/ppermute | solution.py:313
  198.9 20.3 %all-to-all-start.3 = ((s32[256,1,12]{2,1,0:T(1,128)}), s32[256,1,12]{2,1,0:T(1,128)S(1)}, u32[]{:S(2)}, u32[]{:S(2)}) async-start(s32[256,1,12]{2,1,0:T(1,128)} %bitcast.8), calls=%async_computation.3 | async-start | bytes 262144 | tf_op jit(solution)/shard_map/all_to_all | solution.py:357
  219.2 50.3 %all-to-all-start.2 = ((bf16[128,24,256]{2,1,0:T(8,128)(2,1)}), bf16[128,24,256]{2,1,0:T(8,128)(2,1)S(1)}, u32[]{:S(2)}, u32[]{:S(2)}) async-start(bf16[128,24,256]{2,1,0:T(8,128)(2,1)} %bitcast.13), calls=%async_computation.2 | async-start | bytes 3145728 | tf_op jit(solution)/shard_map/all_to_all | solution.py:375
  (5 other events, 3.5 us)
where the time goes:
time: 272 us; the launch traced here: 271 us
  blocking collectives  84.9 us (31%)
  waiting for transfers between devices  68.6 us (25%)
  Pallas kernels  66.3 us (24%)
  starting transfers between devices  24.6 us (9%)
  local copies, waits for them, and re-layouts  18 us (7%)
  matrix products  7.1 us (3%)
    all_to_all x1, blocking collectives, local(): packed = lax.all_to_all(packed, ('x', 'y', 'z'), 0, 0, tiled=True)  57.9 us
    all_to_all x1, waiting for transfers between devices, local(): arrived = lax.all_to_all(send_rows, ('y', 'z', 'x'), 0, 0, tiled=True)  41 us
    all_to_all x1, blocking collectives, local(): packed = lax.all_to_all(packed, PLANE, 0, 0, tiled=True)  27 us
    ppermute x12, waiting for transfers between devices, shift(): lax.ppermute(value, axis, [(i, (i + step) % size) for i in range(size)])  21.9 us
    pallas_call x1, Pallas kernels, invert_factor(): pl.pallas_call(invert_kernel, in_specs=[pl.BlockSpec(memory_space=pltpu.S...  15.8 us
    pallas_call x1, Pallas kernels, project_half(): pl.pallas_call(whiten_kernel, in_specs=[pl.BlockSpec(memory_space=pltpu.S...  12.2 us
    pallas_call x2, Pallas kernels, cross_of_half(): pl.pallas_call(cross_kernel, grid_spec=pltpu.PrefetchScalarGridSpec(num_s...  10.1 us
    pallas_call x2, Pallas kernels, product_of_half(): pl.pallas_call(product_kernel, grid_spec=pltpu.PrefetchScalarGridSpec(num...  9.63 us
  transfers between devices with their start and end apart: 14, of which 4 were waited for; matrix products, arithmetic and copies ran while one was open for 4% of the time, Pallas kernels for 13%

commit v1 on v0

--- a/solution.py
+++ b/solution.py
@@ -19,6 +19,17 @@
 
 def dot_f32(a, b, dims=(((1,), (0,)), ((), ()))):
     return lax.dot_general(a, b, dims, precision=HIGHEST, preferred_element_type=jnp.float32)
+
+
+def split_two(a):
+    high = a.astype(jnp.bfloat16)
+    return high, (a - high.astype(jnp.float32)).astype(jnp.bfloat16)
+
+
+def dot_split(a, b):
+    (ah, al), (bh, bl) = a, b
+    mul = functools.partial(jnp.dot, preferred_element_type=jnp.float32)
+    return mul(ah, bh) + (mul(ah, bl) + mul(al, bh))
 
 
 def invert_kernel(spot_ref, *refs):
@@ -114,19 +125,21 @@
     trace_value = jnp.sum(cov_total * eye_matrix, axis=(0, 1), keepdims=True)
     left_iter = cov_total / trace_value
     right_iter = 1.5 * eye_matrix - 0.5 * left_iter
-    left_iter = dot_f32(left_iter, right_iter)
+    right_parts = split_two(right_iter)
+    left_parts = split_two(dot_split(split_two(left_iter), right_parts))
     for step_index in range(1, NS_STEPS):
-        middle = 1.5 * eye_matrix - 0.5 * dot_f32(right_iter, left_iter)
+        middle = split_two(1.5 * eye_matrix - 0.5 * dot_split(right_parts, left_parts))
+        right_iter = dot_split(middle, right_parts)
         if step_index < NS_STEPS - 1:
-            left_iter = dot_f32(left_iter, middle)
-        right_iter = dot_f32(middle, right_iter)
+            left_parts = split_two(dot_split(left_parts, middle))
+            right_parts = split_two(right_iter)
     factor = right_iter / jnp.sqrt(trace_value)
-    weight = dot_f32(inverse, factor, ROW_DIMS)
+    weight = split_two(dot_f32(inverse, factor, ROW_DIMS))
     height = out_ref.shape[0] // len(parts)
     for step, part_ref in enumerate(parts):
         place = lax.rem(spot_ref[0] + len(parts) - step, len(parts))
         rows = pl.ds(pl.multiple_of(place * height, height), height)
-        out_ref[rows, :] = dot_f32(part_ref[...], weight).astype(jnp.bfloat16)
+        out_ref[rows, :] = dot_split(split_two(part_ref[...]), weight).astype(jnp.bfloat16)
 
 
 def project_half(spot, inverse, moment, other, parts):
@@ -141,86 +154,102 @@
     )(spot, inverse, moment, other, *parts)
 
 
-def cross_kernel(half_ref, rows_ref, sketch_ref, cross_ref, *rest):
+def chunk_kernel(spot_ref, rows_ref, sketch_ref, give_ref, keep_ref):
+    chunk, core = spot_ref[0], spot_ref[1]
+    rank = sketch_ref.shape[1]
+    width = give_ref.shape[1] - 128
+    half = rows_ref.shape[1] // 2
     sketch = sketch_ref[...]
-    cross_ref[...] = lax.dot_general(
-        rows_ref[...], sketch, ROW_DIMS, preferred_element_type=jnp.float32
+    mul = functools.partial(
+        lax.dot_general, dimension_numbers=ROW_DIMS, preferred_element_type=jnp.float32
     )
-    if rest:
-
-        @pl.when(pl.program_id(0) == 0)
-        def _():
-            rest[0][...] = lax.dot_general(
-                sketch, sketch, ROW_DIMS, preferred_element_type=jnp.float32
-            )
-
-
-def cross_of_half(half, embeddings, sketch, with_gram):
+    gram = mul(sketch, sketch)
+    gram = pltpu.roll(gram, rank - chunk * (rank * width // half), 1)[:, :128]
+    for out_ref, place in ((give_ref, 1 - core), (keep_ref, core)):
+        columns = pl.ds(pl.multiple_of(place * half + chunk * width, width), width)
+        out_ref[:, :width] = mul(sketch, rows_ref[:, columns])
+        out_ref[:, width:] = gram
+
+
+def cross_chunk(spot, embeddings, sketch, chunks):
     depth, dim = embeddings.shape
     rank = sketch.shape[1]
-    width, steps = 512, dim // 2 // 512
-    out_shape = [jax.ShapeDtypeStruct((dim // 2, rank), jnp.float32)]
-    out_specs = [pl.BlockSpec((width, rank), lambda i, half: (i, 0))]
-    if with_gram:
-        out_shape.append(jax.ShapeDtypeStruct((rank, rank), jnp.float32))
-        out_specs.append(pl.BlockSpec((rank, rank), lambda i, half: (0, 0)))
-    return pl.pallas_call(
-        cross_kernel,
-        grid_spec=pltpu.PrefetchScalarGridSpec(
-            num_scalar_prefetch=1,
-            grid=(steps,),
-            in_specs=[
-                pl.BlockSpec((depth, width), lambda i, half: (0, half[0] * steps + i)),
-                pl.BlockSpec((depth, rank), lambda i, half: (0, 0)),
-            ],
-            out_specs=out_specs,
+    width = dim // 2 // chunks
+    shape = jax.ShapeDtypeStruct((rank, width + 128), jnp.float32)
+    return pl.pallas_call(
+        chunk_kernel,
+        in_specs=[pl.BlockSpec(memory_space=pltpu.SMEM)]
+        + [pl.BlockSpec(memory_space=pltpu.VMEM)] * 2,
+        out_shape=[shape, shape],
+        compiler_params=pltpu.CompilerParams(vmem_limit_bytes=32 * 2**20),
+        cost_estimate=pl.CostEstimate(
+            flops=2 * depth * rank * (2 * width + rank), bytes_accessed=3000000, transcendentals=0
         ),
-        out_shape=out_shape,
-        cost_estimate=pl.CostEstimate(
-            flops=depth * dim * rank, bytes_accessed=depth * dim + dim * rank * 2, transcendentals=0
-        ),
-        name="cross_of_half",
-    )(half, embeddings, sketch)
-
-
-def product_kernel(half_ref, rows_ref, basis_ref, *refs):
-    begin_ref, out_ref, sum_ref = (None,) * (3 - len(refs)) + refs
-    step = pl.program_id(0)
-    term = jnp.dot(rows_ref[...], basis_ref[...], preferred_element_type=jnp.float32)
-
-    @pl.when(step == 0)
-    def _():
-        sum_ref[...] = term if begin_ref is None else term + begin_ref[...]
-
-    @pl.when(step > 0)
-    def _():
-        sum_ref[...] += term
-
-    @pl.when(step == pl.num_programs(0) - 1)
-    def _():
-        out_ref[...] = sum_ref[...].astype(out_ref.dtype)
+        name="cross_chunk",
+    )(spot, embeddings, sketch)
+
+
+def line_kernel(gram_piece, *refs):
+    parts, out_ref = refs[:-1], refs[-1]
+    plane, _, rank = out_ref.shape
+    width = parts[0].shape[1] - 128
+    total = parts[0][...] + parts[1][...]
+    for part_ref in parts[2:]:
+        total = total + part_ref[...]
+    piece = width // plane
+    out_ref[:, :piece, :] = total[:, :width].T.reshape(plane, piece, rank)
+    gram = total[:, width:].T[: plane * gram_piece].reshape(plane, gram_piece, rank)
+    fill = jnp.zeros((plane, out_ref.shape[1] - piece - gram_piece, rank), jnp.float32)
+    out_ref[:, piece:, :] = jnp.concatenate([gram, fill], axis=1)
+
+
+def line_total(parts, plane, gram_piece):
+    rank, width = parts[0].shape
+    rows = (width - 128) // plane + gram_piece
+    rows += -rows % 8
+    return pl.pallas_call(
+        functools.partial(line_kernel, gram_piece),
+        out_shape=jax.ShapeDtypeStruct((plane, rows, rank), jnp.float32),
+        compiler_params=pltpu.CompilerParams(vmem_limit_bytes=32 * 2**20),
+        cost_estimate=pl.CostEstimate(flops=1000000, bytes_accessed=4000000, transcendentals=0),
+        name="line_total",
+    )(*parts)
+
+
+def plane_kernel(parts_ref, out_ref):
+    out_ref[...] = jnp.broadcast_to(jnp.sum(parts_ref[...], axis=0, keepdims=True), out_ref.shape)
+
+
+def plane_total(parts):
+    return pl.pallas_call(
+        plane_kernel,
+        out_shape=jax.ShapeDtypeStruct(parts.shape, jnp.float32),
+        cost_estimate=pl.CostEstimate(flops=1000000, bytes_accessed=1600000, transcendentals=0),
+        name="plane_total",
+    )(parts)
+
+
+def product_kernel(core_ref, rows_ref, basis_ref, *refs):
+    half, width = basis_ref.shape[0], 512
+    total = None if len(refs) == 1 else refs[0][...]
+    for step in range(half // width):
+        columns = pl.ds(pl.multiple_of(core_ref[0] * half + step * width, width), width)
+        basis = basis_ref[step * width : (step + 1) * width, :]
+        term = jnp.dot(rows_ref[:, columns], basis, preferred_element_type=jnp.float32)
+        total = term if total is None else total + term
+    refs[-1][...] = total.astype(refs[-1].dtype)
 
 
 def product_of_half(half, embeddings, basis, begin, out_type):
     depth, dim = embeddings.shape
     rank = basis.shape[1]
-    width, steps = 512, dim // 2 // 512
-    whole = pl.BlockSpec((depth, rank), lambda i, half: (0, 0))
     extra = [] if begin is None else [begin]
     return pl.pallas_call(
         product_kernel,
-        grid_spec=pltpu.PrefetchScalarGridSpec(
-            num_scalar_prefetch=1,
-            grid=(steps,),
-            in_specs=[
-                pl.BlockSpec((depth, width), lambda i, half: (0, half[0] * steps + i)),
-                pl.BlockSpec((width, rank), lambda i, half: (i, 0)),
-            ]
-            + [whole] * len(extra),
-            out_specs=whole,
-            scratch_shapes=[pltpu.VMEM((depth, rank), jnp.float32)],
-        ),
+        in_specs=[pl.BlockSpec(memory_space=pltpu.SMEM)]
+        + [pl.BlockSpec(memory_space=pltpu.VMEM)] * (2 + len(extra)),
         out_shape=jax.ShapeDtypeStruct((depth, rank), out_type),
+        compiler_params=pltpu.CompilerParams(vmem_limit_bytes=32 * 2**20),
         cost_estimate=pl.CostEstimate(
             flops=depth * dim * rank, bytes_accessed=depth * dim + dim * rank, transcendentals=0
         ),
@@ -228,54 +257,55 @@
     )(half, embeddings, basis, *extra)
 
 
-def pack_kernel(keep_ref, got_ref, gram_ref, gram_got_ref, out_ref):
-    count, _, rank = out_ref.shape
-    cross = keep_ref[...] + got_ref[...]
-    gram = gram_ref[...] + gram_got_ref[...]
-    pieces = [cross.reshape(count, -1, rank)]
-    for term in range(3):
-        short = gram.astype(jnp.bfloat16).astype(jnp.float32)
-        pieces.append(short.reshape(count, -1, rank))
-        gram = gram - short
-    filled = sum(p.shape[1] for p in pieces)
-    pieces.append(jnp.zeros((count, out_ref.shape[1] - filled, rank), jnp.float32))
-    out_ref[...] = jnp.concatenate(pieces, axis=1).astype(jnp.bfloat16)
-
-
-def pack_partials(keep, got, gram, gram_got, chips):
-    half, rank = keep.shape
-    steps = 8
-    rows = half // chips + 3 * rank // chips
-    rows += -rows % 8
-    return pl.pallas_call(
-        pack_kernel,
-        grid=(steps,),
-        in_specs=[pl.BlockSpec((half // steps, rank), lambda i: (i, 0))] * 2
-        + [pl.BlockSpec((rank // steps, rank), lambda i: (i, 0))] * 2,
-        out_specs=pl.BlockSpec((chips // steps, rows, rank), lambda i: (i, 0, 0)),
-        out_shape=jax.ShapeDtypeStruct((chips, rows, rank), jnp.bfloat16),
-        cost_estimate=pl.CostEstimate(flops=4000000, bytes_accessed=6000000, transcendentals=0),
-        name="pack_partials",
-    )(keep, got, gram, gram_got)
-
-
-def total_kernel(piece, gram_piece, parts_ref, out_ref):
-    total = jnp.sum(parts_ref[...].astype(jnp.float32), axis=0)
-    gram = sum(total[piece + t * gram_piece : piece + (t + 1) * gram_piece] for t in range(3))
-    fill = jnp.zeros((out_ref.shape[1] - piece - gram_piece, total.shape[1]), jnp.float32)
-    mine = jnp.concatenate([total[:piece], gram, fill], axis=0)
-    out_ref[...] = jnp.broadcast_to(mine[None], out_ref.shape)
-
-
-def total_partials(parts, piece, gram_piece, copies):
-    rows = piece + gram_piece
-    rows += -rows % 8
-    return pl.pallas_call(
-        functools.partial(total_kernel, piece, gram_piece),
-        out_shape=jax.ShapeDtypeStruct((copies, rows, parts.shape[2]), jnp.float32),
-        cost_estimate=pl.CostEstimate(flops=1000000, bytes_accessed=1600000, transcendentals=0),
-        name="total_partials",
-    )(parts)
+def route_kernel(capacity, ids_ref, map_ref, dest_ref, label_ref):
+    ids = ids_ref[...]
+    count, (high, low) = ids.shape[1], map_ref.shape
+    owner_count = label_ref.shape[0]
+    bf16 = jnp.bfloat16
+
+    def rows_of(size):
+        return lax.broadcasted_iota(jnp.int32, (size, count), 0)
+
+    picked = (rows_of(high) == ids // low).astype(bf16)
+    found = lax.dot_general(
+        map_ref[...].astype(bf16), picked, ROW_DIMS, preferred_element_type=jnp.float32
+    )
+    owner = jnp.sum(jnp.where(rows_of(low) == ids % low, found, 0.0), axis=0, keepdims=True)
+    owner = owner.astype(jnp.int32)
+    mine = rows_of(owner_count) == owner
+    order = lax.broadcasted_iota(jnp.int32, (count, count), 1)
+    earlier = (lax.broadcasted_iota(jnp.int32, (count, count), 0) < order).astype(bf16)
+    onehot = mine.astype(bf16)
+    before = jnp.dot(onehot, earlier, preferred_element_type=jnp.float32)
+    slot = jnp.sum(jnp.where(mine, before, 0.0), axis=0, keepdims=True).astype(jnp.int32)
+    dest_ref[...] = owner * capacity + slot
+    value = ids + 1
+    labels = None
+    for digit in range(3):
+        short = (value // 128**digit) % 128
+        spread = jnp.where(rows_of(16) == slot, short.astype(jnp.float32), 0.0).astype(bf16)
+        term = lax.dot_general(
+            onehot, spread, (((1,), (1,)), ((), ())), preferred_element_type=jnp.float32
+        )
+        term = term.astype(jnp.int32) * 128**digit
+        labels = term if labels is None else labels + term
+    label_ref[...] = (labels - 1)[:, :capacity]
+
+
+def route_rows(list_ids, owner_map, owner_count, capacity):
+    count = list_ids.shape[0]
+    return pl.pallas_call(
+        functools.partial(route_kernel, capacity),
+        out_shape=[
+            jax.ShapeDtypeStruct((1, count), jnp.int32),
+            jax.ShapeDtypeStruct((owner_count, capacity), jnp.int32),
+        ],
+        compiler_params=pltpu.CompilerParams(vmem_limit_bytes=32 * 2**20),
+        cost_estimate=pl.CostEstimate(
+            flops=2_000_000_000, bytes_accessed=1048576, transcendentals=0
+        ),
+        name="route_rows",
+    )(list_ids.reshape(1, count), owner_map.reshape(-1, 128))
 
 
 def place_kernel(target_ref, first_ref, second_ref, out_ref):
@@ -329,13 +359,23 @@
         jnp.bfloat16
     )
 
-    give, gram_part = cross_of_half(other_half, embeddings, sketch, True)
-    got, gram_got = shift(give, "narrow", 1), shift(gram_part, "narrow", 1)
-    (keep,) = cross_of_half(own_half, embeddings, sketch, False)
-    packed = pack_partials(keep, got, gram_part, gram_got, chips)
-    packed = lax.all_to_all(packed, ("x", "y", "z"), 0, 0, tiled=True)
-
-    packed = total_partials(packed, piece, gram_piece, plane)
+    capacity = 4 * row_count // dev_count
+    dest_index, labels = route_rows(list_ids, owner_map, dev_count, capacity)
+
+    parts = []
+    for step in list(range(1, line)) + [0]:
+        where = jnp.stack([(lax.axis_index("x") + step) % line, core])
+        give, keep = cross_chunk(where, embeddings, sketch, line)
+        got = shift(give, "narrow", 1)
+        if step:
+            parts.append(shift(keep + got, "x", step))
+        else:
+            parts += [keep, got]
+    labels, parts[0] = lax.optimization_barrier((labels, parts[0]))
+    arrived_labels = lax.all_to_all(labels, ALL, 0, 0, tiled=True)
+
+    packed = line_total(parts[::-1], plane, gram_piece)
+    packed = plane_total(lax.all_to_all(packed, PLANE, 0, 0, tiled=True))
     packed = lax.all_to_all(packed, PLANE, 0, 0, tiled=True)
     gram_line = packed[:, piece : piece + gram_piece].reshape(-1, rank)
     gram_parts = [gram_line] + [shift(gram_line, "x", step) for step in range(1, line)]
@@ -343,26 +383,14 @@
     cross_line = packed[:, :piece].reshape(-1, rank)
     cross_parts = [cross_line] + [shift(cross_line, "x", step) for step in range(1, line)]
 
-    capacity = 4 * row_count // dev_count
-    owners = owner_map[list_ids]
-    onehot = owners[:, None] == jnp.arange(dev_count, dtype=jnp.int32)[None, :]
-    ids = jnp.arange(row_count, dtype=jnp.int32)
-    earlier = (ids[:, None] > ids[None, :]).astype(jnp.bfloat16)
-    before = jnp.dot(earlier, onehot.astype(jnp.bfloat16), preferred_element_type=jnp.float32)
-    slot_index = jnp.sum(jnp.where(onehot, before, 0.0), axis=1).astype(jnp.int32)
-    dest_index = owners * capacity + slot_index
-
-    labels = jnp.full((dev_count * capacity,), -1, jnp.int32).at[dest_index].set(list_ids)
-    labels = labels.reshape(dev_count, capacity)
-    arrived_labels = lax.all_to_all(labels, ALL, 0, 0, tiled=True)
-
-    both_dest = jnp.stack([dest_index, shift(dest_index, "narrow", 1)])
+    both_dest = jnp.concatenate([dest_index, shift(dest_index, "narrow", 1)])
     both_owner = both_dest // capacity
     source = jnp.stack([core, 1 - core])[:, None]
     target = ((both_owner % chips) * cores + source) * capacity + both_dest % capacity
     target = jnp.where(both_owner // chips == core, target, -1)
 
     inverse = invert_factor(spot, gram_parts)
+    inverse, cross_parts = lax.optimization_barrier((inverse, cross_parts))
     moment = moment_of(cross_parts)
     basis = project_half(spot, inverse, moment, shift(moment, "narrow", 1), cross_parts)
     other_basis = shift(basis, "narrow", 1)

time: 272 us -> 244 us (0.90)
  blocking collectives: 84.9 us -> 61.1 us
  Pallas kernels: 66.3 us -> 47.8 us
  waiting for transfers between devices: 68.6 us -> 80.9 us
  starting transfers between devices: 24.6 us -> 32.4 us
  local copies, waits for them, and re-layouts: 18 us -> 12.1 us
    all_to_all x1, blocking collectives: 57.9 us -> 33.9 us  [local(): packed = plane_total(lax.all_to_all(packed, PLANE, 0, 0, tiled=True))]
    pallas_call x6 -> x9, Pallas kernels: 28.5 us -> 13.1 us  [the longest x4 6.31 us: cross_chunk(): pl.pallas_call(chunk_kernel, in_specs=[pl.BlockSpec(memory_space=pltpu.SM...]
    ppermute x12 -> x17, waiting for transfers between devices: 21.9 us -> 33.5 us  [shift(): lax.ppermute(value, axis, [(i, (i + step) % size) for i in range(size)])]
    ppermute x12 -> x17, starting transfers between devices: 8.44 us -> 16.2 us  [shift(): lax.ppermute(value, axis, [(i, (i + step) % size) for i in range(size)])]
    gather x1 -> x0, local copies, waits for them, and re-layouts: 4.46 us -> none  [local(): owners = owner_map[list_ids]]
    scatter x1 -> x0, local copies, waits for them, and re-layouts: 3.39 us -> none  [local(): jnp.full((dev_count * capacity,), -1, jnp.int32).at[dest_index]]
    pallas_call x1, Pallas kernels: 12.2 us -> 9.03 us  [project_half(): pl.pallas_call(whiten_kernel, in_specs=[pl.BlockSpec(memory_space=pltpu.S...]
    unnamed x31 -> x41, local copies, waits for them, and re-layouts: 7.59 us -> 10.4 us
  transfers between devices with their start and end apart: 14 -> 19, of which waited for: 4 -> 9; matrix products, arithmetic and copies ran while one was open for 4% -> 1% of each run, Pallas kernels for 13% -> 12%
where the time goes in v1:
time: 244 us; the launch traced here: 243 us
  waiting for transfers between devices  80.9 us (33%)
  blocking collectives  61.1 us (25%)
  Pallas kernels  47.8 us (20%)
  starting transfers between devices  32.4 us (13%)
  local copies, waits for them, and re-layouts  12.1 us (5%)
  matrix products  5.95 us (2%)
    all_to_all x1, waiting for transfers between devices, local(): arrived = lax.all_to_all(send_rows, ('y', 'z', 'x'), 0, 0, tiled=True)  41 us
    all_to_all x1, blocking collectives, local(): packed = plane_total(lax.all_to_all(packed, PLANE, 0, 0, tiled=True))  33.9 us
    ppermute x17, waiting for transfers between devices, shift(): lax.ppermute(value, axis, [(i, (i + step) % size) for i in range(size)])  33.5 us
    all_to_all x1, blocking collectives, local(): packed = lax.all_to_all(packed, PLANE, 0, 0, tiled=True)  27.3 us
    ppermute x17, starting transfers between devices, shift(): lax.ppermute(value, axis, [(i, (i + step) % size) for i in range(size)])  16.2 us
    pallas_call x1, Pallas kernels, invert_factor(): pl.pallas_call(invert_kernel, in_specs=[pl.BlockSpec(memory_space=pltpu.S...  15.8 us
    unnamed x41, local copies, waits for them, and re-layouts  10.4 us
    pallas_call x1, Pallas kernels, project_half(): pl.pallas_call(whiten_kernel, in_specs=[pl.BlockSpec(memory_space=pltpu.S...  9.03 us
  transfers between devices with their start and end apart: 19, of which 9 were waited for; matrix products, arithmetic and copies ran while one was open for 1% of the time, Pallas kernels for 12%

profile of v1, /device:TPU:32, one launch (start us, length us, event | category | flops | bytes accessed | tf_op | source)
XLA Modules:
  0.0 243.4 jit_solution(14829939065701987509)
XLA Ops:
  0.7 5.9 %fusion.2.sketch_ref = bf16[768,256]{1,0:T(8,128)(2,1)S(1)} fusion(bf16[768,4096]{1,0:T(8,128)(2,1)} %rows_ref.11, s32[4096,256]{1,0:T(8,128)} %param.5), kind=kOutput, calls=%fused_computation.2 | convolution fusion | flops 1611857920 | bytes 10878976 | tf_op jit(solution)/shard_map/dot_general | solution.py:358
  6.7 1.9 cross_chunk.7
  8.6 1.9 cross_chunk.6
  11.1 2.8 %copy-done = bf16[768,4096]{1,0:T(8,128)(2,1)S(1)} copy-done((bf16[768,4096]{1,0:T(8,128)(2,1)S(1)}, bf16[768,4096]{1,0:T(8,128)(2,1)}, u32[]{:S(2)}) %copy-start) | copy-done | bytes 6291480
  19.9 2.8 %collective-permute-start.5 = (f32[256,640]{1,0:T(8,128)S(1)}, f32[256,640]{1,0:T(8,128)S(1)}, u32[]{:S(2)}, u32[]{:S(2)}) collective-permute-start(f32[256,640]{1,0:T(8,128)S(1)} %add.65), channel_id=1, source_target_pairs={{0,2},{1,3},{2,0},{3,1},{4,6},{5,7},{6,4},{7,5},{8,10},{9,11},{10,... | collective-permute-start | bytes 1966088 | tf_op jit(solution)/shard_map/ppermute | solution.py:343
  24.4 2.5 %route_rows.1 = (s32[1,768]{1,0:T(1,128)S(1)}, s32[256,12]{1,0:T(8,128)}) custom-call(s32[1,768]{1,0:T(1,128)S(1)} %reshape.37.ids_ref, s32[2048,128]{1,0:T(8,128)S(1)} %bitcast.21), custom_call_target="tpu_custom_call" | custom-call | flops 2000000000 | bytes 1048576 | tf_op jit(solution)/shard_map/route_rows/pallas_call | solution.py:297
  26.8 9.5 %collective-permute-done.7.refs_4_ = f32[256,640]{1,0:T(8,128)S(1)} collective-permute-done((f32[256,640]{1,0:T(8,128)S(1)}, f32[256,640]{1,0:T(8,128)S(1)}, u32[]{:S(2)}, u32[]{:S(2)}) %collective-permute-start.7) | collective-permute-done | bytes 655392 | tf_op jit(solution)/shard_map/ppermute | solution.py:343
  36.3 15.0 %collective-permute-done.5.refs_3_ = f32[256,640]{1,0:T(8,128)S(1)} collective-permute-done((f32[256,640]{1,0:T(8,128)S(1)}, f32[256,640]{1,0:T(8,128)S(1)}, u32[]{:S(2)}, u32[]{:S(2)}) %collective-permute-start.5) | collective-permute-done | bytes 655392 | tf_op jit(solution)/shard_map/ppermute | solution.py:343
  51.7 33.9 %all_to_all.24.parts_ref = f32[32,24,256]{2,1,0:T(8,128)} all-to-all(f32[32,24,256]{2,1,0:T(8,128)S(1)} %line_total.1), channel_id=1, replica_groups=mesh['narrow'=2,'y'=4,'z'=8,'x'=4] {'y','z'}, dimensions={0} | all-to-all | bytes 1572864 | tf_op jit(solution)/shard_map/all_to_all | solution.py:378
  85.5 2.1 plane_total.1
  87.6 27.3 %all_to_all.25 = f32[32,24,256]{2,1,0:T(8,128)S(1)} all-to-all(f32[32,24,256]{2,1,0:T(8,128)} %plane_total.1), channel_id=1, replica_groups=mesh['narrow'=2,'y'=4,'z'=8,'x'=4] {'y','z'}, dimensions={0} | all-to-all | bytes 1572864 | tf_op jit(solution)/shard_map/all_to_all | solution.py:379
  115.0 2.2 collective-permute-start.8
  121.2 2.1 collective-permute-start.13
  126.2 15.8 %invert_factor.1.inverse_ref = f32[256,256]{1,0:T(8,128)} custom-call(s32[1]{0:T(128)} %bitcast.3.spot_ref, f32[64,256]{1,0:T(8,128)} %copy-done.8, f32[64,256]{1,0:T(8,128)} %copy-done.15, f32[64,256]{1,0:T(8,128)} %copy-done.17, f32[64,256]{1,0:T(8,128)} %copy-done.16), custom_call_target="tpu_custom_call" | custom-call | flops 20000000000 | bytes 524288 | tf_op jit(solution)/shard_map/invert_factor/pallas_call | solution.py:86
  142.0 4.0 %collective-permute-done.11.refs_1_ = f32[512,256]{1,0:T(8,128)S(1)} collective-permute-done((f32[512,256]{1,0:T(8,128)S(1)}, f32[512,256]{1,0:T(8,128)S(1)}, u32[]{:S(2)}, u32[]{:S(2)}) %collective-permute-start.11) | collective-permute-done | bytes 524320 | tf_op jit(solution)/shard_map/ppermute | solution.py:343
  146.8 4.3 %moment_of.1.moment_ref = f32[256,256]{1,0:T(8,128)} custom-call(f32[512,256]{1,0:T(8,128)} %bitcast.28, f32[512,256]{1,0:T(8,128)} %copy-done.12, f32[512,256]{1,0:T(8,128)} %copy-done.11, f32[512,256]{1,0:T(8,128)} %copy-done.10), custom_call_target="tpu_custom_call" | custom-call | flops 4000000000 | bytes 2359296 | tf_op jit(solution)/shard_map/moment_of/pallas_call | solution.py:108
  151.1 1.7 collective-permute-done.14.other_ref
  153.5 9.0 %project_half.1.basis_ref = bf16[2048,256]{1,0:T(8,128)(2,1)} custom-call(s32[1]{0:T(128)} %bitcast.3.spot_ref, f32[256,256]{1,0:T(8,128)} %invert_factor.1.inverse_ref, f32[256,256]{1,0:T(8,128)} %moment_of.1.moment_ref, f32[256,256]{1,0:T(8,128)} %copy-done.14, f32[512,256]{1,0:T(8,128)} %bitcast.29, f32[512,256]{1,0:T(8,128)} %copy-done.12, ...), custom_call_target="tpu_custom_call" | custom-call | flops 12000000000 | bytes 4194304 | tf_op jit(solution)/shard_map/project_half/pallas_call | solution.py:147
  162.7 2.8 %copy-done.1 = bf16[768,4096]{1,0:T(8,128)(2,1)S(1)} copy-done((bf16[768,4096]{1,0:T(8,128)(2,1)S(1)}, bf16[768,4096]{1,0:T(8,128)(2,1)}, u32[]{:S(2)}) %copy-start.1) | copy-done | bytes 6291480
  171.2 8.3 %all-to-all-start.3 = ((s32[256,1,12]{2,1,0:T(1,128)}), s32[256,1,12]{2,1,0:T(1,128)S(1)}, u32[]{:S(2)}, u32[]{:S(2)}) async-start(s32[256,1,12]{2,1,0:T(1,128)} %bitcast.14), calls=%async_computation.3 | async-start | bytes 262144 | tf_op jit(solution)/shard_map/all_to_all | solution.py:375
  180.3 5.6 %place_rows.1 = bf16[3072,256]{1,0:T(8,128)(2,1)} custom-call(s32[2,768]{1,0:T(2,128)} %compare_select_fusion.target_ref, bf16[768,256]{1,0:T(8,128)(2,1)} %copy-done.5, bf16[768,256]{1,0:T(8,128)(2,1)} %copy-done.13), custom_call_target="tpu_custom_call" | custom-call | flops 2415919104 | bytes 3145728 | tf_op jit(solution)/shard_map/place_rows/pallas_call | solution.py:327
  185.8 6.4 %all-to-all-done.3 = s32[256,1,12]{2,1,0:T(1,128)S(1)} async-done(((s32[256,1,12]{2,1,0:T(1,128)}), s32[256,1,12]{2,1,0:T(1,128)S(1)}, u32[]{:S(2)}, u32[]{:S(2)}) %all-to-all-start.3) | async-done | bytes 12320 | tf_op jit(solution)/shard_map/all_to_all | solution.py:375
  192.3 7.9 %all-to-all-start.2 = ((bf16[128,24,256]{2,1,0:T(8,128)(2,1)}), bf16[128,24,256]{2,1,0:T(8,128)(2,1)S(1)}, u32[]{:S(2)}, u32[]{:S(2)}) async-start(bf16[128,24,256]{2,1,0:T(8,128)(2,1)} %bitcast.23), calls=%async_computation.2 | async-start | bytes 3145728 | tf_op jit(solution)/shard_map/all_to_all | solution.py:403
  200.8 41.0 %all-to-all-done.2 = bf16[128,24,256]{2,1,0:T(8,128)(2,1)S(1)} async-done(((bf16[128,24,256]{2,1,0:T(8,128)(2,1)}), bf16[128,24,256]{2,1,0:T(8,128)(2,1)S(1)}, u32[]{:S(2)}, u32[]{:S(2)}) %all-to-all-start.2) | async-done | bytes 1572896 | tf_op jit(solution)/shard_map/all_to_all | solution.py:403
  (85 shorter events, 25.9 us)
Async XLA Ops:
  8.6 8.5 %collective-permute-start.6 = (f32[256,640]{1,0:T(8,128)}, f32[256,640]{1,0:T(8,128)}, u32[]{:S(2)}, u32[]{:S(2)}) collective-permute-start(f32[256,640]{1,0:T(8,128)} %get-tuple-element.30), channel_id=1, source_target_pairs={{0,128},{128,0},{1,129},{129,1},{2,130},{130,2},{3,131},{131,3},{4... | collective-permute-start | bytes 1966088 | tf_op jit(solution)/shard_map/ppermute | solution.py:343
  10.5 9.4 %collective-permute-start.4 = (f32[256,640]{1,0:T(8,128)}, f32[256,640]{1,0:T(8,128)S(1)}, u32[]{:S(2)}, u32[]{:S(2)}) collective-permute-start(f32[256,640]{1,0:T(8,128)} %get-tuple-element.27), channel_id=1, source_target_pairs={{0,128},{128,0},{1,129},{129,1},{2,130},{130,2},{3,131},{131,3},{4... | collective-permute-start | bytes 1966088 | tf_op jit(solution)/shard_map/ppermute | solution.py:343
  15.2 7.6 %collective-permute-start.2 = (f32[256,640]{1,0:T(8,128)S(1)}, f32[256,640]{1,0:T(8,128)S(1)}, u32[]{:S(2)}, u32[]{:S(2)}) collective-permute-start(f32[256,640]{1,0:T(8,128)S(1)} %get-tuple-element.25), channel_id=1, source_target_pairs={{0,128},{128,0},{1,129},{129,1},{2,130},{130,2},{3,131},{131,3},{4... | collective-permute-start | bytes 1966088 | tf_op jit(solution)/shard_map/ppermute | solution.py:343
  16.5 7.8 %copy-start.9 = (s32[768]{0:T(1024)S(1)}, s32[768]{0:T(1024)}, u32[]{:S(2)}) copy-start(s32[768]{0:T(1024)} %param.6) | copy-start | bytes 9220
  16.5 7.8 %copy-start.6 = (s32[262144]{0:T(1024)S(1)}, s32[262144]{0:T(1024)}, u32[]{:S(2)}) copy-start(s32[262144]{0:T(1024)} %param.7) | copy-start | bytes 3145732
  16.6 19.8 %collective-permute-start.1 = (f32[256,640]{1,0:T(8,128)S(1)}, f32[256,640]{1,0:T(8,128)S(1)}, u32[]{:S(2)}, u32[]{:S(2)}) collective-permute-start(f32[256,640]{1,0:T(8,128)S(1)} %get-tuple-element.22), channel_id=1, source_target_pairs={{0,128},{128,0},{1,129},{129,1},{2,130},{130,2},{3,131},{131,3},{4... | collective-permute-start | bytes 1966088 | tf_op jit(solution)/shard_map/ppermute | solution.py:343
  18.3 18.0 %collective-permute-start.7 = (f32[256,640]{1,0:T(8,128)S(1)}, f32[256,640]{1,0:T(8,128)S(1)}, u32[]{:S(2)}, u32[]{:S(2)}) collective-permute-start(f32[256,640]{1,0:T(8,128)S(1)} %add.68), channel_id=1, source_target_pairs={{0,1},{1,2},{2,3},{3,0},{4,5},{5,6},{6,7},{7,4},{8,9},{9,10},{10,1... | collective-permute-start | bytes 1966088 | tf_op jit(solution)/shard_map/ppermute | solution.py:343
  19.9 31.4 %collective-permute-start.5 = (f32[256,640]{1,0:T(8,128)S(1)}, f32[256,640]{1,0:T(8,128)S(1)}, u32[]{:S(2)}, u32[]{:S(2)}) collective-permute-start(f32[256,640]{1,0:T(8,128)S(1)} %add.65), channel_id=1, source_target_pairs={{0,2},{1,3},{2,0},{3,1},{4,6},{5,7},{6,4},{7,5},{8,10},{9,11},{10,... | collective-permute-start | bytes 1966088 | tf_op jit(solution)/shard_map/ppermute | solution.py:343
  22.8 28.5 %collective-permute-start.3 = (f32[256,640]{1,0:T(8,128)S(1)}, f32[256,640]{1,0:T(8,128)S(1)}, u32[]{:S(2)}, u32[]{:S(2)}) collective-permute-start(f32[256,640]{1,0:T(8,128)S(1)} %add.62), channel_id=1, source_target_pairs={{0,3},{1,0},{2,1},{3,2},{4,7},{5,4},{6,5},{7,6},{8,11},{9,8},{10,9... | collective-permute-start | bytes 1966088 | tf_op jit(solution)/shard_map/ppermute | solution.py:343
  115.0 10.6 %copy-start.8 = (f32[64,256]{1,0:T(8,128)}, f32[64,256]{1,0:T(8,128)S(1)}, u32[]{:S(2)}) copy-start(f32[64,256]{1,0:T(8,128)S(1)} %reshape.40.refs_0_) | copy-start | bytes 196612
  115.0 6.1 %collective-permute-start.8 = (f32[64,256]{1,0:T(8,128)S(1)}, f32[64,256]{1,0:T(8,128)S(1)}, u32[]{:S(2)}, u32[]{:S(2)}) collective-permute-start(f32[64,256]{1,0:T(8,128)S(1)} %reshape.40.refs_0_), channel_id=1, source_target_pairs={{0,1},{1,2},{2,3},{3,0},{4,5},{5,6},{6,7},{7,4},{8,9},{9,10},{10,1... | collective-permute-start | bytes 196616 | tf_op jit(solution)/shard_map/ppermute | solution.py:343
  117.2 7.0 %collective-permute-start.10 = (f32[64,256]{1,0:T(8,128)S(1)}, f32[64,256]{1,0:T(8,128)S(1)}, u32[]{:S(2)}, u32[]{:S(2)}) collective-permute-start(f32[64,256]{1,0:T(8,128)S(1)} %reshape.40.refs_0_), channel_id=1, source_target_pairs={{0,3},{1,0},{2,1},{3,2},{4,7},{5,4},{6,5},{7,6},{8,11},{9,8},{10,9... | collective-permute-start | bytes 196616 | tf_op jit(solution)/shard_map/ppermute | solution.py:343
  118.9 6.6 %collective-permute-start.9 = (f32[64,256]{1,0:T(8,128)S(1)}, f32[64,256]{1,0:T(8,128)S(1)}, u32[]{:S(2)}, u32[]{:S(2)}) collective-permute-start(f32[64,256]{1,0:T(8,128)S(1)} %reshape.40.refs_0_), channel_id=1, source_target_pairs={{0,2},{1,3},{2,0},{3,1},{4,6},{5,7},{6,4},{7,5},{8,10},{9,11},{10,... | collective-permute-start | bytes 196616 | tf_op jit(solution)/shard_map/ppermute | solution.py:343
  121.2 20.8 %copy-start.7 = (f32[32,16,256]{2,1,0:T(8,128)}, f32[32,16,256]{2,1,0:T(8,128)S(1)}, u32[]{:S(2)}) copy-start(f32[32,16,256]{2,1,0:T(8,128)S(1)} %slice.7) | copy-start | bytes 1572868
  121.2 20.8 %collective-permute-start.13 = (f32[512,256]{1,0:T(8,128)S(1)}, f32[512,256]{1,0:T(8,128)S(1)}, u32[]{:S(2)}, u32[]{:S(2)}) collective-permute-start(f32[512,256]{1,0:T(8,128)S(1)} %bitcast.25), channel_id=1, source_target_pairs={{0,3},{1,0},{2,1},{3,2},{4,7},{5,4},{6,5},{7,6},{8,11},{9,8},{10,9... | collective-permute-start | bytes 1572872 | tf_op jit(solution)/shard_map/ppermute | solution.py:343
  123.3 18.7 %collective-permute-start.12 = (f32[512,256]{1,0:T(8,128)S(1)}, f32[512,256]{1,0:T(8,128)S(1)}, u32[]{:S(2)}, u32[]{:S(2)}) collective-permute-start(f32[512,256]{1,0:T(8,128)S(1)} %bitcast.26), channel_id=1, source_target_pairs={{0,2},{1,3},{2,0},{3,1},{4,6},{5,7},{6,4},{7,5},{8,10},{9,11},{10,... | collective-permute-start | bytes 1572872 | tf_op jit(solution)/shard_map/ppermute | solution.py:343
  124.0 22.0 %collective-permute-start.11 = (f32[512,256]{1,0:T(8,128)S(1)}, f32[512,256]{1,0:T(8,128)S(1)}, u32[]{:S(2)}, u32[]{:S(2)}) collective-permute-start(f32[512,256]{1,0:T(8,128)S(1)} %bitcast.27), channel_id=1, source_target_pairs={{0,1},{1,2},{2,3},{3,0},{4,5},{5,6},{6,7},{7,4},{8,9},{9,10},{10,1... | collective-permute-start | bytes 1572872 | tf_op jit(solution)/shard_map/ppermute | solution.py:343
  151.1 1.7 collective-permute-start.14
  162.6 5.1 %collective-permute-start.15 = (bf16[2048,256]{1,0:T(8,128)(2,1)}, bf16[2048,256]{1,0:T(8,128)(2,1)S(1)}, u32[]{:S(2)}, u32[]{:S(2)}) collective-permute-start(bf16[2048,256]{1,0:T(8,128)(2,1)} %project_half.1.basis_ref), channel_id=1, source_target_pairs={{0,128},{128,0},{1,129},{129,1},{2,130},{130,2},{3,131},{131,3},{4... | collective-permute-start | bytes 3145736 | tf_op jit(solution)/shard_map/ppermute | solution.py:343
  168.7 10.8 %copy-start.5 = (bf16[768,256]{1,0:T(8,128)(2,1)}, bf16[768,256]{1,0:T(8,128)(2,1)S(1)}, u32[]{:S(2)}) copy-start(bf16[768,256]{1,0:T(8,128)(2,1)S(1)} %product_of_half.3.first_ref) | copy-start | bytes 1179652
  168.7 10.8 %collective-permute-start.16 = (bf16[768,256]{1,0:T(8,128)(2,1)S(1)}, bf16[768,256]{1,0:T(8,128)(2,1)S(1)}, u32[]{:S(2)}, u32[]{:S(2)}) collective-permute-start(bf16[768,256]{1,0:T(8,128)(2,1)S(1)} %product_of_half.3.first_ref), channel_id=1, source_target_pairs={{0,128},{128,0},{1,129},{129,1},{2,130},{130,2},{3,131},{131,3},{4... | collective-permute-start | bytes 1179656 | tf_op jit(solution)/shard_map/ppermute | solution.py:343
  169.2 1.4 collective-permute-start
  171.2 21.1 %all-to-all-start.3 = ((s32[256,1,12]{2,1,0:T(1,128)}), s32[256,1,12]{2,1,0:T(1,128)S(1)}, u32[]{:S(2)}, u32[]{:S(2)}) async-start(s32[256,1,12]{2,1,0:T(1,128)} %bitcast.14), calls=%async_computation.3 | async-start | bytes 262144 | tf_op jit(solution)/shard_map/all_to_all | solution.py:375
  192.3 49.6 %all-to-all-start.2 = ((bf16[128,24,256]{2,1,0:T(8,128)(2,1)}), bf16[128,24,256]{2,1,0:T(8,128)(2,1)S(1)}, u32[]{:S(2)}, u32[]{:S(2)}) async-start(bf16[128,24,256]{2,1,0:T(8,128)(2,1)} %bitcast.23), calls=%async_computation.2 | async-start | bytes 3145728 | tf_op jit(solution)/shard_map/all_to_all | solution.py:403
  (15 other events, 39.5 us)

commit v2 on v1

--- a/solution.py
+++ b/solution.py
@@ -9,12 +9,14 @@
 from jax.sharding import PartitionSpec as P
 
 NS_STEPS = 6
-BLOCK = 32
+BLOCK = 64
 TILE = 8
 ALL = ("narrow", "y", "z", "x")
 PLANE = ("y", "z")
 HIGHEST = lax.Precision.HIGHEST
 ROW_DIMS = (((0,), (0,)), ((), ()))
+SLOTS = 16
+GRANT = pltpu.CompilerParams(vmem_limit_bytes=16 * 2**20)
 
 
 def dot_f32(a, b, dims=(((1,), (0,)), ((), ()))):
@@ -89,6 +91,7 @@
         + [pl.BlockSpec(memory_space=pltpu.VMEM)] * len(parts),
         out_shape=jax.ShapeDtypeStruct((rank, rank), jnp.float32),
         scratch_shapes=[pltpu.VMEM((rank, 2 * rank), jnp.float32)],
+        compiler_params=GRANT,
         cost_estimate=pl.CostEstimate(flops=20_000_000_000, bytes_accessed=524288, transcendentals=0),
         name="invert_factor",
     )(spot, *parts)
@@ -108,6 +111,7 @@
     return pl.pallas_call(
         moment_kernel,
         out_shape=jax.ShapeDtypeStruct((rank, rank), jnp.float32),
+        compiler_params=GRANT,
         cost_estimate=pl.CostEstimate(flops=4_000_000_000, bytes_accessed=2359296, transcendentals=0),
         name="moment_of",
     )(*parts)
@@ -149,13 +153,14 @@
         in_specs=[pl.BlockSpec(memory_space=pltpu.SMEM)]
         + [pl.BlockSpec(memory_space=pltpu.VMEM)] * (3 + len(parts)),
         out_shape=jax.ShapeDtypeStruct((chunk * len(parts), rank), jnp.bfloat16),
+        compiler_params=GRANT,
         cost_estimate=pl.CostEstimate(flops=12_000_000_000, bytes_accessed=4194304, transcendentals=0),
         name="project_half",
     )(spot, inverse, moment, other, *parts)
 
 
-def chunk_kernel(spot_ref, rows_ref, sketch_ref, give_ref, keep_ref):
-    chunk, core = spot_ref[0], spot_ref[1]
+def chunk_kernel(spot_ref, rows_ref, sketch_ref, label_ref, give_ref, keep_ref):
+    chunk, core, here, line = (spot_ref[i] for i in range(4))
     rank = sketch_ref.shape[1]
     width = give_ref.shape[1] - 128
     half = rows_ref.shape[1] // 2
@@ -165,13 +170,18 @@
     )
     gram = mul(sketch, sketch)
     gram = pltpu.roll(gram, rank - chunk * (rank * width // half), 1)[:, :128]
+    lane = lax.broadcasted_iota(jnp.int32, gram.shape, 1)
+    gram = jnp.where(lane < rank * width // half, gram, 0.0)
+    mine = pl.ds(pl.multiple_of((core * line + here) * SLOTS, SLOTS), SLOTS)
     for out_ref, place in ((give_ref, 1 - core), (keep_ref, core)):
         columns = pl.ds(pl.multiple_of(place * half + chunk * width, width), width)
         out_ref[:, :width] = mul(sketch, rows_ref[:, columns])
         out_ref[:, width:] = gram
-
-
-def cross_chunk(spot, embeddings, sketch, chunks):
+        theirs = pl.ds(pl.multiple_of((place * line + chunk) * SLOTS, SLOTS), SLOTS)
+        out_ref[mine, width:] += label_ref[theirs, :]
+
+
+def cross_chunk(spot, embeddings, sketch, labels, chunks):
     depth, dim = embeddings.shape
     rank = sketch.shape[1]
     width = dim // 2 // chunks
@@ -179,14 +189,30 @@
     return pl.pallas_call(
         chunk_kernel,
         in_specs=[pl.BlockSpec(memory_space=pltpu.SMEM)]
-        + [pl.BlockSpec(memory_space=pltpu.VMEM)] * 2,
+        + [pl.BlockSpec(memory_space=pltpu.VMEM)] * 3,
         out_shape=[shape, shape],
-        compiler_params=pltpu.CompilerParams(vmem_limit_bytes=32 * 2**20),
+        compiler_params=GRANT,
         cost_estimate=pl.CostEstimate(
             flops=2 * depth * rank * (2 * width + rank), bytes_accessed=3000000, transcendentals=0
         ),
         name="cross_chunk",
-    )(spot, embeddings, sketch)
+    )(spot, embeddings, sketch, labels)
+
+
+def join_kernel(side, keep_ref, got_ref, extra_ref, out_ref):
+    height = extra_ref.shape[0]
+    out_ref[...] = keep_ref[...] + got_ref[...]
+    out_ref[side * height : (side + 1) * height, :] += extra_ref[...]
+
+
+def join_chunk(keep, got, extra, side):
+    return pl.pallas_call(
+        functools.partial(join_kernel, side),
+        out_shape=jax.ShapeDtypeStruct(keep.shape, jnp.float32),
+        compiler_params=GRANT,
+        cost_estimate=pl.CostEstimate(flops=400000, bytes_accessed=2000000, transcendentals=0),
+        name="join_chunk",
+    )(keep, got, extra)
 
 
 def line_kernel(gram_piece, *refs):
@@ -198,32 +224,38 @@
         total = total + part_ref[...]
     piece = width // plane
     out_ref[:, :piece, :] = total[:, :width].T.reshape(plane, piece, rank)
-    gram = total[:, width:].T[: plane * gram_piece].reshape(plane, gram_piece, rank)
-    fill = jnp.zeros((plane, out_ref.shape[1] - piece - gram_piece, rank), jnp.float32)
-    out_ref[:, piece:, :] = jnp.concatenate([gram, fill], axis=1)
+    tail = total[:, width:].T.reshape(2, plane, gram_piece, rank)
+    fill = jnp.zeros((plane, out_ref.shape[1] - piece - 2 * gram_piece, rank), jnp.float32)
+    out_ref[:, piece:, :] = jnp.concatenate([tail[0], tail[1], fill], axis=1)
 
 
 def line_total(parts, plane, gram_piece):
     rank, width = parts[0].shape
-    rows = (width - 128) // plane + gram_piece
+    rows = (width - 128) // plane + 2 * gram_piece
     rows += -rows % 8
     return pl.pallas_call(
         functools.partial(line_kernel, gram_piece),
         out_shape=jax.ShapeDtypeStruct((plane, rows, rank), jnp.float32),
-        compiler_params=pltpu.CompilerParams(vmem_limit_bytes=32 * 2**20),
+        compiler_params=GRANT,
         cost_estimate=pl.CostEstimate(flops=1000000, bytes_accessed=4000000, transcendentals=0),
         name="line_total",
     )(*parts)
 
 
-def plane_kernel(parts_ref, out_ref):
+def plane_kernel(label_row, parts_ref, out_ref, label_ref):
     out_ref[...] = jnp.broadcast_to(jnp.sum(parts_ref[...], axis=0, keepdims=True), out_ref.shape)
-
-
-def plane_total(parts):
-    return pl.pallas_call(
-        plane_kernel,
-        out_shape=jax.ShapeDtypeStruct(parts.shape, jnp.float32),
+    label_ref[...] = parts_ref[:, label_row, :].astype(jnp.int32) - 1
+
+
+def plane_total(parts, label_row):
+    plane, _, rank = parts.shape
+    return pl.pallas_call(
+        functools.partial(plane_kernel, label_row),
+        out_shape=[
+            jax.ShapeDtypeStruct(parts.shape, jnp.float32),
+            jax.ShapeDtypeStruct((plane, rank), jnp.int32),
+        ],
+        compiler_params=GRANT,
         cost_estimate=pl.CostEstimate(flops=1000000, bytes_accessed=1600000, transcendentals=0),
         name="plane_total",
     )(parts)
@@ -249,7 +281,7 @@
         in_specs=[pl.BlockSpec(memory_space=pltpu.SMEM)]
         + [pl.BlockSpec(memory_space=pltpu.VMEM)] * (2 + len(extra)),
         out_shape=jax.ShapeDtypeStruct((depth, rank), out_type),
-        compiler_params=pltpu.CompilerParams(vmem_limit_bytes=32 * 2**20),
+        compiler_params=GRANT,
         cost_estimate=pl.CostEstimate(
             flops=depth * dim * rank, bytes_accessed=depth * dim + dim * rank, transcendentals=0
         ),
@@ -257,10 +289,10 @@
     )(half, embeddings, basis, *extra)
 
 
-def route_kernel(capacity, ids_ref, map_ref, dest_ref, label_ref):
+def route_kernel(capacity, line, plane, ids_ref, map_ref, dest_ref, label_ref):
     ids = ids_ref[...]
     count, (high, low) = ids.shape[1], map_ref.shape
-    owner_count = label_ref.shape[0]
+    owner_count = 2 * plane * line
     bf16 = jnp.bfloat16
 
     def rows_of(size):
@@ -275,32 +307,37 @@
     mine = rows_of(owner_count) == owner
     order = lax.broadcasted_iota(jnp.int32, (count, count), 1)
     earlier = (lax.broadcasted_iota(jnp.int32, (count, count), 0) < order).astype(bf16)
-    onehot = mine.astype(bf16)
-    before = jnp.dot(onehot, earlier, preferred_element_type=jnp.float32)
+    before = jnp.dot(mine.astype(bf16), earlier, preferred_element_type=jnp.float32)
     slot = jnp.sum(jnp.where(mine, before, 0.0), axis=0, keepdims=True).astype(jnp.int32)
     dest_ref[...] = owner * capacity + slot
     value = ids + 1
+    core, chip = owner // (plane * line), owner % (plane * line)
+    row = (core * line + chip % line) * SLOTS + slot
+    lane = rows_of(128) == 64 + 2 * (chip // line)
+    lane = lane.astype(bf16)
     labels = None
     for digit in range(3):
         short = (value // 128**digit) % 128
-        spread = jnp.where(rows_of(16) == slot, short.astype(jnp.float32), 0.0).astype(bf16)
+        spread = jnp.where(rows_of(2 * line * SLOTS) == row, short.astype(jnp.float32), 0.0)
         term = lax.dot_general(
-            onehot, spread, (((1,), (1,)), ((), ())), preferred_element_type=jnp.float32
+            spread.astype(bf16),
+            lane,
+            (((1,), (1,)), ((), ())),
+            preferred_element_type=jnp.float32,
         )
-        term = term.astype(jnp.int32) * 128**digit
-        labels = term if labels is None else labels + term
-    label_ref[...] = (labels - 1)[:, :capacity]
-
-
-def route_rows(list_ids, owner_map, owner_count, capacity):
+        labels = term if labels is None else labels + term * 128**digit
+    label_ref[...] = labels
+
+
+def route_rows(list_ids, owner_map, capacity, line, plane):
     count = list_ids.shape[0]
     return pl.pallas_call(
-        functools.partial(route_kernel, capacity),
+        functools.partial(route_kernel, capacity, line, plane),
         out_shape=[
             jax.ShapeDtypeStruct((1, count), jnp.int32),
-            jax.ShapeDtypeStruct((owner_count, capacity), jnp.int32),
+            jax.ShapeDtypeStruct((2 * line * SLOTS, 128), jnp.float32),
         ],
-        compiler_params=pltpu.CompilerParams(vmem_limit_bytes=32 * 2**20),
+        compiler_params=GRANT,
         cost_estimate=pl.CostEstimate(
             flops=2_000_000_000, bytes_accessed=1048576, transcendentals=0
         ),
@@ -308,31 +345,38 @@
     )(list_ids.reshape(1, count), owner_map.reshape(-1, 128))
 
 
-def place_kernel(target_ref, first_ref, second_ref, out_ref):
-    tile = out_ref.shape[0]
-    base = pl.program_id(0) * tile
-    depth = first_ref.shape[0]
-    slots = base + lax.broadcasted_iota(jnp.int32, (tile, depth), 0)
-    total = None
+def place_kernel(capacity, target_ref, first_ref, second_ref, out_ref):
+    pairs, _, width = out_ref.shape
+    count = pairs * 2 * capacity
+    slots = pl.program_id(0) * count + lax.broadcasted_iota(
+        jnp.int32, (count, first_ref.shape[0]), 0
+    )
+    found = []
     for part, rows_ref in enumerate((first_ref, second_ref)):
         onehot = (slots == target_ref[part : part + 1, :]).astype(jnp.bfloat16)
         term = jnp.dot(onehot, rows_ref[...], preferred_element_type=jnp.float32)
-        total = term if total is None else total + term
-    out_ref[...] = total.astype(jnp.bfloat16)
-
-
-def place_rows(target, first, second, count):
-    tile = 512
+        found.append(term.reshape(pairs, 2 * capacity, width))
+    a, b = found
+    out_ref[...] = jnp.concatenate(
+        [a[:, :capacity], b[:, :capacity], a[:, capacity:], b[:, capacity:]], axis=1
+    ).astype(jnp.bfloat16)
+
+
+def place_rows(target, first, second, chips, capacity):
+    pairs = 16
     depth, width = first.shape
     return pl.pallas_call(
-        place_kernel,
-        grid=(count // tile,),
+        functools.partial(place_kernel, capacity),
+        grid=(chips // 2 // pairs,),
         in_specs=[pl.BlockSpec((2, depth), lambda i: (0, 0))]
         + [pl.BlockSpec((depth, width), lambda i: (0, 0))] * 2,
-        out_specs=pl.BlockSpec((tile, width), lambda i: (i, 0)),
-        out_shape=jax.ShapeDtypeStruct((count, width), jnp.bfloat16),
+        out_specs=pl.BlockSpec((pairs, 4 * capacity, width), lambda i: (i, 0, 0)),
+        out_shape=jax.ShapeDtypeStruct((chips // 2, 4 * capacity, width), jnp.bfloat16),
+        compiler_params=GRANT,
         cost_estimate=pl.CostEstimate(
-            flops=4 * count * depth * width, bytes_accessed=4 * count * width, transcendentals=0
+            flops=4 * chips * capacity * depth * width,
+            bytes_accessed=8 * chips * capacity * width,
+            transcendentals=0,
         ),
         name="place_rows",
     )(target, first, second)
@@ -360,34 +404,38 @@
     )
 
     capacity = 4 * row_count // dev_count
-    dest_index, labels = route_rows(list_ids, owner_map, dev_count, capacity)
-
-    parts = []
-    for step in list(range(1, line)) + [0]:
-        where = jnp.stack([(lax.axis_index("x") + step) % line, core])
-        give, keep = cross_chunk(where, embeddings, sketch, line)
-        got = shift(give, "narrow", 1)
-        if step:
-            parts.append(shift(keep + got, "x", step))
-        else:
-            parts += [keep, got]
-    labels, parts[0] = lax.optimization_barrier((labels, parts[0]))
-    arrived_labels = lax.all_to_all(labels, ALL, 0, 0, tiled=True)
-
-    packed = line_total(parts[::-1], plane, gram_piece)
-    packed = plane_total(lax.all_to_all(packed, PLANE, 0, 0, tiled=True))
+    here = lax.axis_index("x")
+    dest_index, labels = route_rows(list_ids, owner_map, capacity, line, plane)
+
+    def chunk_at(step):
+        where = jnp.stack([(here + step) % line, core, here, jnp.int32(line)])
+        give, keep = cross_chunk(where, embeddings, sketch, labels, line)
+        return keep, shift(give, "narrow", 1)
+
+    far, up, down, near = (chunk_at(step) for step in (2, 1, 3, 0))
+    far = far[0] + far[1]
+    from_below = shift(far[: rank // 2], "x", 1)
+    from_above = shift(far[rank // 2 :], "x", line - 1)
+    from_below = shift(join_chunk(*up, from_below, 0), "x", 1)
+    from_above = shift(join_chunk(*down, from_above, 1), "x", line - 1)
+
+    packed = line_total([*near, from_below, from_above], plane, gram_piece)
+    packed = lax.all_to_all(packed, PLANE, 0, 0, tiled=True)
+    packed, arrived_labels = plane_total(packed, piece + gram_piece)
     packed = lax.all_to_all(packed, PLANE, 0, 0, tiled=True)
     gram_line = packed[:, piece : piece + gram_piece].reshape(-1, rank)
     gram_parts = [gram_line] + [shift(gram_line, "x", step) for step in range(1, line)]
     packed, gram_parts[1] = lax.optimization_barrier((packed, gram_parts[1]))
     cross_line = packed[:, :piece].reshape(-1, rank)
     cross_parts = [cross_line] + [shift(cross_line, "x", step) for step in range(1, line)]
+    arrived_labels = arrived_labels[:, : cores * line * SLOTS].reshape(plane, cores, line, SLOTS)
+    arrived_labels = arrived_labels[..., :capacity].transpose(1, 0, 2, 3)
 
     both_dest = jnp.concatenate([dest_index, shift(dest_index, "narrow", 1)])
     both_owner = both_dest // capacity
-    source = jnp.stack([core, 1 - core])[:, None]
-    target = ((both_owner % chips) * cores + source) * capacity + both_dest % capacity
+    target = (both_owner % chips) * capacity + both_dest % capacity
     target = jnp.where(both_owner // chips == core, target, -1)
+    target = jnp.where(core == 0, target, target[::-1])
 
     inverse = invert_factor(spot, gram_parts)
     inverse, cross_parts = lax.optimization_barrier((inverse, cross_parts))
@@ -396,8 +444,13 @@
     other_basis = shift(basis, "narrow", 1)
     begun = product_of_half(own_half, embeddings, basis, None, jnp.float32)
     reduced = product_of_half(other_half, embeddings, other_basis, begun, jnp.bfloat16)
+    other = shift(reduced, "narrow", 1)
     send_rows = place_rows(
-        target, reduced, shift(reduced, "narrow", 1), chips * cores * capacity
+        target,
+        jnp.where(core == 0, reduced, other),
+        jnp.where(core == 0, other, reduced),
+        chips,
+        capacity,
     )
     send_rows = send_rows.reshape(chips, cores * capacity, rank)
     arrived = lax.all_to_all(send_rows, ("y", "z", "x"), 0, 0, tiled=True)

time: 244 us -> 212 us (0.87)
  Pallas kernels: 47.8 us -> 34.6 us
  starting transfers between devices: 32.4 us -> 22.9 us
  waiting for transfers between devices: 80.9 us -> 77.8 us
  blocking collectives: 61.1 us -> 58.6 us
    all_to_all x1 -> x0, blocking collectives: 33.9 us -> none  [local(): packed = plane_total(lax.all_to_all(packed, PLANE, 0, 0, tiled=True))]
    all_to_all x1 -> x2, blocking collectives: 27.3 us -> 58.6 us  [local(): packed = lax.all_to_all(packed, PLANE, 0, 0, tiled=True)]
    all_to_all x1 -> x0, starting transfers between devices: 8.27 us -> none  [local(): arrived_labels = lax.all_to_all(labels, ALL, 0, 0, tiled=True)]
    all_to_all x1 -> x0, waiting for transfers between devices: 6.44 us -> none  [local(): arrived_labels = lax.all_to_all(labels, ALL, 0, 0, tiled=True)]
    pallas_call x3 -> x5, Pallas kernels: 10.1 us -> 5.83 us  [the longest x1 2.94 us: place_rows(): pl.pallas_call(functools.partial(place_kernel, capacity), grid=(chips //...]
    pallas_call x1, Pallas kernels: 15.8 us -> 11.8 us  [invert_factor(): pl.pallas_call(invert_kernel, in_specs=[pl.BlockSpec(memory_space=pltpu.S...]
    ppermute x17 -> x18, waiting for transfers between devices: 33.5 us -> 36.9 us  [shift(): lax.ppermute(value, axis, [(i, (i + step) % size) for i in range(size)])]
    pallas_call x1, Pallas kernels: 9.03 us -> 6.3 us  [project_half(): pl.pallas_call(whiten_kernel, in_specs=[pl.BlockSpec(memory_space=pltpu.S...]
  transfers between devices with their start and end apart: 19 -> 19, of which waited for: 9 -> 10; matrix products, arithmetic and copies ran while one was open for 1% -> 1% of each run, Pallas kernels for 12% -> 9%
where the time goes in v2:
time: 212 us; the launch traced here: 211 us
  waiting for transfers between devices  77.8 us (37%)
  blocking collectives  58.6 us (28%)
  Pallas kernels  34.6 us (16%)
  starting transfers between devices  22.9 us (11%)
  local copies, waits for them, and re-layouts  10.7 us (5%)
  matrix products  4.02 us (2%)
    all_to_all x2, blocking collectives, local(): packed = lax.all_to_all(packed, PLANE, 0, 0, tiled=True)  58.6 us
    all_to_all x1, waiting for transfers between devices, local(): arrived = lax.all_to_all(send_rows, ('y', 'z', 'x'), 0, 0, tiled=True)  40.8 us
    ppermute x18, waiting for transfers between devices, shift(): lax.ppermute(value, axis, [(i, (i + step) % size) for i in range(size)])  36.9 us
    ppermute x18, starting transfers between devices, shift(): lax.ppermute(value, axis, [(i, (i + step) % size) for i in range(size)])  14.8 us
    pallas_call x1, Pallas kernels, invert_factor(): pl.pallas_call(invert_kernel, in_specs=[pl.BlockSpec(memory_space=pltpu.S...  11.8 us
    all_to_all x1, starting transfers between devices, local(): arrived = lax.all_to_all(send_rows, ('y', 'z', 'x'), 0, 0, tiled=True)  8.14 us
    unnamed x17, local copies, waits for them, and re-layouts  7.83 us
    pallas_call x4, Pallas kernels, cross_chunk(): pl.pallas_call(chunk_kernel, in_specs=[pl.BlockSpec(memory_space=pltpu.SM...  6.33 us
  transfers between devices with their start and end apart: 19, of which 10 were waited for; matrix products, arithmetic and copies ran while one was open for 1% of the time, Pallas kernels for 9%

profile of v2, /device:TPU:32, one launch (start us, length us, event | category | flops | bytes accessed | tf_op | source)
XLA Modules:
  0.0 211.1 jit_solution(4438245316956342999)
XLA Ops:
  2.7 1.5 route_rows.1
  4.4 4.0 %fusion.2.sketch_ref = bf16[768,256]{1,0:T(8,128)(2,1)S(1)} fusion(bf16[768,4096]{1,0:T(8,128)(2,1)S(1)} %copy-done, s32[4096,256]{1,0:T(8,128)} %param.5), kind=kOutput, calls=%fused_computation.2 | convolution fusion | flops 1611857920 | bytes 10878976 | tf_op jit(solution)/shard_map/dot_general | solution.py:402
  8.5 1.9 cross_chunk.6
  10.5 1.9 cross_chunk.7
  13.0 2.8 %copy-done.1 = bf16[768,4096]{1,0:T(8,128)(2,1)S(1)} copy-done((bf16[768,4096]{1,0:T(8,128)(2,1)S(1)}, bf16[768,4096]{1,0:T(8,128)(2,1)}, u32[]{:S(2)}) %copy-start.1) | copy-done | bytes 6291480
  18.4 2.8 %collective-permute-start.7 = (f32[128,640]{1,0:T(8,128)S(1)}, f32[128,640]{1,0:T(8,128)S(1)}, u32[]{:S(2)}, u32[]{:S(2)}) collective-permute-start(f32[128,640]{1,0:T(8,128)S(1)} %get-tuple-element.48), channel_id=1, source_target_pairs={{0,3},{1,0},{2,1},{3,2},{4,7},{5,4},{6,5},{7,6},{8,11},{9,8},{10,9... | collective-permute-start | bytes 983048 | tf_op jit(solution)/shard_map/ppermute | solution.py:387
  22.8 6.0 %collective-permute-done.7.extra_ref = f32[128,640]{1,0:T(8,128)S(1)} collective-permute-done((f32[128,640]{1,0:T(8,128)S(1)}, f32[128,640]{1,0:T(8,128)S(1)}, u32[]{:S(2)}, u32[]{:S(2)}) %collective-permute-start.7) | collective-permute-done | bytes 327712 | tf_op jit(solution)/shard_map/ppermute | solution.py:387
  30.0 3.8 %collective-permute-start.8 = (f32[256,640]{1,0:T(8,128)S(1)}, f32[256,640]{1,0:T(8,128)S(1)}, u32[]{:S(2)}, u32[]{:S(2)}) collective-permute-start(f32[256,640]{1,0:T(8,128)S(1)} %join_chunk.3), channel_id=1, source_target_pairs={{0,3},{1,0},{2,1},{3,2},{4,7},{5,4},{6,5},{7,6},{8,11},{9,8},{10,9... | collective-permute-start | bytes 1966088 | tf_op jit(solution)/shard_map/ppermute | solution.py:387
  34.0 13.6 %collective-permute-done.8.refs_3_ = f32[256,640]{1,0:T(8,128)S(1)} collective-permute-done((f32[256,640]{1,0:T(8,128)S(1)}, f32[256,640]{1,0:T(8,128)S(1)}, u32[]{:S(2)}, u32[]{:S(2)}) %collective-permute-start.8) | collective-permute-done | bytes 655392 | tf_op jit(solution)/shard_map/ppermute | solution.py:387
  47.5 3.6 %collective-permute-done.5.refs_2_ = f32[256,640]{1,0:T(8,128)S(1)} collective-permute-done((f32[256,640]{1,0:T(8,128)S(1)}, f32[256,640]{1,0:T(8,128)S(1)}, u32[]{:S(2)}, u32[]{:S(2)}) %collective-permute-start.5) | collective-permute-done | bytes 655392 | tf_op jit(solution)/shard_map/ppermute | solution.py:387
  51.5 32.9 %all_to_all.15.parts_ref = f32[32,24,256]{2,1,0:T(8,128)S(1)} all-to-all(f32[32,24,256]{2,1,0:T(8,128)S(1)} %line_total.1), channel_id=1, replica_groups=mesh['narrow'=2,'y'=4,'z'=8,'x'=4] {'y','z'}, dimensions={0} | all-to-all | bytes 1572864 | tf_op jit(solution)/shard_map/all_to_all | solution.py:423
  84.5 25.7 %all_to_all.16 = f32[32,24,256]{2,1,0:T(8,128)S(1)} all-to-all(f32[32,24,256]{2,1,0:T(8,128)S(1)} %get-tuple-element.31), channel_id=1, replica_groups=mesh['narrow'=2,'y'=4,'z'=8,'x'=4] {'y','z'}, dimensions={0} | all-to-all | bytes 1572864 | tf_op jit(solution)/shard_map/all_to_all | solution.py:425
  111.1 2.5 %collective-permute-start.11 = (f32[64,256]{1,0:T(8,128)S(1)}, f32[64,256]{1,0:T(8,128)S(1)}, u32[]{:S(2)}, u32[]{:S(2)}) collective-permute-start(f32[64,256]{1,0:T(8,128)S(1)} %reshape.42.refs_0_), channel_id=1, source_target_pairs={{0,3},{1,0},{2,1},{3,2},{4,7},{5,4},{6,5},{7,6},{8,11},{9,8},{10,9... | collective-permute-start | bytes 196616 | tf_op jit(solution)/shard_map/ppermute | solution.py:387
  113.6 2.2 %collective-permute-done.9.refs_1_ = f32[64,256]{1,0:T(8,128)S(1)} collective-permute-done((f32[64,256]{1,0:T(8,128)S(1)}, f32[64,256]{1,0:T(8,128)S(1)}, u32[]{:S(2)}, u32[]{:S(2)}) %collective-permute-start.9) | collective-permute-done | bytes 65568 | tf_op jit(solution)/shard_map/ppermute | solution.py:387
  118.7 1.5 collective-permute-done.10.refs_2_
  120.2 11.8 %invert_factor.1.inverse_ref = f32[256,256]{1,0:T(8,128)S(1)} custom-call(s32[1]{0:T(128)} %bitcast.2.spot_ref, f32[64,256]{1,0:T(8,128)S(1)} %reshape.42.refs_0_, f32[64,256]{1,0:T(8,128)S(1)} %collective-permute-done.9.refs_1_, f32[64,256]{1,0:T(8,128)S(1)} %collective-permute-done.10.refs_2_, f32[64,256]{1,0:T(8,128)S(1)} %collective-permute-done.11.refs_3_), custom_call_target="tpu_custom_call" | custom-call | flops 20000000000 | bytes 524288 | tf_op jit(solution)/shard_map/invert_factor/pallas_call | solution.py:88
  132.8 6.3 %collective-permute-done.12.refs_1_ = f32[512,256]{1,0:T(8,128)S(1)} collective-permute-done((f32[512,256]{1,0:T(8,128)S(1)}, f32[512,256]{1,0:T(8,128)S(1)}, u32[]{:S(2)}, u32[]{:S(2)}) %collective-permute-start.12) | collective-permute-done | bytes 524320 | tf_op jit(solution)/shard_map/ppermute | solution.py:387
  139.2 2.1 %moment_of.1.moment_ref = f32[256,256]{1,0:T(8,128)S(1)} custom-call(f32[512,256]{1,0:T(8,128)S(1)} %bitcast.24, f32[512,256]{1,0:T(8,128)S(1)} %collective-permute-done.12.refs_1_, f32[512,256]{1,0:T(8,128)S(1)} %collective-permute-done.13.refs_2_, f32[512,256]{1,0:T(8,128)S(1)} %collective-permute-done.14.refs_3_), custom_call_target="tpu_custom_call" | custom-call | flops 4000000000 | bytes 2359296 | tf_op jit(solution)/shard_map/moment_of/pallas_call | solution.py:111
  141.6 1.5 collective-permute-done.15.other_ref
  143.2 6.3 %project_half.1.basis_ref = bf16[2048,256]{1,0:T(8,128)(2,1)S(1)} custom-call(s32[1]{0:T(128)} %bitcast.2.spot_ref, f32[256,256]{1,0:T(8,128)S(1)} %invert_factor.1.inverse_ref, f32[256,256]{1,0:T(8,128)S(1)} %moment_of.1.moment_ref, f32[256,256]{1,0:T(8,128)S(1)} %collective-permute-done.15.other_ref, f32[512,256]{1,0:T(8,128)S(1)} %bitcast.25, ...), custom_call_target="tpu_custom_call" | custom-call | flops 12000000000 | bytes 4194304 | tf_op jit(solution)/shard_map/project_half/pallas_call | solution.py:151
  149.7 2.8 %copy-done.2 = bf16[768,4096]{1,0:T(8,128)(2,1)S(1)} copy-done((bf16[768,4096]{1,0:T(8,128)(2,1)S(1)}, bf16[768,4096]{1,0:T(8,128)(2,1)}, u32[]{:S(2)}) %copy-start.2) | copy-done | bytes 6291480
  156.7 2.9 %place_rows.1 = bf16[64,48,256]{2,1,0:T(8,128)(2,1)} custom-call(s32[2,768]{1,0:T(2,128)S(1)} %broadcast_select_fusion.2.target_ref, bf16[768,256]{1,0:T(8,128)(2,1)S(1)} %get-tuple-element.47.first_ref, bf16[768,256]{1,0:T(8,128)(2,1)S(1)} %get-tuple-element.46.second_ref), custom_call_target="tpu_custom_call" | custom-call | flops 1207959552 | bytes 3145728 | tf_op jit(solution)/shard_map/place_rows/pallas_call | solution.py:368
  159.6 8.1 %all-to-all-start.2 = ((bf16[128,24,256]{2,1,0:T(8,128)(2,1)}), bf16[128,24,256]{2,1,0:T(8,128)(2,1)S(1)}, u32[]{:S(2)}, u32[]{:S(2)}) async-start(bf16[128,24,256]{2,1,0:T(8,128)(2,1)} %bitcast.9), calls=%async_computation.2 | async-start | bytes 3145728 | tf_op jit(solution)/shard_map/all_to_all | solution.py:456
  168.7 40.8 %all-to-all-done.2 = bf16[128,24,256]{2,1,0:T(8,128)(2,1)S(1)} async-done(((bf16[128,24,256]{2,1,0:T(8,128)(2,1)}), bf16[128,24,256]{2,1,0:T(8,128)(2,1)S(1)}, u32[]{:S(2)}, u32[]{:S(2)}) %all-to-all-start.2) | async-done | bytes 1572896 | tf_op jit(solution)/shard_map/all_to_all | solution.py:456
  (68 shorter events, 20.6 us)
Async XLA Ops:
  1.3 3.1 %copy-start = (bf16[768,4096]{1,0:T(8,128)(2,1)S(1)}, bf16[768,4096]{1,0:T(8,128)(2,1)}, u32[]{:S(2)}) copy-start(bf16[768,4096]{1,0:T(8,128)(2,1)} %rows_ref.11) | copy-start | bytes 18874372
  10.5 6.7 %collective-permute-start.3 = (f32[256,640]{1,0:T(8,128)}, f32[256,640]{1,0:T(8,128)}, u32[]{:S(2)}, u32[]{:S(2)}) collective-permute-start(f32[256,640]{1,0:T(8,128)} %get-tuple-element.28), channel_id=1, source_target_pairs={{0,128},{128,0},{1,129},{129,1},{2,130},{130,2},{3,131},{131,3},{4... | collective-permute-start | bytes 1966088 | tf_op jit(solution)/shard_map/ppermute | solution.py:387
  10.5 10.8 %slice-start = ((s8[6291456]{0:T(1024)(128)(4,1)}), s8[2097152]{0:T(1024)(128)(4,1)S(1)}, s32[]{:S(2)}) async-start(s8[6291456]{0:T(1024)(128)(4,1)} %bitcast.19), calls=%async_computation.3 | async-start | bytes 4194304
  12.4 10.4 %collective-permute-start.6 = (f32[256,640]{1,0:T(8,128)}, f32[256,640]{1,0:T(8,128)}, u32[]{:S(2)}, u32[]{:S(2)}) collective-permute-start(f32[256,640]{1,0:T(8,128)} %get-tuple-element.30), channel_id=1, source_target_pairs={{0,128},{128,0},{1,129},{129,1},{2,130},{130,2},{3,131},{131,3},{4... | collective-permute-start | bytes 1966088 | tf_op jit(solution)/shard_map/ppermute | solution.py:387
  13.0 2.8 %copy-start.1 = (bf16[768,4096]{1,0:T(8,128)(2,1)S(1)}, bf16[768,4096]{1,0:T(8,128)(2,1)}, u32[]{:S(2)}) copy-start(bf16[768,4096]{1,0:T(8,128)(2,1)} %rows_ref.11) | copy-start | bytes 18874372
  15.7 5.5 %slice-start.1 = ((s8[6291456]{0:T(1024)(128)(4,1)}), s8[4194304]{0:T(1024)(128)(4,1)S(1)}, s32[]{:S(2)}) async-start(s8[6291456]{0:T(1024)(128)(4,1)} %bitcast.19), calls=%async_computation.4 | async-start | bytes 8388608
  17.0 16.7 %collective-permute-start.2 = (f32[256,640]{1,0:T(8,128)S(1)}, f32[256,640]{1,0:T(8,128)S(1)}, u32[]{:S(2)}, u32[]{:S(2)}) collective-permute-start(f32[256,640]{1,0:T(8,128)S(1)} %get-tuple-element.26), channel_id=1, source_target_pairs={{0,128},{128,0},{1,129},{129,1},{2,130},{130,2},{3,131},{131,3},{4... | collective-permute-start | bytes 1966088 | tf_op jit(solution)/shard_map/ppermute | solution.py:387
  18.4 10.4 %collective-permute-start.7 = (f32[128,640]{1,0:T(8,128)S(1)}, f32[128,640]{1,0:T(8,128)S(1)}, u32[]{:S(2)}, u32[]{:S(2)}) collective-permute-start(f32[128,640]{1,0:T(8,128)S(1)} %get-tuple-element.48), channel_id=1, source_target_pairs={{0,3},{1,0},{2,1},{3,2},{4,7},{5,4},{6,5},{7,6},{8,11},{9,8},{10,9... | collective-permute-start | bytes 983048 | tf_op jit(solution)/shard_map/ppermute | solution.py:387
  21.2 12.5 %collective-permute-start.4 = (f32[128,640]{1,0:T(8,128)S(1)}, f32[128,640]{1,0:T(8,128)S(1)}, u32[]{:S(2)}, u32[]{:S(2)}) collective-permute-start(f32[128,640]{1,0:T(8,128)S(1)} %get-tuple-element.49), channel_id=1, source_target_pairs={{0,1},{1,2},{2,3},{3,0},{4,5},{5,6},{6,7},{7,4},{8,9},{9,10},{10,1... | collective-permute-start | bytes 983048 | tf_op jit(solution)/shard_map/ppermute | solution.py:387
  22.5 11.4 %collective-permute-start.1 = (f32[256,640]{1,0:T(8,128)S(1)}, f32[256,640]{1,0:T(8,128)S(1)}, u32[]{:S(2)}, u32[]{:S(2)}) collective-permute-start(f32[256,640]{1,0:T(8,128)S(1)} %get-tuple-element.24), channel_id=1, source_target_pairs={{0,128},{128,0},{1,129},{129,1},{2,130},{130,2},{3,131},{131,3},{4... | collective-permute-start | bytes 1966088 | tf_op jit(solution)/shard_map/ppermute | solution.py:387
  30.0 17.6 %collective-permute-start.8 = (f32[256,640]{1,0:T(8,128)S(1)}, f32[256,640]{1,0:T(8,128)S(1)}, u32[]{:S(2)}, u32[]{:S(2)}) collective-permute-start(f32[256,640]{1,0:T(8,128)S(1)} %join_chunk.3), channel_id=1, source_target_pairs={{0,3},{1,0},{2,1},{3,2},{4,7},{5,4},{6,5},{7,6},{8,11},{9,8},{10,9... | collective-permute-start | bytes 1966088 | tf_op jit(solution)/shard_map/ppermute | solution.py:387
  33.9 17.3 %collective-permute-start.5 = (f32[256,640]{1,0:T(8,128)S(1)}, f32[256,640]{1,0:T(8,128)S(1)}, u32[]{:S(2)}, u32[]{:S(2)}) collective-permute-start(f32[256,640]{1,0:T(8,128)S(1)} %join_chunk.2), channel_id=1, source_target_pairs={{0,1},{1,2},{2,3},{3,0},{4,5},{5,6},{6,7},{7,4},{8,9},{9,10},{10,1... | collective-permute-start | bytes 1966088 | tf_op jit(solution)/shard_map/ppermute | solution.py:387
  110.3 5.6 %collective-permute-start.9 = (f32[64,256]{1,0:T(8,128)S(1)}, f32[64,256]{1,0:T(8,128)S(1)}, u32[]{:S(2)}, u32[]{:S(2)}) collective-permute-start(f32[64,256]{1,0:T(8,128)S(1)} %reshape.42.refs_0_), channel_id=1, source_target_pairs={{0,1},{1,2},{2,3},{3,0},{4,5},{5,6},{6,7},{7,4},{8,9},{9,10},{10,1... | collective-permute-start | bytes 196616 | tf_op jit(solution)/shard_map/ppermute | solution.py:387
  111.1 7.6 %collective-permute-start.11 = (f32[64,256]{1,0:T(8,128)S(1)}, f32[64,256]{1,0:T(8,128)S(1)}, u32[]{:S(2)}, u32[]{:S(2)}) collective-permute-start(f32[64,256]{1,0:T(8,128)S(1)} %reshape.42.refs_0_), channel_id=1, source_target_pairs={{0,3},{1,0},{2,1},{3,2},{4,7},{5,4},{6,5},{7,6},{8,11},{9,8},{10,9... | collective-permute-start | bytes 196616 | tf_op jit(solution)/shard_map/ppermute | solution.py:387
  113.6 6.6 %collective-permute-start.10 = (f32[64,256]{1,0:T(8,128)S(1)}, f32[64,256]{1,0:T(8,128)S(1)}, u32[]{:S(2)}, u32[]{:S(2)}) collective-permute-start(f32[64,256]{1,0:T(8,128)S(1)} %reshape.42.refs_0_), channel_id=1, source_target_pairs={{0,2},{1,3},{2,0},{3,1},{4,6},{5,7},{6,4},{7,5},{8,10},{9,11},{10,... | collective-permute-start | bytes 196616 | tf_op jit(solution)/shard_map/ppermute | solution.py:387
  115.9 16.1 %collective-permute-start.14 = (f32[512,256]{1,0:T(8,128)S(1)}, f32[512,256]{1,0:T(8,128)S(1)}, u32[]{:S(2)}, u32[]{:S(2)}) collective-permute-start(f32[512,256]{1,0:T(8,128)S(1)} %bitcast.21), channel_id=1, source_target_pairs={{0,3},{1,0},{2,1},{3,2},{4,7},{5,4},{6,5},{7,6},{8,11},{9,8},{10,9... | collective-permute-start | bytes 1572872 | tf_op jit(solution)/shard_map/ppermute | solution.py:387
  116.5 16.4 %collective-permute-start.13 = (f32[512,256]{1,0:T(8,128)S(1)}, f32[512,256]{1,0:T(8,128)S(1)}, u32[]{:S(2)}, u32[]{:S(2)}) collective-permute-start(f32[512,256]{1,0:T(8,128)S(1)} %bitcast.22), channel_id=1, source_target_pairs={{0,2},{1,3},{2,0},{3,1},{4,6},{5,7},{6,4},{7,5},{8,10},{9,11},{10,... | collective-permute-start | bytes 1572872 | tf_op jit(solution)/shard_map/ppermute | solution.py:387
  117.5 21.6 %collective-permute-start.12 = (f32[512,256]{1,0:T(8,128)S(1)}, f32[512,256]{1,0:T(8,128)S(1)}, u32[]{:S(2)}, u32[]{:S(2)}) collective-permute-start(f32[512,256]{1,0:T(8,128)S(1)} %bitcast.23), channel_id=1, source_target_pairs={{0,1},{1,2},{2,3},{3,0},{4,5},{5,6},{6,7},{7,4},{8,9},{9,10},{10,1... | collective-permute-start | bytes 1572872 | tf_op jit(solution)/shard_map/ppermute | solution.py:387
  141.3 1.8 collective-permute-start.15
  149.5 4.0 %collective-permute-start.16 = (bf16[2048,256]{1,0:T(8,128)(2,1)S(1)}, bf16[2048,256]{1,0:T(8,128)(2,1)S(1)}, u32[]{:S(2)}, u32[]{:S(2)}) collective-permute-start(bf16[2048,256]{1,0:T(8,128)(2,1)S(1)} %project_half.1.basis_ref), channel_id=1, source_target_pairs={{0,128},{128,0},{1,129},{129,1},{2,130},{130,2},{3,131},{131,3},{4... | collective-permute-start | bytes 3145736 | tf_op jit(solution)/shard_map/ppermute | solution.py:387
  149.7 2.8 %copy-start.2 = (bf16[768,4096]{1,0:T(8,128)(2,1)S(1)}, bf16[768,4096]{1,0:T(8,128)(2,1)}, u32[]{:S(2)}) copy-start(bf16[768,4096]{1,0:T(8,128)(2,1)} %rows_ref.11) | copy-start | bytes 18874372
  154.5 2.1 %collective-permute-start.17 = (bf16[768,256]{1,0:T(8,128)(2,1)S(1)}, bf16[768,256]{1,0:T(8,128)(2,1)S(1)}, u32[]{:S(2)}, u32[]{:S(2)}) collective-permute-start(bf16[768,256]{1,0:T(8,128)(2,1)S(1)} %product_of_half.3), channel_id=1, source_target_pairs={{0,128},{128,0},{1,129},{129,1},{2,130},{130,2},{3,131},{131,3},{4... | collective-permute-start | bytes 1179656 | tf_op jit(solution)/shard_map/ppermute | solution.py:387
  154.9 1.4 collective-permute-start
  159.6 49.9 %all-to-all-start.2 = ((bf16[128,24,256]{2,1,0:T(8,128)(2,1)}), bf16[128,24,256]{2,1,0:T(8,128)(2,1)S(1)}, u32[]{:S(2)}, u32[]{:S(2)}) async-start(bf16[128,24,256]{2,1,0:T(8,128)(2,1)} %bitcast.9), calls=%async_computation.2 | async-start | bytes 3145728 | tf_op jit(solution)/shard_map/all_to_all | solution.py:456
  (3 other events, 4.7 us)

commit v3 on v2

--- a/solution.py
+++ b/solution.py
@@ -10,12 +10,13 @@
 
 NS_STEPS = 6
 BLOCK = 64
-TILE = 8
+TILE = 16
 ALL = ("narrow", "y", "z", "x")
 PLANE = ("y", "z")
 HIGHEST = lax.Precision.HIGHEST
 ROW_DIMS = (((0,), (0,)), ((), ()))
 SLOTS = 16
+SPOTS = 4
 GRANT = pltpu.CompilerParams(vmem_limit_bytes=16 * 2**20)
 
 
@@ -160,32 +161,28 @@
 
 
 def chunk_kernel(spot_ref, rows_ref, sketch_ref, label_ref, give_ref, keep_ref):
-    chunk, core, here, line = (spot_ref[i] for i in range(4))
+    chunk, core, line = (spot_ref[i] for i in range(3))
     rank = sketch_ref.shape[1]
-    width = give_ref.shape[1] - 128
+    width = give_ref.shape[1]
     half = rows_ref.shape[1] // 2
+    count = label_ref.shape[0] // 2 // SPOTS
     sketch = sketch_ref[...]
-    mul = functools.partial(
-        lax.dot_general, dimension_numbers=ROW_DIMS, preferred_element_type=jnp.float32
-    )
-    gram = mul(sketch, sketch)
-    gram = pltpu.roll(gram, rank - chunk * (rank * width // half), 1)[:, :128]
-    lane = lax.broadcasted_iota(jnp.int32, gram.shape, 1)
-    gram = jnp.where(lane < rank * width // half, gram, 0.0)
-    mine = pl.ds(pl.multiple_of((core * line + here) * SLOTS, SLOTS), SLOTS)
     for out_ref, place in ((give_ref, 1 - core), (keep_ref, core)):
         columns = pl.ds(pl.multiple_of(place * half + chunk * width, width), width)
-        out_ref[:, :width] = mul(sketch, rows_ref[:, columns])
-        out_ref[:, width:] = gram
-        theirs = pl.ds(pl.multiple_of((place * line + chunk) * SLOTS, SLOTS), SLOTS)
-        out_ref[mine, width:] += label_ref[theirs, :]
+        out_ref[:rank, :] = lax.dot_general(
+            sketch, rows_ref[:, columns], ROW_DIMS, preferred_element_type=jnp.float32
+        )
+        start = (place * line + chunk) * count
+        for block in range(width // 128):
+            rows = pl.ds(pl.multiple_of(start + 8 * block, 8), 8)
+            out_ref[rank:, 128 * block : 128 * (block + 1)] = label_ref[rows, :]
 
 
 def cross_chunk(spot, embeddings, sketch, labels, chunks):
     depth, dim = embeddings.shape
     rank = sketch.shape[1]
     width = dim // 2 // chunks
-    shape = jax.ShapeDtypeStruct((rank, width + 128), jnp.float32)
+    shape = jax.ShapeDtypeStruct((rank + 8, width), jnp.float32)
     return pl.pallas_call(
         chunk_kernel,
         in_specs=[pl.BlockSpec(memory_space=pltpu.SMEM)]
@@ -193,16 +190,17 @@
         out_shape=[shape, shape],
         compiler_params=GRANT,
         cost_estimate=pl.CostEstimate(
-            flops=2 * depth * rank * (2 * width + rank), bytes_accessed=3000000, transcendentals=0
+            flops=4 * depth * rank * width, bytes_accessed=3000000, transcendentals=0
         ),
         name="cross_chunk",
     )(spot, embeddings, sketch, labels)
 
 
 def join_kernel(side, keep_ref, got_ref, extra_ref, out_ref):
-    height = extra_ref.shape[0]
+    height, whole = extra_ref.shape[0], out_ref.shape[0]
+    rows = slice(0, height) if side == 0 else slice(whole - height, whole)
     out_ref[...] = keep_ref[...] + got_ref[...]
-    out_ref[side * height : (side + 1) * height, :] += extra_ref[...]
+    out_ref[rows, :] += extra_ref[...]
 
 
 def join_chunk(keep, got, extra, side):
@@ -215,45 +213,49 @@
     )(keep, got, extra)
 
 
-def line_kernel(gram_piece, *refs):
+def line_kernel(*refs):
     parts, out_ref = refs[:-1], refs[-1]
-    plane, _, rank = out_ref.shape
-    width = parts[0].shape[1] - 128
+    plane = out_ref.shape[0]
     total = parts[0][...] + parts[1][...]
     for part_ref in parts[2:]:
         total = total + part_ref[...]
+    rank, width = total.shape[0] - 8, total.shape[1]
     piece = width // plane
-    out_ref[:, :piece, :] = total[:, :width].T.reshape(plane, piece, rank)
-    tail = total[:, width:].T.reshape(2, plane, gram_piece, rank)
-    fill = jnp.zeros((plane, out_ref.shape[1] - piece - 2 * gram_piece, rank), jnp.float32)
-    out_ref[:, piece:, :] = jnp.concatenate([tail[0], tail[1], fill], axis=1)
-
-
-def line_total(parts, plane, gram_piece):
-    rank, width = parts[0].shape
-    rows = (width - 128) // plane + 2 * gram_piece
-    rows += -rows % 8
-    return pl.pallas_call(
-        functools.partial(line_kernel, gram_piece),
-        out_shape=jax.ShapeDtypeStruct((plane, rows, rank), jnp.float32),
+    turned = total[:rank, :].T.reshape(plane, piece, rank)
+    out_ref[:, :piece, :] = turned[:, :, :128]
+    out_ref[:, piece : 2 * piece, :] = turned[:, :, 128:]
+    labels = [total[rank:, 128 * k : 128 * (k + 1)] for k in range(width // 128)]
+    labels = jnp.concatenate(labels, axis=0).reshape(plane, 1, 128)
+    fill = jnp.zeros((plane, out_ref.shape[1] - 2 * piece - 1, 128), jnp.float32)
+    out_ref[:, 2 * piece :, :] = jnp.concatenate([labels, fill], axis=1)
+
+
+def line_total(parts, plane):
+    rows = 2 * (parts[0].shape[1] // plane) + 8
+    return pl.pallas_call(
+        line_kernel,
+        out_shape=jax.ShapeDtypeStruct((plane, rows, 128), jnp.float32),
         compiler_params=GRANT,
         cost_estimate=pl.CostEstimate(flops=1000000, bytes_accessed=4000000, transcendentals=0),
         name="line_total",
     )(*parts)
 
 
-def plane_kernel(label_row, parts_ref, out_ref, label_ref):
-    out_ref[...] = jnp.broadcast_to(jnp.sum(parts_ref[...], axis=0, keepdims=True), out_ref.shape)
-    label_ref[...] = parts_ref[:, label_row, :].astype(jnp.int32) - 1
-
-
-def plane_total(parts, label_row):
-    plane, _, rank = parts.shape
-    return pl.pallas_call(
-        functools.partial(plane_kernel, label_row),
+def plane_kernel(parts_ref, out_ref, label_ref):
+    piece = out_ref.shape[1]
+    total = jnp.sum(parts_ref[:, : 2 * piece, :], axis=0)
+    total = jnp.concatenate([total[:piece], total[piece:]], axis=1)
+    out_ref[...] = jnp.broadcast_to(total[None], out_ref.shape)
+    label_ref[...] = parts_ref[:, 2 * piece, :].astype(jnp.int32) - 1
+
+
+def plane_total(parts, piece):
+    plane, _, lanes = parts.shape
+    return pl.pallas_call(
+        plane_kernel,
         out_shape=[
-            jax.ShapeDtypeStruct(parts.shape, jnp.float32),
-            jax.ShapeDtypeStruct((plane, rank), jnp.int32),
+            jax.ShapeDtypeStruct((plane, piece, 2 * lanes), jnp.float32),
+            jax.ShapeDtypeStruct((plane, lanes), jnp.int32),
         ],
         compiler_params=GRANT,
         cost_estimate=pl.CostEstimate(flops=1000000, bytes_accessed=1600000, transcendentals=0),
@@ -289,7 +291,7 @@
     )(half, embeddings, basis, *extra)
 
 
-def route_kernel(capacity, line, plane, ids_ref, map_ref, dest_ref, label_ref):
+def route_kernel(capacity, line, plane, spot_ref, ids_ref, map_ref, dest_ref, label_ref):
     ids = ids_ref[...]
     count, (high, low) = ids.shape[1], map_ref.shape
     owner_count = 2 * plane * line
@@ -312,37 +314,36 @@
     dest_ref[...] = owner * capacity + slot
     value = ids + 1
     core, chip = owner // (plane * line), owner % (plane * line)
-    row = (core * line + chip % line) * SLOTS + slot
-    lane = rows_of(128) == 64 + 2 * (chip // line)
-    lane = lane.astype(bf16)
+    row = (core * line + chip % line) * plane + chip // line
+    row = (rows_of(owner_count) == row).astype(bf16)
+    lane = rows_of(2 * line * SLOTS) == spot_ref[0] * SLOTS + slot
     labels = None
     for digit in range(3):
         short = (value // 128**digit) % 128
-        spread = jnp.where(rows_of(2 * line * SLOTS) == row, short.astype(jnp.float32), 0.0)
+        spread = jnp.where(lane, short.astype(jnp.float32), 0.0).astype(bf16)
         term = lax.dot_general(
-            spread.astype(bf16),
-            lane,
-            (((1,), (1,)), ((), ())),
-            preferred_element_type=jnp.float32,
+            row, spread, (((1,), (1,)), ((), ())), preferred_element_type=jnp.float32
         )
         labels = term if labels is None else labels + term * 128**digit
     label_ref[...] = labels
 
 
-def route_rows(list_ids, owner_map, capacity, line, plane):
+def route_rows(spot, list_ids, owner_map, capacity, line, plane):
     count = list_ids.shape[0]
     return pl.pallas_call(
         functools.partial(route_kernel, capacity, line, plane),
+        in_specs=[pl.BlockSpec(memory_space=pltpu.SMEM)]
+        + [pl.BlockSpec(memory_space=pltpu.VMEM)] * 2,
         out_shape=[
             jax.ShapeDtypeStruct((1, count), jnp.int32),
-            jax.ShapeDtypeStruct((2 * line * SLOTS, 128), jnp.float32),
+            jax.ShapeDtypeStruct((2 * line * plane, 2 * line * SLOTS), jnp.float32),
         ],
         compiler_params=GRANT,
         cost_estimate=pl.CostEstimate(
             flops=2_000_000_000, bytes_accessed=1048576, transcendentals=0
         ),
         name="route_rows",
-    )(list_ids.reshape(1, count), owner_map.reshape(-1, 128))
+    )(spot, list_ids.reshape(1, count), owner_map.reshape(-1, 128))
 
 
 def place_kernel(capacity, target_ref, first_ref, second_ref, out_ref):
@@ -387,6 +388,11 @@
     return lax.ppermute(value, axis, [(i, (i + step) % size) for i in range(size)])
 
 
+def pair_sum(value, axis, distance):
+    size = lax.axis_size(axis)
+    return value + lax.ppermute(value, axis, [(i, i ^ distance) for i in range(size)])
+
+
 def local(embeddings, sketch_seed, list_ids, owner_map):
     row_count, dim = embeddings.shape
     rank = sketch_seed.shape[1]
@@ -394,21 +400,21 @@
     plane = lax.axis_size("y") * lax.axis_size("z")
     chips = plane * line
     dev_count = cores * chips
-    core = lax.axis_index("narrow")
-    spot = lax.axis_index("x").reshape(1)
+    core, here = lax.axis_index("narrow"), lax.axis_index("x")
     own_half, other_half = core.reshape(1), (1 - core).reshape(1)
-    piece, gram_piece = dim // dev_count, rank // chips
+    piece = dim // dev_count
+    capacity = 4 * row_count // dev_count
     seed_matrix = sketch_seed.astype(jnp.bfloat16)
     sketch = jnp.dot(embeddings, seed_matrix, preferred_element_type=jnp.float32).astype(
         jnp.bfloat16
     )
-
-    capacity = 4 * row_count // dev_count
-    here = lax.axis_index("x")
-    dest_index, labels = route_rows(list_ids, owner_map, capacity, line, plane)
+    embeddings = jnp.where(core >= 0, embeddings, jnp.bfloat16(0))
+    list_ids, sketch = lax.optimization_barrier((list_ids, sketch))
+    spot = (core * line + here).reshape(1)
+    dest_index, labels = route_rows(spot, list_ids, owner_map, capacity, line, plane)
 
     def chunk_at(step):
-        where = jnp.stack([(here + step) % line, core, here, jnp.int32(line)])
+        where = jnp.stack([(here + step) % line, core, jnp.int32(line)])
         give, keep = cross_chunk(where, embeddings, sketch, labels, line)
         return keep, shift(give, "narrow", 1)
 
@@ -419,16 +425,29 @@
     from_below = shift(join_chunk(*up, from_below, 0), "x", 1)
     from_above = shift(join_chunk(*down, from_above, 1), "x", line - 1)
 
-    packed = line_total([*near, from_below, from_above], plane, gram_piece)
+    gram = lax.dot_general(sketch, sketch, ROW_DIMS, preferred_element_type=jnp.float32)
+    gram_give = lax.dynamic_slice_in_dim(gram, (1 - core) * (rank // 2), rank // 2)
+    gram = lax.dynamic_slice_in_dim(gram, core * (rank // 2), rank // 2)
+    gram = gram + shift(gram_give, "narrow", 1)
+    steps = []
+    for axis in ("x", "y", "z"):
+        distance = 1
+        while distance < lax.axis_size(axis):
+            gram = pair_sum(gram, axis, distance)
+            steps.append(gram)
+            distance *= 2
+    gram_parts = [gram, shift(gram, "narrow", 1)]
+
+    packed = line_total([*near, from_below, from_above], plane)
+    packed, _ = lax.optimization_barrier((packed, steps[-2]))
     packed = lax.all_to_all(packed, PLANE, 0, 0, tiled=True)
-    packed, arrived_labels = plane_total(packed, piece + gram_piece)
+    packed, gram_parts = lax.optimization_barrier((packed, gram_parts))
+    inverse = invert_factor(own_half, gram_parts)
+    packed, arrived_labels = plane_total(packed, piece)
     packed = lax.all_to_all(packed, PLANE, 0, 0, tiled=True)
-    gram_line = packed[:, piece : piece + gram_piece].reshape(-1, rank)
-    gram_parts = [gram_line] + [shift(gram_line, "x", step) for step in range(1, line)]
-    packed, gram_parts[1] = lax.optimization_barrier((packed, gram_parts[1]))
-    cross_line = packed[:, :piece].reshape(-1, rank)
+    cross_line = packed.reshape(-1, rank)
     cross_parts = [cross_line] + [shift(cross_line, "x", step) for step in range(1, line)]
-    arrived_labels = arrived_labels[:, : cores * line * SLOTS].reshape(plane, cores, line, SLOTS)
+    arrived_labels = arrived_labels.reshape(plane, cores, line, SLOTS)
     arrived_labels = arrived_labels[..., :capacity].transpose(1, 0, 2, 3)
 
     both_dest = jnp.concatenate([dest_index, shift(dest_index, "narrow", 1)])
@@ -437,10 +456,10 @@
     target = jnp.where(both_owner // chips == core, target, -1)
     target = jnp.where(core == 0, target, target[::-1])
 
-    inverse = invert_factor(spot, gram_parts)
-    inverse, cross_parts = lax.optimization_barrier((inverse, cross_parts))
+    cross_parts, inverse = lax.optimization_barrier((cross_parts, inverse))
     moment = moment_of(cross_parts)
-    basis = project_half(spot, inverse, moment, shift(moment, "narrow", 1), cross_parts)
+    other_moment = shift(moment, "narrow", 1)
+    basis = project_half(here.reshape(1), inverse, moment, other_moment, cross_parts)
     other_basis = shift(basis, "narrow", 1)
     begun = product_of_half(own_half, embeddings, basis, None, jnp.float32)
     reduced = product_of_half(other_half, embeddings, other_basis, begun, jnp.bfloat16)

time: 212 us -> 228 us (1.075)
  blocking collectives: 58.6 us -> 23.7 us
  starting transfers between devices: 22.9 us -> 47.3 us
  waiting for transfers between devices: 77.8 us -> 97.8 us
  other arithmetic: 1.56 us -> 8.5 us
    ppermute x0 -> x7, waiting for transfers between devices: none -> 39.2 us  [pair_sum(): lax.ppermute(value, axis, [(i, i ^ distance) for i in range(size)])]
    all_to_all x2 -> x1, blocking collectives: 58.6 us -> 23.7 us  [local(): packed = lax.all_to_all(packed, PLANE, 0, 0, tiled=True)]
    ppermute x18 -> x17, waiting for transfers between devices: 36.9 us -> 17.9 us  [shift(): lax.ppermute(value, axis, [(i, (i + step) % size) for i in range(size)])]
    ppermute x0 -> x7, starting transfers between devices: none -> 16.7 us  [pair_sum(): lax.ppermute(value, axis, [(i, i ^ distance) for i in range(size)])]
    all_to_all x0 -> x1, starting transfers between devices: none -> 11.6 us  [local(): packed = lax.all_to_all(packed, PLANE, 0, 0, tiled=True)]
    select_n x0 -> x1, other arithmetic: none -> 5.96 us  [local(): embeddings = jnp.where(core >= 0, embeddings, jnp.bfloat16(0))]
    ppermute x18 -> x17, starting transfers between devices: 14.8 us -> 11.2 us  [shift(): lax.ppermute(value, axis, [(i, (i + step) % size) for i in range(size)])]
    unnamed x17 -> x15, local copies, waits for them, and re-layouts: 7.83 us -> 7.1 us
  transfers between devices with their start and end apart: 19 -> 26, of which waited for: 10 -> 14; matrix products, arithmetic and copies ran while one was open for 1% -> 2% of each run, Pallas kernels for 9% -> 7%
where the time goes in v3:
time: 228 us
  waiting for transfers between devices  97.8 us (43%)
  starting transfers between devices  47.3 us (21%)
  Pallas kernels  33.8 us (15%)
  blocking collectives  23.7 us (10%)
  local copies, waits for them, and re-layouts  9.82 us (4%)
  other arithmetic  8.5 us (4%)
  matrix products  6.11 us (3%)
    all_to_all x1, waiting for transfers between devices, local(): arrived = lax.all_to_all(send_rows, ('y', 'z', 'x'), 0, 0, tiled=True)  40.7 us
    ppermute x7, waiting for transfers between devices, pair_sum(): lax.ppermute(value, axis, [(i, i ^ distance) for i in range(size)])  39.2 us
    all_to_all x1, blocking collectives, local(): packed = lax.all_to_all(packed, PLANE, 0, 0, tiled=True)  23.7 us
    ppermute x17, waiting for transfers between devices, shift(): lax.ppermute(value, axis, [(i, (i + step) % size) for i in range(size)])  17.9 us
    ppermute x7, starting transfers between devices, pair_sum(): lax.ppermute(value, axis, [(i, i ^ distance) for i in range(size)])  16.7 us
    all_to_all x1, starting transfers between devices, local(): packed = lax.all_to_all(packed, PLANE, 0, 0, tiled=True)  11.6 us
    ppermute x17, starting transfers between devices, shift(): lax.ppermute(value, axis, [(i, (i + step) % size) for i in range(size)])  11.2 us
    pallas_call x1, Pallas kernels, invert_factor(): pl.pallas_call(invert_kernel, in_specs=[pl.BlockSpec(memory_space=pltpu.S...  10.8 us
  transfers between devices with their start and end apart: 26, of which 14 were waited for; matrix products, arithmetic and copies ran while one was open for 2% of the time, Pallas kernels for 7%

profile of v3, /device:TPU:32, one launch (start us, length us, event | category | flops | bytes accessed | tf_op | source)
XLA Modules:
  0.0 227.9 jit_solution(14932256465880099265)
XLA Ops:
  0.7 5.8 %fusion.2.sketch_ref = bf16[768,256]{1,0:T(8,128)(2,1)S(1)} fusion(bf16[768,4096]{1,0:T(8,128)(2,1)} %param.4, s32[4096,256]{1,0:T(8,128)} %param.5), kind=kOutput, calls=%fused_computation.3 | convolution fusion | flops 1611857920 | bytes 10878976 | tf_op jit(solution)/shard_map/dot_general | solution.py:408
  6.5 6.0 %broadcast_select_fusion.rows_ref = bf16[768,4096]{1,0:T(8,128)(2,1)} fusion(bf16[768,4096]{1,0:T(8,128)(2,1)} %param.4, pred[]{:T(512)S(6)} %ge.3), kind=kLoop, calls=%fused_computation | loop fusion | flops 3145728 | bytes 12582913 | tf_op jit(solution)/shard_map/jit(_where)/select_n | solution.py:411
  18.6 2.8 %copy-done.1 = bf16[768,4096]{1,0:T(8,128)(2,1)S(1)} copy-done((bf16[768,4096]{1,0:T(8,128)(2,1)S(1)}, bf16[768,4096]{1,0:T(8,128)(2,1)}, u32[]{:S(2)}) %copy-start.1) | copy-done | bytes 6291480
  31.2 8.1 %collective-permute-done.10 = f32[128,256]{1,0:T(8,128)S(1)} collective-permute-done((f32[128,256]{1,0:T(8,128)S(1)}, f32[128,256]{1,0:T(8,128)S(1)}, u32[]{:S(2)}, u32[]{:S(2)}) %collective-permute-start.10) | collective-permute-done | bytes 131104 | tf_op jit(solution)/shard_map/ppermute | solution.py:393
  39.3 2.8 %collective-permute-start.11 = (f32[128,256]{1,0:T(8,128)S(1)}, f32[128,256]{1,0:T(8,128)S(1)}, u32[]{:S(2)}, u32[]{:S(2)}) collective-permute-start(f32[128,256]{1,0:T(8,128)S(1)} %add.88), channel_id=1, source_target_pairs={{0,2},{1,3},{2,0},{3,1},{4,6},{5,7},{6,4},{7,5},{8,10},{9,11},{10,... | collective-permute-start | bytes 393224 | tf_op jit(solution)/shard_map/ppermute | solution.py:393
  42.1 2.8 %copy-done.2 = bf16[768,4096]{1,0:T(8,128)(2,1)S(1)} copy-done((bf16[768,4096]{1,0:T(8,128)(2,1)S(1)}, bf16[768,4096]{1,0:T(8,128)(2,1)}, u32[]{:S(2)}) %copy-start.2) | copy-done | bytes 6291480
  46.6 3.3 %collective-permute-start.8 = (f32[264,512]{1,0:T(8,128)S(1)}, f32[264,512]{1,0:T(8,128)S(1)}, u32[]{:S(2)}, u32[]{:S(2)}) collective-permute-start(f32[264,512]{1,0:T(8,128)S(1)} %join_chunk.3), channel_id=1, source_target_pairs={{0,3},{1,0},{2,1},{3,2},{4,7},{5,4},{6,5},{7,6},{8,11},{9,8},{10,9... | collective-permute-start | bytes 1622024 | tf_op jit(solution)/shard_map/ppermute | solution.py:388
  51.6 3.8 %collective-permute-done.12 = f32[128,256]{1,0:T(8,128)S(1)} collective-permute-done((f32[128,256]{1,0:T(8,128)S(1)}, f32[128,256]{1,0:T(8,128)S(1)}, u32[]{:S(2)}, u32[]{:S(2)}) %collective-permute-start.12) | collective-permute-done | bytes 131104 | tf_op jit(solution)/shard_map/ppermute | solution.py:393
  55.4 3.3 %collective-permute-start.13 = (f32[128,256]{1,0:T(8,128)S(1)}, f32[128,256]{1,0:T(8,128)S(1)}, u32[]{:S(2)}, u32[]{:S(2)}) collective-permute-start(f32[128,256]{1,0:T(8,128)S(1)} %add.90), channel_id=1, source_target_pairs={{0,64},{32,96},{64,0},{96,32},{1,65},{33,97},{65,1},{97,33},{2,66}... | collective-permute-start | bytes 393224 | tf_op jit(solution)/shard_map/ppermute | solution.py:393
  58.6 3.3 %collective-permute-done.13 = f32[128,256]{1,0:T(8,128)S(1)} collective-permute-done((f32[128,256]{1,0:T(8,128)S(1)}, f32[128,256]{1,0:T(8,128)S(1)}, u32[]{:S(2)}, u32[]{:S(2)}) %collective-permute-start.13) | collective-permute-done | bytes 131104 | tf_op jit(solution)/shard_map/ppermute | solution.py:393
  62.6 4.4 %collective-permute-done.14 = f32[128,256]{1,0:T(8,128)S(1)} collective-permute-done((f32[128,256]{1,0:T(8,128)S(1)}, f32[128,256]{1,0:T(8,128)S(1)}, u32[]{:S(2)}, u32[]{:S(2)}) %collective-permute-start.14) | collective-permute-done | bytes 131104 | tf_op jit(solution)/shard_map/ppermute | solution.py:393
  67.0 3.3 %collective-permute-start.15 = (f32[128,256]{1,0:T(8,128)S(1)}, f32[128,256]{1,0:T(8,128)S(1)}, u32[]{:S(2)}, u32[]{:S(2)}) collective-permute-start(f32[128,256]{1,0:T(8,128)S(1)} %add.92), channel_id=1, source_target_pairs={{0,8},{4,12},{8,0},{12,4},{16,24},{20,28},{24,16},{28,20},{1,9},{5... | collective-permute-start | bytes 393224 | tf_op jit(solution)/shard_map/ppermute | solution.py:393
  70.4 3.8 %collective-permute-done.15 = f32[128,256]{1,0:T(8,128)S(1)} collective-permute-done((f32[128,256]{1,0:T(8,128)S(1)}, f32[128,256]{1,0:T(8,128)S(1)}, u32[]{:S(2)}, u32[]{:S(2)}) %collective-permute-start.15) | collective-permute-done | bytes 131104 | tf_op jit(solution)/shard_map/ppermute | solution.py:393
  75.3 11.6 %all-to-all-start = ((f32[32,40,128]{2,1,0:T(8,128)}), f32[32,40,128]{2,1,0:T(8,128)S(1)}, u32[]{:S(2)}, u32[]{:S(2)}) async-start(f32[32,40,128]{2,1,0:T(8,128)} %line_total.1), calls=%async_computation | async-start | bytes 1310720 | tf_op jit(solution)/shard_map/all_to_all | solution.py:443
  86.9 4.6 %collective-permute-start.16 = (f32[128,256]{1,0:T(8,128)S(1)}, f32[128,256]{1,0:T(8,128)S(1)}, u32[]{:S(2)}, u32[]{:S(2)}) collective-permute-start(f32[128,256]{1,0:T(8,128)S(1)} %add.93), channel_id=1, source_target_pairs={{0,16},{4,20},{8,24},{12,28},{16,0},{20,4},{24,8},{28,12},{1,17},{... | collective-permute-start | bytes 393224 | tf_op jit(solution)/shard_map/ppermute | solution.py:393
  91.4 15.9 %collective-permute-done.16 = f32[128,256]{1,0:T(8,128)S(1)} collective-permute-done((f32[128,256]{1,0:T(8,128)S(1)}, f32[128,256]{1,0:T(8,128)S(1)}, u32[]{:S(2)}, u32[]{:S(2)}) %collective-permute-start.16) | collective-permute-done | bytes 131104 | tf_op jit(solution)/shard_map/ppermute | solution.py:393
  108.9 23.7 %all_to_all.15 = f32[32,16,256]{2,1,0:T(8,128)S(1)} all-to-all(f32[32,16,256]{2,1,0:T(8,128)S(1)} %get-tuple-element.39), channel_id=1, replica_groups=mesh['narrow'=2,'y'=4,'z'=8,'x'=4] {'y','z'}, dimensions={0} | all-to-all | bytes 1048576 | tf_op jit(solution)/shard_map/all_to_all | solution.py:447
  134.5 10.8 %invert_factor.1.inverse_ref = f32[256,256]{1,0:T(8,128)S(1)} custom-call(s32[1]{0:T(128)} %bitcast.5.spot_ref.core_ref, f32[128,256]{1,0:T(8,128)S(1)} %add.94.refs_0_, f32[128,256]{1,0:T(8,128)S(1)} %collective-permute-done.17.refs_1_), custom_call_target="tpu_custom_call" | custom-call | flops 20000000000 | bytes 524288 | tf_op jit(solution)/shard_map/invert_factor/pallas_call | solution.py:89
  147.4 2.4 %collective-permute-done.19.refs_2_ = f32[512,256]{1,0:T(8,128)S(1)} collective-permute-done((f32[512,256]{1,0:T(8,128)S(1)}, f32[512,256]{1,0:T(8,128)S(1)}, u32[]{:S(2)}, u32[]{:S(2)}) %collective-permute-start.19) | collective-permute-done | bytes 524320 | tf_op jit(solution)/shard_map/ppermute | solution.py:388
  149.8 7.8 %collective-permute-done.18.refs_1_ = f32[512,256]{1,0:T(8,128)S(1)} collective-permute-done((f32[512,256]{1,0:T(8,128)S(1)}, f32[512,256]{1,0:T(8,128)S(1)}, u32[]{:S(2)}, u32[]{:S(2)}) %collective-permute-start.18) | collective-permute-done | bytes 524320 | tf_op jit(solution)/shard_map/ppermute | solution.py:388
  161.6 6.3 %project_half.1.basis_ref = bf16[2048,256]{1,0:T(8,128)(2,1)S(1)} custom-call(s32[1]{0:T(128)} %bitcast.3.spot_ref, f32[256,256]{1,0:T(8,128)S(1)} %invert_factor.1.inverse_ref, f32[256,256]{1,0:T(8,128)S(1)} %moment_of.1.moment_ref, f32[256,256]{1,0:T(8,128)S(1)} %collective-permute-done.21.other_ref, f32[512,256]{1,0:T(8,128)S(1)} %bitcast.28, ...), custom_call_target="tpu_custom_call" | custom-call | flops 12000000000 | bytes 4194304 | tf_op jit(solution)/shard_map/project_half/pallas_call | solution.py:152
  173.9 2.9 %place_rows.1 = bf16[64,48,256]{2,1,0:T(8,128)(2,1)} custom-call(s32[2,768]{1,0:T(2,128)S(1)} %broadcast_select_fusion.3.target_ref, bf16[768,256]{1,0:T(8,128)(2,1)S(1)} %get-tuple-element.55.first_ref, bf16[768,256]{1,0:T(8,128)(2,1)S(1)} %get-tuple-element.54.second_ref), custom_call_target="tpu_custom_call" | custom-call | flops 1207959552 | bytes 3145728 | tf_op jit(solution)/shard_map/place_rows/pallas_call | solution.py:369
  176.9 7.8 %all-to-all-start.2 = ((bf16[128,24,256]{2,1,0:T(8,128)(2,1)}), bf16[128,24,256]{2,1,0:T(8,128)(2,1)S(1)}, u32[]{:S(2)}, u32[]{:S(2)}) async-start(bf16[128,24,256]{2,1,0:T(8,128)(2,1)} %bitcast.10), calls=%async_computation.2 | async-start | bytes 3145728 | tf_op jit(solution)/shard_map/all_to_all | solution.py:475
  185.6 40.7 %all-to-all-done.2 = bf16[128,24,256]{2,1,0:T(8,128)(2,1)S(1)} async-done(((bf16[128,24,256]{2,1,0:T(8,128)(2,1)}), bf16[128,24,256]{2,1,0:T(8,128)(2,1)S(1)}, u32[]{:S(2)}, u32[]{:S(2)}) %all-to-all-start.2) | async-done | bytes 1572896 | tf_op jit(solution)/shard_map/all_to_all | solution.py:475
  (87 shorter events, 39.1 us)
Async XLA Ops:
  17.0 8.4 %collective-permute-start.3 = (f32[264,512]{1,0:T(8,128)}, f32[264,512]{1,0:T(8,128)}, u32[]{:S(2)}, u32[]{:S(2)}) collective-permute-start(f32[264,512]{1,0:T(8,128)} %get-tuple-element.34), channel_id=1, source_target_pairs={{0,128},{128,0},{1,129},{129,1},{2,130},{130,2},{3,131},{131,3},{4... | collective-permute-start | bytes 1622024 | tf_op jit(solution)/shard_map/ppermute | solution.py:388
  18.0 12.0 %collective-permute-start.9 = (f32[128,256]{1,0:T(8,128)}, f32[128,256]{1,0:T(8,128)}, u32[]{:S(2)}, u32[]{:S(2)}) collective-permute-start(f32[128,256]{1,0:T(8,128)} %constant_dynamic-slice_fusion), channel_id=1, source_target_pairs={{0,128},{128,0},{1,129},{129,1},{2,130},{130,2},{3,131},{131,3},{4... | collective-permute-start | bytes 393224 | tf_op jit(solution)/shard_map/ppermute | solution.py:388
  23.1 23.0 %collective-permute-start.2 = (f32[264,512]{1,0:T(8,128)}, f32[264,512]{1,0:T(8,128)S(1)}, u32[]{:S(2)}, u32[]{:S(2)}) collective-permute-start(f32[264,512]{1,0:T(8,128)} %get-tuple-element.32), channel_id=1, source_target_pairs={{0,128},{128,0},{1,129},{129,1},{2,130},{130,2},{3,131},{131,3},{4... | collective-permute-start | bytes 1622024 | tf_op jit(solution)/shard_map/ppermute | solution.py:388
  24.9 21.7 %collective-permute-start.6 = (f32[264,512]{1,0:T(8,128)}, f32[264,512]{1,0:T(8,128)S(1)}, u32[]{:S(2)}, u32[]{:S(2)}) collective-permute-start(f32[264,512]{1,0:T(8,128)} %get-tuple-element.36), channel_id=1, source_target_pairs={{0,128},{128,0},{1,129},{129,1},{2,130},{130,2},{3,131},{131,3},{4... | collective-permute-start | bytes 1622024 | tf_op jit(solution)/shard_map/ppermute | solution.py:388
  26.6 19.6 %collective-permute-start.4 = (f32[128,512]{1,0:T(8,128)S(1)}, f32[128,512]{1,0:T(8,128)S(1)}, u32[]{:S(2)}, u32[]{:S(2)}) collective-permute-start(f32[128,512]{1,0:T(8,128)S(1)} %slice.12), channel_id=1, source_target_pairs={{0,1},{1,2},{2,3},{3,0},{4,5},{5,6},{6,7},{7,4},{8,9},{9,10},{10,1... | collective-permute-start | bytes 786440 | tf_op jit(solution)/shard_map/ppermute | solution.py:388
  28.2 18.4 %collective-permute-start.7 = (f32[136,512]{1,0:T(8,128)S(1)}, f32[136,512]{1,0:T(8,128)S(1)}, u32[]{:S(2)}, u32[]{:S(2)}) collective-permute-start(f32[136,512]{1,0:T(8,128)S(1)} %slice.13), channel_id=1, source_target_pairs={{0,3},{1,0},{2,1},{3,2},{4,7},{5,4},{6,5},{7,6},{8,11},{9,8},{10,9... | collective-permute-start | bytes 835592 | tf_op jit(solution)/shard_map/ppermute | solution.py:388
  30.8 8.4 %collective-permute-start.10 = (f32[128,256]{1,0:T(8,128)S(1)}, f32[128,256]{1,0:T(8,128)S(1)}, u32[]{:S(2)}, u32[]{:S(2)}) collective-permute-start(f32[128,256]{1,0:T(8,128)S(1)} %dynamic-slice_add_fusion), channel_id=1, source_target_pairs={{0,1},{1,0},{2,3},{3,2},{4,5},{5,4},{6,7},{7,6},{8,9},{9,8},{10,11... | collective-permute-start | bytes 393224 | tf_op jit(solution)/shard_map/ppermute | solution.py:393
  39.3 10.6 %collective-permute-start.11 = (f32[128,256]{1,0:T(8,128)S(1)}, f32[128,256]{1,0:T(8,128)S(1)}, u32[]{:S(2)}, u32[]{:S(2)}) collective-permute-start(f32[128,256]{1,0:T(8,128)S(1)} %add.88), channel_id=1, source_target_pairs={{0,2},{1,3},{2,0},{3,1},{4,6},{5,7},{6,4},{7,5},{8,10},{9,11},{10,... | collective-permute-start | bytes 393224 | tf_op jit(solution)/shard_map/ppermute | solution.py:393
  46.1 28.1 %collective-permute-start.1 = (f32[264,512]{1,0:T(8,128)S(1)}, f32[264,512]{1,0:T(8,128)S(1)}, u32[]{:S(2)}, u32[]{:S(2)}) collective-permute-start(f32[264,512]{1,0:T(8,128)S(1)} %get-tuple-element.30), channel_id=1, source_target_pairs={{0,128},{128,0},{1,129},{129,1},{2,130},{130,2},{3,131},{131,3},{4... | collective-permute-start | bytes 1622024 | tf_op jit(solution)/shard_map/ppermute | solution.py:388
  46.3 27.9 %collective-permute-start.5 = (f32[264,512]{1,0:T(8,128)S(1)}, f32[264,512]{1,0:T(8,128)S(1)}, u32[]{:S(2)}, u32[]{:S(2)}) collective-permute-start(f32[264,512]{1,0:T(8,128)S(1)} %join_chunk.2), channel_id=1, source_target_pairs={{0,1},{1,2},{2,3},{3,0},{4,5},{5,6},{6,7},{7,4},{8,9},{9,10},{10,1... | collective-permute-start | bytes 1622024 | tf_op jit(solution)/shard_map/ppermute | solution.py:388
  46.6 27.6 %collective-permute-start.8 = (f32[264,512]{1,0:T(8,128)S(1)}, f32[264,512]{1,0:T(8,128)S(1)}, u32[]{:S(2)}, u32[]{:S(2)}) collective-permute-start(f32[264,512]{1,0:T(8,128)S(1)} %join_chunk.3), channel_id=1, source_target_pairs={{0,3},{1,0},{2,1},{3,2},{4,7},{5,4},{6,5},{7,6},{8,11},{9,8},{10,9... | collective-permute-start | bytes 1622024 | tf_op jit(solution)/shard_map/ppermute | solution.py:388
  49.9 5.4 %collective-permute-start.12 = (f32[128,256]{1,0:T(8,128)S(1)}, f32[128,256]{1,0:T(8,128)S(1)}, u32[]{:S(2)}, u32[]{:S(2)}) collective-permute-start(f32[128,256]{1,0:T(8,128)S(1)} %add.89), channel_id=1, source_target_pairs={{0,32},{32,0},{64,96},{96,64},{1,33},{33,1},{65,97},{97,65},{2,34}... | collective-permute-start | bytes 393224 | tf_op jit(solution)/shard_map/ppermute | solution.py:393
  55.4 6.6 %collective-permute-start.13 = (f32[128,256]{1,0:T(8,128)S(1)}, f32[128,256]{1,0:T(8,128)S(1)}, u32[]{:S(2)}, u32[]{:S(2)}) collective-permute-start(f32[128,256]{1,0:T(8,128)S(1)} %add.90), channel_id=1, source_target_pairs={{0,64},{32,96},{64,0},{96,32},{1,65},{33,97},{65,1},{97,33},{2,66}... | collective-permute-start | bytes 393224 | tf_op jit(solution)/shard_map/ppermute | solution.py:393
  62.0 5.1 %collective-permute-start.14 = (f32[128,256]{1,0:T(8,128)S(1)}, f32[128,256]{1,0:T(8,128)S(1)}, u32[]{:S(2)}, u32[]{:S(2)}) collective-permute-start(f32[128,256]{1,0:T(8,128)S(1)} %add.91), channel_id=1, source_target_pairs={{0,4},{4,0},{8,12},{12,8},{16,20},{20,16},{24,28},{28,24},{1,5},{5... | collective-permute-start | bytes 393224 | tf_op jit(solution)/shard_map/ppermute | solution.py:393
  67.0 7.1 %collective-permute-start.15 = (f32[128,256]{1,0:T(8,128)S(1)}, f32[128,256]{1,0:T(8,128)S(1)}, u32[]{:S(2)}, u32[]{:S(2)}) collective-permute-start(f32[128,256]{1,0:T(8,128)S(1)} %add.92), channel_id=1, source_target_pairs={{0,8},{4,12},{8,0},{12,4},{16,24},{20,28},{24,16},{28,20},{1,9},{5... | collective-permute-start | bytes 393224 | tf_op jit(solution)/shard_map/ppermute | solution.py:393
  75.3 33.5 %all-to-all-start = ((f32[32,40,128]{2,1,0:T(8,128)}), f32[32,40,128]{2,1,0:T(8,128)S(1)}, u32[]{:S(2)}, u32[]{:S(2)}) async-start(f32[32,40,128]{2,1,0:T(8,128)} %line_total.1), calls=%async_computation | async-start | bytes 1310720 | tf_op jit(solution)/shard_map/all_to_all | solution.py:443
  86.9 20.4 %collective-permute-start.16 = (f32[128,256]{1,0:T(8,128)S(1)}, f32[128,256]{1,0:T(8,128)S(1)}, u32[]{:S(2)}, u32[]{:S(2)}) collective-permute-start(f32[128,256]{1,0:T(8,128)S(1)} %add.93), channel_id=1, source_target_pairs={{0,16},{4,20},{8,24},{12,28},{16,0},{20,4},{24,8},{28,12},{1,17},{... | collective-permute-start | bytes 393224 | tf_op jit(solution)/shard_map/ppermute | solution.py:393
  132.5 14.9 %collective-permute-start.20 = (f32[512,256]{1,0:T(8,128)S(1)}, f32[512,256]{1,0:T(8,128)S(1)}, u32[]{:S(2)}, u32[]{:S(2)}) collective-permute-start(f32[512,256]{1,0:T(8,128)S(1)} %bitcast.24), channel_id=1, source_target_pairs={{0,3},{1,0},{2,1},{3,2},{4,7},{5,4},{6,5},{7,6},{8,11},{9,8},{10,9... | collective-permute-start | bytes 1572872 | tf_op jit(solution)/shard_map/ppermute | solution.py:388
  133.4 16.4 %collective-permute-start.19 = (f32[512,256]{1,0:T(8,128)S(1)}, f32[512,256]{1,0:T(8,128)S(1)}, u32[]{:S(2)}, u32[]{:S(2)}) collective-permute-start(f32[512,256]{1,0:T(8,128)S(1)} %bitcast.25), channel_id=1, source_target_pairs={{0,2},{1,3},{2,0},{3,1},{4,6},{5,7},{6,4},{7,5},{8,10},{9,11},{10,... | collective-permute-start | bytes 1572872 | tf_op jit(solution)/shard_map/ppermute | solution.py:388
  133.7 23.9 %collective-permute-start.18 = (f32[512,256]{1,0:T(8,128)S(1)}, f32[512,256]{1,0:T(8,128)S(1)}, u32[]{:S(2)}, u32[]{:S(2)}) collective-permute-start(f32[512,256]{1,0:T(8,128)S(1)} %bitcast.26), channel_id=1, source_target_pairs={{0,1},{1,2},{2,3},{3,0},{4,5},{5,6},{6,7},{7,4},{8,9},{9,10},{10,1... | collective-permute-start | bytes 1572872 | tf_op jit(solution)/shard_map/ppermute | solution.py:388
  159.8 1.8 collective-permute-start.21
  168.0 2.7 %collective-permute-start.22 = (bf16[2048,256]{1,0:T(8,128)(2,1)S(1)}, bf16[2048,256]{1,0:T(8,128)(2,1)S(1)}, u32[]{:S(2)}, u32[]{:S(2)}) collective-permute-start(bf16[2048,256]{1,0:T(8,128)(2,1)S(1)} %project_half.1.basis_ref), channel_id=1, source_target_pairs={{0,128},{128,0},{1,129},{129,1},{2,130},{130,2},{3,131},{131,3},{4... | collective-permute-start | bytes 3145736 | tf_op jit(solution)/shard_map/ppermute | solution.py:388
  171.7 2.1 collective-permute-start.23
  176.9 49.5 %all-to-all-start.2 = ((bf16[128,24,256]{2,1,0:T(8,128)(2,1)}), bf16[128,24,256]{2,1,0:T(8,128)(2,1)S(1)}, u32[]{:S(2)}, u32[]{:S(2)}) async-start(bf16[128,24,256]{2,1,0:T(8,128)(2,1)} %bitcast.10), calls=%async_computation.2 | async-start | bytes 3145728 | tf_op jit(solution)/shard_map/all_to_all | solution.py:475
  (9 other events, 40.3 us)

commit v4 on v2

--- a/solution.py
+++ b/solution.py
@@ -10,7 +10,7 @@
 
 NS_STEPS = 6
 BLOCK = 64
-TILE = 8
+TILE = 16
 ALL = ("narrow", "y", "z", "x")
 PLANE = ("y", "z")
 HIGHEST = lax.Precision.HIGHEST
@@ -100,14 +100,14 @@
 def moment_kernel(*refs):
     total = None
     for part_ref in refs[:-1]:
-        part = part_ref[...]
+        part = whole_rows(part_ref[...])
         term = dot_f32(part, part, ROW_DIMS)
         total = term if total is None else total + term
     refs[-1][...] = total
 
 
 def moment_of(parts):
-    rank = parts[0].shape[1]
+    rank = 2 * parts[0].shape[2]
     return pl.pallas_call(
         moment_kernel,
         out_shape=jax.ShapeDtypeStruct((rank, rank), jnp.float32),
@@ -143,11 +143,11 @@
     for step, part_ref in enumerate(parts):
         place = lax.rem(spot_ref[0] + len(parts) - step, len(parts))
         rows = pl.ds(pl.multiple_of(place * height, height), height)
-        out_ref[rows, :] = dot_split(split_two(part_ref[...]), weight).astype(jnp.bfloat16)
+        out_ref[rows, :] = dot_split(split_two(whole_rows(part_ref[...])), weight).astype(jnp.bfloat16)
 
 
 def project_half(spot, inverse, moment, other, parts):
-    chunk, rank = parts[0].shape
+    chunk, rank = parts[0].shape[0] * parts[0].shape[1] // 2, inverse.shape[0]
     return pl.pallas_call(
         whiten_kernel,
         in_specs=[pl.BlockSpec(memory_space=pltpu.SMEM)]
@@ -159,29 +159,31 @@
     )(spot, inverse, moment, other, *parts)
 
 
-def chunk_kernel(spot_ref, rows_ref, sketch_ref, label_ref, give_ref, keep_ref):
-    chunk, core, here, line = (spot_ref[i] for i in range(4))
+def chunk_kernel(spot_ref, rows_ref, sketch_ref, label_ref, *out_refs):
+    core, here, line = (spot_ref[i] for i in range(3))
     rank = sketch_ref.shape[1]
-    width = give_ref.shape[1] - 128
+    width = out_refs[0].shape[1] - 128
     half = rows_ref.shape[1] // 2
     sketch = sketch_ref[...]
     mul = functools.partial(
         lax.dot_general, dimension_numbers=ROW_DIMS, preferred_element_type=jnp.float32
     )
-    gram = mul(sketch, sketch)
-    gram = pltpu.roll(gram, rank - chunk * (rank * width // half), 1)[:, :128]
-    lane = lax.broadcasted_iota(jnp.int32, gram.shape, 1)
-    gram = jnp.where(lane < rank * width // half, gram, 0.0)
+    gram_whole = mul(sketch, sketch)
+    lane = lax.broadcasted_iota(jnp.int32, (rank, 128), 1)
     mine = pl.ds(pl.multiple_of((core * line + here) * SLOTS, SLOTS), SLOTS)
-    for out_ref, place in ((give_ref, 1 - core), (keep_ref, core)):
-        columns = pl.ds(pl.multiple_of(place * half + chunk * width, width), width)
-        out_ref[:, :width] = mul(sketch, rows_ref[:, columns])
-        out_ref[:, width:] = gram
-        theirs = pl.ds(pl.multiple_of((place * line + chunk) * SLOTS, SLOTS), SLOTS)
-        out_ref[mine, width:] += label_ref[theirs, :]
-
-
-def cross_chunk(spot, embeddings, sketch, labels, chunks):
+    for step in range(len(out_refs) // 2):
+        chunk = spot_ref[3 + step]
+        gram = pltpu.roll(gram_whole, rank - chunk * (rank * width // half), 1)[:, :128]
+        gram = jnp.where(lane < rank * width // half, gram, 0.0)
+        for out_ref, place in zip(out_refs[2 * step :], (1 - core, core)):
+            columns = pl.ds(pl.multiple_of(place * half + chunk * width, width), width)
+            out_ref[:, :width] = mul(sketch, rows_ref[:, columns])
+            out_ref[:, width:] = gram
+            theirs = pl.ds(pl.multiple_of((place * line + chunk) * SLOTS, SLOTS), SLOTS)
+            out_ref[mine, width:] += label_ref[theirs, :]
+
+
+def cross_chunks(spot, embeddings, sketch, labels, chunks, count):
     depth, dim = embeddings.shape
     rank = sketch.shape[1]
     width = dim // 2 // chunks
@@ -190,12 +192,12 @@
         chunk_kernel,
         in_specs=[pl.BlockSpec(memory_space=pltpu.SMEM)]
         + [pl.BlockSpec(memory_space=pltpu.VMEM)] * 3,
-        out_shape=[shape, shape],
+        out_shape=[shape] * (2 * count),
         compiler_params=GRANT,
         cost_estimate=pl.CostEstimate(
-            flops=2 * depth * rank * (2 * width + rank), bytes_accessed=3000000, transcendentals=0
+            flops=4 * depth * rank * width * count, bytes_accessed=3000000, transcendentals=0
         ),
-        name="cross_chunk",
+        name="cross_chunks",
     )(spot, embeddings, sketch, labels)
 
 
@@ -217,25 +219,30 @@
 
 def line_kernel(gram_piece, *refs):
     parts, out_ref = refs[:-1], refs[-1]
-    plane, _, rank = out_ref.shape
-    width = parts[0].shape[1] - 128
+    plane = out_ref.shape[0]
     total = parts[0][...] + parts[1][...]
     for part_ref in parts[2:]:
         total = total + part_ref[...]
+    rank, width = total.shape[0], total.shape[1] - 128
     piece = width // plane
-    out_ref[:, :piece, :] = total[:, :width].T.reshape(plane, piece, rank)
+    turned = total[:, :width].T.reshape(plane, piece, rank)
+    out_ref[:, :piece, :] = turned[:, :, :128]
+    out_ref[:, piece : 2 * piece, :] = turned[:, :, 128:]
     tail = total[:, width:].T.reshape(2, plane, gram_piece, rank)
-    fill = jnp.zeros((plane, out_ref.shape[1] - piece - 2 * gram_piece, rank), jnp.float32)
-    out_ref[:, piece:, :] = jnp.concatenate([tail[0], tail[1], fill], axis=1)
+    gram, labels = tail[0], tail[1][:, :1, :128]
+    fill = jnp.zeros((plane, out_ref.shape[1] - 2 * (piece + gram_piece) - 1, 128), jnp.float32)
+    out_ref[:, 2 * piece :, :] = jnp.concatenate(
+        [gram[:, :, :128], gram[:, :, 128:], labels, fill], axis=1
+    )
 
 
 def line_total(parts, plane, gram_piece):
-    rank, width = parts[0].shape
-    rows = (width - 128) // plane + 2 * gram_piece
+    width = parts[0].shape[1] - 128
+    rows = 2 * (width // plane + gram_piece) + 1
     rows += -rows % 8
     return pl.pallas_call(
         functools.partial(line_kernel, gram_piece),
-        out_shape=jax.ShapeDtypeStruct((plane, rows, rank), jnp.float32),
+        out_shape=jax.ShapeDtypeStruct((plane, rows, 128), jnp.float32),
         compiler_params=GRANT,
         cost_estimate=pl.CostEstimate(flops=1000000, bytes_accessed=4000000, transcendentals=0),
         name="line_total",
@@ -248,17 +255,23 @@
 
 
 def plane_total(parts, label_row):
-    plane, _, rank = parts.shape
+    plane, _, lanes = parts.shape
     return pl.pallas_call(
         functools.partial(plane_kernel, label_row),
         out_shape=[
             jax.ShapeDtypeStruct(parts.shape, jnp.float32),
-            jax.ShapeDtypeStruct((plane, rank), jnp.int32),
+            jax.ShapeDtypeStruct((plane, lanes), jnp.int32),
         ],
         compiler_params=GRANT,
         cost_estimate=pl.CostEstimate(flops=1000000, bytes_accessed=1600000, transcendentals=0),
         name="plane_total",
     )(parts)
+
+
+def whole_rows(part):
+    plane, pair, lanes = part.shape
+    sides = [part[:, : pair // 2], part[:, pair // 2 :]]
+    return jnp.concatenate([t.reshape(plane * pair // 2, lanes) for t in sides], axis=1)
 
 
 def product_kernel(core_ref, rows_ref, basis_ref, *refs):
@@ -407,35 +420,40 @@
     here = lax.axis_index("x")
     dest_index, labels = route_rows(list_ids, owner_map, capacity, line, plane)
 
-    def chunk_at(step):
-        where = jnp.stack([(here + step) % line, core, here, jnp.int32(line)])
-        give, keep = cross_chunk(where, embeddings, sketch, labels, line)
-        return keep, shift(give, "narrow", 1)
-
-    far, up, down, near = (chunk_at(step) for step in (2, 1, 3, 0))
+    def chunks_at(*steps):
+        places = [(here + step) % line for step in steps]
+        spot = jnp.stack([core, here, jnp.int32(line)] + places)
+        pairs = cross_chunks(spot, embeddings, sketch, labels, line, len(steps))
+        return [(pairs[2 * i + 1], shift(pairs[2 * i], "narrow", 1)) for i in range(len(steps))]
+
+    (far,) = chunks_at(2)
+    up, down, near = chunks_at(1, 3, 0)
     far = far[0] + far[1]
     from_below = shift(far[: rank // 2], "x", 1)
     from_above = shift(far[rank // 2 :], "x", line - 1)
     from_below = shift(join_chunk(*up, from_below, 0), "x", 1)
     from_above = shift(join_chunk(*down, from_above, 1), "x", line - 1)
 
-    packed = line_total([*near, from_below, from_above], plane, gram_piece)
-    packed = lax.all_to_all(packed, PLANE, 0, 0, tiled=True)
-    packed, arrived_labels = plane_total(packed, piece + gram_piece)
-    packed = lax.all_to_all(packed, PLANE, 0, 0, tiled=True)
-    gram_line = packed[:, piece : piece + gram_piece].reshape(-1, rank)
-    gram_parts = [gram_line] + [shift(gram_line, "x", step) for step in range(1, line)]
-    packed, gram_parts[1] = lax.optimization_barrier((packed, gram_parts[1]))
-    cross_line = packed[:, :piece].reshape(-1, rank)
-    cross_parts = [cross_line] + [shift(cross_line, "x", step) for step in range(1, line)]
-    arrived_labels = arrived_labels[:, : cores * line * SLOTS].reshape(plane, cores, line, SLOTS)
-    arrived_labels = arrived_labels[..., :capacity].transpose(1, 0, 2, 3)
-
     both_dest = jnp.concatenate([dest_index, shift(dest_index, "narrow", 1)])
     both_owner = both_dest // capacity
     target = (both_owner % chips) * capacity + both_dest % capacity
     target = jnp.where(both_owner // chips == core, target, -1)
     target = jnp.where(core == 0, target, target[::-1])
+
+    packed = line_total([*near, from_below, from_above], plane, gram_piece)
+    packed = lax.all_to_all(packed, PLANE, 0, 0, tiled=True)
+    packed, target = lax.optimization_barrier((packed, target))
+    packed, arrived_labels = plane_total(packed, 2 * (piece + gram_piece))
+    packed = lax.all_to_all(packed, PLANE, 0, 0, tiled=True)
+    gram_line = packed[:, 2 * piece : 2 * (piece + gram_piece)]
+    gram_line = jnp.concatenate([gram_line[:, :gram_piece], gram_line[:, gram_piece:]], axis=2)
+    gram_line = gram_line.reshape(-1, rank)
+    gram_parts = [gram_line] + [shift(gram_line, "x", step) for step in range(1, line)]
+    packed, gram_parts[1] = lax.optimization_barrier((packed, gram_parts[1]))
+    cross_line = packed[:, : 2 * piece]
+    cross_parts = [cross_line] + [shift(cross_line, "x", step) for step in range(1, line)]
+    arrived_labels = arrived_labels[:, : cores * line * SLOTS].reshape(plane, cores, line, SLOTS)
+    arrived_labels = arrived_labels[..., :capacity].transpose(1, 0, 2, 3)
 
     inverse = invert_factor(spot, gram_parts)
     inverse, cross_parts = lax.optimization_barrier((inverse, cross_parts))

time: 212 us -> 203 us (0.958)
  blocking collectives: 58.6 us -> 22.7 us
  waiting for transfers between devices: 77.8 us -> 98.5 us
  starting transfers between devices: 22.9 us -> 35.3 us
  Pallas kernels: 34.6 us -> 30.4 us
    all_to_all x2 -> x1, blocking collectives: 58.6 us -> 22.7 us  [local(): packed = lax.all_to_all(packed, PLANE, 0, 0, tiled=True)]
    all_to_all x0 -> x1, waiting for transfers between devices: none -> 17.3 us  [local(): packed = lax.all_to_all(packed, PLANE, 0, 0, tiled=True)]
    all_to_all x0 -> x1, starting transfers between devices: none -> 11.4 us  [local(): packed = lax.all_to_all(packed, PLANE, 0, 0, tiled=True)]
    ppermute x18, waiting for transfers between devices: 36.9 us -> 40.3 us  [shift(): lax.ppermute(value, axis, [(i, (i + step) % size) for i in range(size)])]
    pallas_call x4 -> x2, Pallas kernels: 6.33 us -> 3.36 us  [cross_chunks(): pl.pallas_call(chunk_kernel, in_specs=[pl.BlockSpec(memory_space=pltpu.SM...]
    unnamed x17 -> x9, local copies, waits for them, and re-layouts: 7.83 us -> 7.82 us
  transfers between devices with their start and end apart: 19 -> 20, of which waited for: 10 -> 12; matrix products, arithmetic and copies ran while one was open for 1% -> 1% of each run, Pallas kernels for 9% -> 7%
where the time goes in v4:
time: 203 us
  waiting for transfers between devices  98.5 us (49%)
  starting transfers between devices  35.3 us (17%)
  Pallas kernels  30.4 us (15%)
  blocking collectives  22.7 us (11%)
  local copies, waits for them, and re-layouts  10.8 us (5%)
  matrix products  4.02 us (2%)
    all_to_all x1, waiting for transfers between devices, local(): arrived = lax.all_to_all(send_rows, ('y', 'z', 'x'), 0, 0, tiled=True)  40.8 us
    ppermute x18, waiting for transfers between devices, shift(): lax.ppermute(value, axis, [(i, (i + step) % size) for i in range(size)])  40.3 us
    all_to_all x1, blocking collectives, local(): packed = lax.all_to_all(packed, PLANE, 0, 0, tiled=True)  22.7 us
    all_to_all x1, waiting for transfers between devices, local(): packed = lax.all_to_all(packed, PLANE, 0, 0, tiled=True)  17.3 us
    ppermute x18, starting transfers between devices, shift(): lax.ppermute(value, axis, [(i, (i + step) % size) for i in range(size)])  15.6 us
    all_to_all x1, starting transfers between devices, local(): packed = lax.all_to_all(packed, PLANE, 0, 0, tiled=True)  11.4 us
    pallas_call x1, Pallas kernels, invert_factor(): pl.pallas_call(invert_kernel, in_specs=[pl.BlockSpec(memory_space=pltpu.S...  10.8 us
    all_to_all x1, starting transfers between devices, local(): arrived = lax.all_to_all(send_rows, ('y', 'z', 'x'), 0, 0, tiled=True)  8.33 us
  transfers between devices with their start and end apart: 20, of which 12 were waited for; matrix products, arithmetic and copies ran while one was open for 1% of the time, Pallas kernels for 7%

profile of v4, /device:TPU:32, one launch (start us, length us, event | category | flops | bytes accessed | tf_op | source)
XLA Modules:
  0.0 203.0 jit_solution(1622235399075363197)
XLA Ops:
  4.4 4.0 %fusion.2.sketch_ref = bf16[768,256]{1,0:T(8,128)(2,1)S(1)} fusion(bf16[768,4096]{1,0:T(8,128)(2,1)S(1)} %copy-done, s32[4096,256]{1,0:T(8,128)} %param.5), kind=kOutput, calls=%fused_computation.2 | convolution fusion | flops 1611857920 | bytes 10878976 | tf_op jit(solution)/shard_map/dot_general | solution.py:415
  10.0 2.8 %copy-done.1 = bf16[768,4096]{1,0:T(8,128)(2,1)S(1)} copy-done((bf16[768,4096]{1,0:T(8,128)(2,1)S(1)}, bf16[768,4096]{1,0:T(8,128)(2,1)}, u32[]{:S(2)}) %copy-start.1) | copy-done | bytes 6291480
  12.8 2.1 %cross_chunks.2 = (f32[256,640]{1,0:T(8,128)S(1)}, f32[256,640]{1,0:T(8,128)S(1)}, f32[256,640]{1,0:T(8,128)S(1)}, f32[256,640]{1,0:T(8,128)S(1)}, f32[256,640]{1,0:T(8,128)S(1)}, /*index=5*/f32[256,640]{1,0:T(8,128)S(1)}) custom-call(s32[6]{0:T(128)S(1)} %stack.31.spot_ref, bf16[768,4096]{1,0:T(8,128)(2,1)S(1)} %copy-done.1, ...), custom_call_target="tpu_custom_call" | custom-call | flops 1207959552 | bytes 3000000 | tf_op jit(solution)/shard_map/cross_chunks/pallas_call | solution.py:191
  15.7 2.8 %collective-permute-start.6 = (f32[128,640]{1,0:T(8,128)S(1)}, f32[128,640]{1,0:T(8,128)S(1)}, u32[]{:S(2)}, u32[]{:S(2)}) collective-permute-start(f32[128,640]{1,0:T(8,128)S(1)} %get-tuple-element.54), channel_id=1, source_target_pairs={{0,3},{1,0},{2,1},{3,2},{4,7},{5,4},{6,5},{7,6},{8,11},{9,8},{10,9... | collective-permute-start | bytes 983048 | tf_op jit(solution)/shard_map/ppermute | solution.py:400
  18.7 7.4 %collective-permute-done.6.extra_ref = f32[128,640]{1,0:T(8,128)S(1)} collective-permute-done((f32[128,640]{1,0:T(8,128)S(1)}, f32[128,640]{1,0:T(8,128)S(1)}, u32[]{:S(2)}, u32[]{:S(2)}) %collective-permute-start.6) | collective-permute-done | bytes 327712 | tf_op jit(solution)/shard_map/ppermute | solution.py:400
  26.2 3.8 %collective-permute-start.7 = (f32[256,640]{1,0:T(8,128)S(1)}, f32[256,640]{1,0:T(8,128)S(1)}, u32[]{:S(2)}, u32[]{:S(2)}) collective-permute-start(f32[256,640]{1,0:T(8,128)S(1)} %join_chunk.3), channel_id=1, source_target_pairs={{0,3},{1,0},{2,1},{3,2},{4,7},{5,4},{6,5},{7,6},{8,11},{9,8},{10,9... | collective-permute-start | bytes 1966088 | tf_op jit(solution)/shard_map/ppermute | solution.py:400
  30.2 13.6 %collective-permute-done.7.refs_3_ = f32[256,640]{1,0:T(8,128)S(1)} collective-permute-done((f32[256,640]{1,0:T(8,128)S(1)}, f32[256,640]{1,0:T(8,128)S(1)}, u32[]{:S(2)}, u32[]{:S(2)}) %collective-permute-start.7) | collective-permute-done | bytes 655392 | tf_op jit(solution)/shard_map/ppermute | solution.py:400
  43.8 3.6 %collective-permute-done.4.refs_2_ = f32[256,640]{1,0:T(8,128)S(1)} collective-permute-done((f32[256,640]{1,0:T(8,128)S(1)}, f32[256,640]{1,0:T(8,128)S(1)}, u32[]{:S(2)}, u32[]{:S(2)}) %collective-permute-start.4) | collective-permute-done | bytes 655392 | tf_op jit(solution)/shard_map/ppermute | solution.py:400
  48.5 11.4 %all-to-all-start = ((f32[32,40,128]{2,1,0:T(8,128)}), f32[32,40,128]{2,1,0:T(8,128)S(1)}, u32[]{:S(2)}, u32[]{:S(2)}) async-start(f32[32,40,128]{2,1,0:T(8,128)} %line_total.1), calls=%async_computation | async-start | bytes 1310720 | tf_op jit(solution)/shard_map/all_to_all | solution.py:444
  61.6 17.3 %all-to-all-done.parts_ref = f32[32,40,128]{2,1,0:T(8,128)S(1)} async-done(((f32[32,40,128]{2,1,0:T(8,128)}), f32[32,40,128]{2,1,0:T(8,128)S(1)}, u32[]{:S(2)}, u32[]{:S(2)}) %all-to-all-start) | async-done | bytes 655392 | tf_op jit(solution)/shard_map/all_to_all | solution.py:444
  79.0 22.7 %all_to_all.15 = f32[32,40,128]{2,1,0:T(8,128)S(1)} all-to-all(f32[32,40,128]{2,1,0:T(8,128)S(1)} %get-tuple-element.35), channel_id=1, replica_groups=mesh['narrow'=2,'y'=4,'z'=8,'x'=4] {'y','z'}, dimensions={0} | all-to-all | bytes 1310720 | tf_op jit(solution)/shard_map/all_to_all | solution.py:447
  102.4 2.5 %collective-permute-start.10 = (f32[64,256]{1,0:T(8,128)S(1)}, f32[64,256]{1,0:T(8,128)S(1)}, u32[]{:S(2)}, u32[]{:S(2)}) collective-permute-start(f32[64,256]{1,0:T(8,128)S(1)} %reshape.36.refs_0_), channel_id=1, source_target_pairs={{0,2},{1,3},{2,0},{3,1},{4,6},{5,7},{6,4},{7,5},{8,10},{9,11},{10,... | collective-permute-start | bytes 196616 | tf_op jit(solution)/shard_map/ppermute | solution.py:400
  105.2 3.0 %collective-permute-done.9.refs_1_ = f32[64,256]{1,0:T(8,128)S(1)} collective-permute-done((f32[64,256]{1,0:T(8,128)S(1)}, f32[64,256]{1,0:T(8,128)S(1)}, u32[]{:S(2)}, u32[]{:S(2)}) %collective-permute-start.9) | collective-permute-done | bytes 65568 | tf_op jit(solution)/shard_map/ppermute | solution.py:400
  108.4 1.6 collective-permute-start.13
  110.0 1.6 collective-permute-start.14
  111.6 2.7 %collective-permute-done.11.refs_3_ = f32[64,256]{1,0:T(8,128)S(1)} collective-permute-done((f32[64,256]{1,0:T(8,128)S(1)}, f32[64,256]{1,0:T(8,128)S(1)}, u32[]{:S(2)}, u32[]{:S(2)}) %collective-permute-start.11) | collective-permute-done | bytes 65568 | tf_op jit(solution)/shard_map/ppermute | solution.py:400
  114.4 10.8 %invert_factor.1.inverse_ref = f32[256,256]{1,0:T(8,128)S(1)} custom-call(s32[1]{0:T(128)} %bitcast.1.spot_ref, f32[64,256]{1,0:T(8,128)S(1)} %reshape.36.refs_0_, f32[64,256]{1,0:T(8,128)S(1)} %collective-permute-done.9.refs_1_, f32[64,256]{1,0:T(8,128)S(1)} %collective-permute-done.10.refs_2_, f32[64,256]{1,0:T(8,128)S(1)} %collective-permute-done.11.refs_3_), custom_call_target="tpu_custom_call" | custom-call | flops 20000000000 | bytes 524288 | tf_op jit(solution)/shard_map/invert_factor/pallas_call | solution.py:88
  125.1 5.3 %collective-permute-done.12.refs_1_ = f32[32,32,128]{2,1,0:T(8,128)S(1)} collective-permute-done((f32[32,32,128]{2,1,0:T(8,128)S(1)}, f32[32,32,128]{2,1,0:T(8,128)S(1)}, u32[]{:S(2)}, u32[]{:S(2)}) %collective-permute-start.12) | collective-permute-done | bytes 524320 | tf_op jit(solution)/shard_map/ppermute | solution.py:400
  131.1 2.2 %moment_of.1.moment_ref = f32[256,256]{1,0:T(8,128)S(1)} custom-call(f32[32,32,128]{2,1,0:T(8,128)S(1)} %slice.25.refs_0_, f32[32,32,128]{2,1,0:T(8,128)S(1)} %collective-permute-done.12.refs_1_, f32[32,32,128]{2,1,0:T(8,128)S(1)} %collective-permute-done.13.refs_2_, f32[32,32,128]{2,1,0:T(8,128)S(1)} %collective-permute-done.14.refs_3_), custom_call_target="tpu_custom_call" | custom-call | flops 4000000000 | bytes 2359296 | tf_op jit(solution)/shard_map/moment_of/pallas_call | solution.py:111
  135.1 6.3 %project_half.1.basis_ref = bf16[2048,256]{1,0:T(8,128)(2,1)S(1)} custom-call(s32[1]{0:T(128)} %bitcast.1.spot_ref, f32[256,256]{1,0:T(8,128)S(1)} %invert_factor.1.inverse_ref, f32[256,256]{1,0:T(8,128)S(1)} %moment_of.1.moment_ref, f32[256,256]{1,0:T(8,128)S(1)} %collective-permute-done.15.other_ref, f32[32,32,128]{2,1,0:T(8,128)S(1)} %slice.25.refs_0_, ...), custom_call_target="tpu_custom_call" | custom-call | flops 12000000000 | bytes 4194304 | tf_op jit(solution)/shard_map/project_half/pallas_call | solution.py:151
  141.6 2.8 %copy-done.2 = bf16[768,4096]{1,0:T(8,128)(2,1)S(1)} copy-done((bf16[768,4096]{1,0:T(8,128)(2,1)S(1)}, bf16[768,4096]{1,0:T(8,128)(2,1)}, u32[]{:S(2)}) %copy-start.2) | copy-done | bytes 6291480
  148.3 2.9 %place_rows.1 = bf16[64,48,256]{2,1,0:T(8,128)(2,1)} custom-call(s32[2,768]{1,0:T(2,128)S(1)} %broadcast_select_fusion.2.target_ref, bf16[768,256]{1,0:T(8,128)(2,1)S(1)} %get-tuple-element.51.first_ref, bf16[768,256]{1,0:T(8,128)(2,1)S(1)} %get-tuple-element.50.second_ref), custom_call_target="tpu_custom_call" | custom-call | flops 1207959552 | bytes 3145728 | tf_op jit(solution)/shard_map/place_rows/pallas_call | solution.py:381
  151.3 8.3 %all-to-all-start.2 = ((bf16[128,24,256]{2,1,0:T(8,128)(2,1)}), bf16[128,24,256]{2,1,0:T(8,128)(2,1)S(1)}, u32[]{:S(2)}, u32[]{:S(2)}) async-start(bf16[128,24,256]{2,1,0:T(8,128)(2,1)} %bitcast.8), calls=%async_computation.2 | async-start | bytes 3145728 | tf_op jit(solution)/shard_map/all_to_all | solution.py:474
  160.6 40.8 %all-to-all-done.2 = bf16[128,24,256]{2,1,0:T(8,128)(2,1)S(1)} async-done(((bf16[128,24,256]{2,1,0:T(8,128)(2,1)}), bf16[128,24,256]{2,1,0:T(8,128)(2,1)S(1)}, u32[]{:S(2)}, u32[]{:S(2)}) %all-to-all-start.2) | async-done | bytes 1572896 | tf_op jit(solution)/shard_map/all_to_all | solution.py:474
  (58 shorter events, 19.7 us)
Async XLA Ops:
  1.3 3.1 %copy-start = (bf16[768,4096]{1,0:T(8,128)(2,1)S(1)}, bf16[768,4096]{1,0:T(8,128)(2,1)}, u32[]{:S(2)}) copy-start(bf16[768,4096]{1,0:T(8,128)(2,1)} %rows_ref.7) | copy-start | bytes 18874372
  1.3 1.4 copy-start.3
  9.8 5.8 %collective-permute-start.2 = (f32[256,640]{1,0:T(8,128)S(1)}, f32[256,640]{1,0:T(8,128)S(1)}, u32[]{:S(2)}, u32[]{:S(2)}) collective-permute-start(f32[256,640]{1,0:T(8,128)S(1)} %get-tuple-element.29), channel_id=1, source_target_pairs={{0,128},{128,0},{1,129},{129,1},{2,130},{130,2},{3,131},{131,3},{4... | collective-permute-start | bytes 1966088 | tf_op jit(solution)/shard_map/ppermute | solution.py:400
  10.0 2.8 %copy-start.1 = (bf16[768,4096]{1,0:T(8,128)(2,1)S(1)}, bf16[768,4096]{1,0:T(8,128)(2,1)}, u32[]{:S(2)}) copy-start(bf16[768,4096]{1,0:T(8,128)(2,1)} %rows_ref.7) | copy-start | bytes 18874372
  14.9 3.8 %collective-permute-start.5 = (f32[256,640]{1,0:T(8,128)S(1)}, f32[256,640]{1,0:T(8,128)S(1)}, u32[]{:S(2)}, u32[]{:S(2)}) collective-permute-start(f32[256,640]{1,0:T(8,128)S(1)} %get-tuple-element.31), channel_id=1, source_target_pairs={{0,128},{128,0},{1,129},{129,1},{2,130},{130,2},{3,131},{131,3},{4... | collective-permute-start | bytes 1966088 | tf_op jit(solution)/shard_map/ppermute | solution.py:400
  15.5 14.5 %collective-permute-start.1 = (f32[256,640]{1,0:T(8,128)S(1)}, f32[256,640]{1,0:T(8,128)S(1)}, u32[]{:S(2)}, u32[]{:S(2)}) collective-permute-start(f32[256,640]{1,0:T(8,128)S(1)} %get-tuple-element.27), channel_id=1, source_target_pairs={{0,128},{128,0},{1,129},{129,1},{2,130},{130,2},{3,131},{131,3},{4... | collective-permute-start | bytes 1966088 | tf_op jit(solution)/shard_map/ppermute | solution.py:400
  15.7 10.4 %collective-permute-start.6 = (f32[128,640]{1,0:T(8,128)S(1)}, f32[128,640]{1,0:T(8,128)S(1)}, u32[]{:S(2)}, u32[]{:S(2)}) collective-permute-start(f32[128,640]{1,0:T(8,128)S(1)} %get-tuple-element.54), channel_id=1, source_target_pairs={{0,3},{1,0},{2,1},{3,2},{4,7},{5,4},{6,5},{7,6},{8,11},{9,8},{10,9... | collective-permute-start | bytes 983048 | tf_op jit(solution)/shard_map/ppermute | solution.py:400
  18.5 11.4 %collective-permute-start.3 = (f32[128,640]{1,0:T(8,128)S(1)}, f32[128,640]{1,0:T(8,128)S(1)}, u32[]{:S(2)}, u32[]{:S(2)}) collective-permute-start(f32[128,640]{1,0:T(8,128)S(1)} %get-tuple-element.55), channel_id=1, source_target_pairs={{0,1},{1,2},{2,3},{3,0},{4,5},{5,6},{6,7},{7,4},{8,9},{9,10},{10,1... | collective-permute-start | bytes 983048 | tf_op jit(solution)/shard_map/ppermute | solution.py:400
  18.6 11.6 %collective-permute-start = (f32[256,640]{1,0:T(8,128)S(1)}, f32[256,640]{1,0:T(8,128)S(1)}, u32[]{:S(2)}, u32[]{:S(2)}) collective-permute-start(f32[256,640]{1,0:T(8,128)S(1)} %get-tuple-element.25), channel_id=1, source_target_pairs={{0,128},{128,0},{1,129},{129,1},{2,130},{130,2},{3,131},{131,3},{4... | collective-permute-start | bytes 1966088 | tf_op jit(solution)/shard_map/ppermute | solution.py:400
  26.2 17.6 %collective-permute-start.7 = (f32[256,640]{1,0:T(8,128)S(1)}, f32[256,640]{1,0:T(8,128)S(1)}, u32[]{:S(2)}, u32[]{:S(2)}) collective-permute-start(f32[256,640]{1,0:T(8,128)S(1)} %join_chunk.3), channel_id=1, source_target_pairs={{0,3},{1,0},{2,1},{3,2},{4,7},{5,4},{6,5},{7,6},{8,11},{9,8},{10,9... | collective-permute-start | bytes 1966088 | tf_op jit(solution)/shard_map/ppermute | solution.py:400
  30.1 17.3 %collective-permute-start.4 = (f32[256,640]{1,0:T(8,128)S(1)}, f32[256,640]{1,0:T(8,128)S(1)}, u32[]{:S(2)}, u32[]{:S(2)}) collective-permute-start(f32[256,640]{1,0:T(8,128)S(1)} %join_chunk.2), channel_id=1, source_target_pairs={{0,1},{1,2},{2,3},{3,0},{4,5},{5,6},{6,7},{7,4},{8,9},{9,10},{10,1... | collective-permute-start | bytes 1966088 | tf_op jit(solution)/shard_map/ppermute | solution.py:400
  48.5 30.5 %all-to-all-start = ((f32[32,40,128]{2,1,0:T(8,128)}), f32[32,40,128]{2,1,0:T(8,128)S(1)}, u32[]{:S(2)}, u32[]{:S(2)}) async-start(f32[32,40,128]{2,1,0:T(8,128)} %line_total.1), calls=%async_computation | async-start | bytes 1310720 | tf_op jit(solution)/shard_map/all_to_all | solution.py:444
  59.8 1.4 collective-permute-start.8
  101.8 6.5 %collective-permute-start.9 = (f32[64,256]{1,0:T(8,128)S(1)}, f32[64,256]{1,0:T(8,128)S(1)}, u32[]{:S(2)}, u32[]{:S(2)}) collective-permute-start(f32[64,256]{1,0:T(8,128)S(1)} %reshape.36.refs_0_), channel_id=1, source_target_pairs={{0,1},{1,2},{2,3},{3,0},{4,5},{5,6},{6,7},{7,4},{8,9},{9,10},{10,1... | collective-permute-start | bytes 196616 | tf_op jit(solution)/shard_map/ppermute | solution.py:400
  102.4 9.2 %collective-permute-start.10 = (f32[64,256]{1,0:T(8,128)S(1)}, f32[64,256]{1,0:T(8,128)S(1)}, u32[]{:S(2)}, u32[]{:S(2)}) collective-permute-start(f32[64,256]{1,0:T(8,128)S(1)} %reshape.36.refs_0_), channel_id=1, source_target_pairs={{0,2},{1,3},{2,0},{3,1},{4,6},{5,7},{6,4},{7,5},{8,10},{9,11},{10,... | collective-permute-start | bytes 196616 | tf_op jit(solution)/shard_map/ppermute | solution.py:400
  104.9 9.4 %collective-permute-start.11 = (f32[64,256]{1,0:T(8,128)S(1)}, f32[64,256]{1,0:T(8,128)S(1)}, u32[]{:S(2)}, u32[]{:S(2)}) collective-permute-start(f32[64,256]{1,0:T(8,128)S(1)} %reshape.36.refs_0_), channel_id=1, source_target_pairs={{0,3},{1,0},{2,1},{3,2},{4,7},{5,4},{6,5},{7,6},{8,11},{9,8},{10,9... | collective-permute-start | bytes 196616 | tf_op jit(solution)/shard_map/ppermute | solution.py:400
  108.3 22.1 %collective-permute-start.12 = (f32[32,32,128]{2,1,0:T(8,128)S(1)}, f32[32,32,128]{2,1,0:T(8,128)S(1)}, u32[]{:S(2)}, u32[]{:S(2)}) collective-permute-start(f32[32,32,128]{2,1,0:T(8,128)S(1)} %slice.25.refs_0_), channel_id=1, source_target_pairs={{0,1},{1,2},{2,3},{3,0},{4,5},{5,6},{6,7},{7,4},{8,9},{9,10},{10,1... | collective-permute-start | bytes 1572872 | tf_op jit(solution)/shard_map/ppermute | solution.py:400
  108.4 22.1 %collective-permute-start.13 = (f32[32,32,128]{2,1,0:T(8,128)S(1)}, f32[32,32,128]{2,1,0:T(8,128)S(1)}, u32[]{:S(2)}, u32[]{:S(2)}) collective-permute-start(f32[32,32,128]{2,1,0:T(8,128)S(1)} %slice.25.refs_0_), channel_id=1, source_target_pairs={{0,2},{1,3},{2,0},{3,1},{4,6},{5,7},{6,4},{7,5},{8,10},{9,11},{10,... | collective-permute-start | bytes 1572872 | tf_op jit(solution)/shard_map/ppermute | solution.py:400
  110.0 21.1 %collective-permute-start.14 = (f32[32,32,128]{2,1,0:T(8,128)S(1)}, f32[32,32,128]{2,1,0:T(8,128)S(1)}, u32[]{:S(2)}, u32[]{:S(2)}) collective-permute-start(f32[32,32,128]{2,1,0:T(8,128)S(1)} %slice.25.refs_0_), channel_id=1, source_target_pairs={{0,3},{1,0},{2,1},{3,2},{4,7},{5,4},{6,5},{7,6},{8,11},{9,8},{10,9... | collective-permute-start | bytes 1572872 | tf_op jit(solution)/shard_map/ppermute | solution.py:400
  133.3 1.8 collective-permute-start.15
  141.4 4.0 %collective-permute-start.16 = (bf16[2048,256]{1,0:T(8,128)(2,1)S(1)}, bf16[2048,256]{1,0:T(8,128)(2,1)S(1)}, u32[]{:S(2)}, u32[]{:S(2)}) collective-permute-start(bf16[2048,256]{1,0:T(8,128)(2,1)S(1)} %project_half.1.basis_ref), channel_id=1, source_target_pairs={{0,128},{128,0},{1,129},{129,1},{2,130},{130,2},{3,131},{131,3},{4... | collective-permute-start | bytes 3145736 | tf_op jit(solution)/shard_map/ppermute | solution.py:400
  141.6 2.8 %copy-start.2 = (bf16[768,4096]{1,0:T(8,128)(2,1)S(1)}, bf16[768,4096]{1,0:T(8,128)(2,1)}, u32[]{:S(2)}) copy-start(bf16[768,4096]{1,0:T(8,128)(2,1)} %rows_ref.7) | copy-start | bytes 18874372
  146.4 1.8 collective-permute-start.17
  151.3 50.1 %all-to-all-start.2 = ((bf16[128,24,256]{2,1,0:T(8,128)(2,1)}), bf16[128,24,256]{2,1,0:T(8,128)(2,1)S(1)}, u32[]{:S(2)}, u32[]{:S(2)}) async-start(bf16[128,24,256]{2,1,0:T(8,128)(2,1)} %bitcast.8), calls=%async_computation.2 | async-start | bytes 3145728 | tf_op jit(solution)/shard_map/all_to_all | solution.py:474

commit v5 on v4

--- a/solution.py
+++ b/solution.py
@@ -159,7 +159,7 @@
     )(spot, inverse, moment, other, *parts)
 
 
-def chunk_kernel(spot_ref, rows_ref, sketch_ref, label_ref, *out_refs):
+def chunk_kernel(steps, spot_ref, rows_ref, sketch_ref, label_ref, *out_refs):
     core, here, line = (spot_ref[i] for i in range(3))
     rank = sketch_ref.shape[1]
     width = out_refs[0].shape[1] - 128
@@ -171,11 +171,11 @@
     gram_whole = mul(sketch, sketch)
     lane = lax.broadcasted_iota(jnp.int32, (rank, 128), 1)
     mine = pl.ds(pl.multiple_of((core * line + here) * SLOTS, SLOTS), SLOTS)
-    for step in range(len(out_refs) // 2):
-        chunk = spot_ref[3 + step]
+    for index, step in enumerate(steps):
+        chunk = lax.rem(here + step, line)
         gram = pltpu.roll(gram_whole, rank - chunk * (rank * width // half), 1)[:, :128]
         gram = jnp.where(lane < rank * width // half, gram, 0.0)
-        for out_ref, place in zip(out_refs[2 * step :], (1 - core, core)):
+        for out_ref, place in zip(out_refs[2 * index :], (1 - core, core)):
             columns = pl.ds(pl.multiple_of(place * half + chunk * width, width), width)
             out_ref[:, :width] = mul(sketch, rows_ref[:, columns])
             out_ref[:, width:] = gram
@@ -183,13 +183,14 @@
             out_ref[mine, width:] += label_ref[theirs, :]
 
 
-def cross_chunks(spot, embeddings, sketch, labels, chunks, count):
+def cross_chunks(spot, embeddings, sketch, labels, chunks, steps):
+    count = len(steps)
     depth, dim = embeddings.shape
     rank = sketch.shape[1]
     width = dim // 2 // chunks
     shape = jax.ShapeDtypeStruct((rank, width + 128), jnp.float32)
     return pl.pallas_call(
-        chunk_kernel,
+        functools.partial(chunk_kernel, steps),
         in_specs=[pl.BlockSpec(memory_space=pltpu.SMEM)]
         + [pl.BlockSpec(memory_space=pltpu.VMEM)] * 3,
         out_shape=[shape] * (2 * count),
@@ -274,6 +275,22 @@
     return jnp.concatenate([t.reshape(plane * pair // 2, lanes) for t in sides], axis=1)
 
 
+def gram_kernel(piece, gram_piece, parts_ref, out_ref):
+    start = 2 * piece
+    out_ref[...] = whole_rows(parts_ref[:, start : start + 2 * gram_piece, :])
+
+
+def gram_rows(parts, piece, gram_piece):
+    plane, _, lanes = parts.shape
+    return pl.pallas_call(
+        functools.partial(gram_kernel, piece, gram_piece),
+        out_shape=jax.ShapeDtypeStruct((plane * gram_piece, 2 * lanes), jnp.float32),
+        compiler_params=GRANT,
+        cost_estimate=pl.CostEstimate(flops=10000, bytes_accessed=200000, transcendentals=0),
+        name="gram_rows",
+    )(parts)
+
+
 def product_kernel(core_ref, rows_ref, basis_ref, *refs):
     half, width = basis_ref.shape[0], 512
     total = None if len(refs) == 1 else refs[0][...]
@@ -303,7 +320,7 @@
 
 
 def route_kernel(capacity, line, plane, ids_ref, map_ref, dest_ref, label_ref):
-    ids = ids_ref[...]
+    ids = jnp.concatenate([ids_ref[k : k + 1, :] for k in range(ids_ref.shape[0])], axis=1)
     count, (high, low) = ids.shape[1], map_ref.shape
     owner_count = 2 * plane * line
     bf16 = jnp.bfloat16
@@ -355,18 +372,18 @@
             flops=2_000_000_000, bytes_accessed=1048576, transcendentals=0
         ),
         name="route_rows",
-    )(list_ids.reshape(1, count), owner_map.reshape(-1, 128))
-
-
-def place_kernel(capacity, target_ref, first_ref, second_ref, out_ref):
+    )(list_ids.reshape(-1, 128), owner_map.reshape(-1, 128))
+
+
+def place_kernel(capacity, first_target, second_target, first_ref, second_ref, out_ref):
     pairs, _, width = out_ref.shape
     count = pairs * 2 * capacity
     slots = pl.program_id(0) * count + lax.broadcasted_iota(
         jnp.int32, (count, first_ref.shape[0]), 0
     )
     found = []
-    for part, rows_ref in enumerate((first_ref, second_ref)):
-        onehot = (slots == target_ref[part : part + 1, :]).astype(jnp.bfloat16)
+    for target_ref, rows_ref in ((first_target, first_ref), (second_target, second_ref)):
+        onehot = (slots == target_ref[...]).astype(jnp.bfloat16)
         term = jnp.dot(onehot, rows_ref[...], preferred_element_type=jnp.float32)
         found.append(term.reshape(pairs, 2 * capacity, width))
     a, b = found
@@ -375,13 +392,13 @@
     ).astype(jnp.bfloat16)
 
 
-def place_rows(target, first, second, chips, capacity):
+def place_rows(targets, first, second, chips, capacity):
     pairs = 16
     depth, width = first.shape
     return pl.pallas_call(
         functools.partial(place_kernel, capacity),
         grid=(chips // 2 // pairs,),
-        in_specs=[pl.BlockSpec((2, depth), lambda i: (0, 0))]
+        in_specs=[pl.BlockSpec((1, depth), lambda i: (0, 0))] * 2
         + [pl.BlockSpec((depth, width), lambda i: (0, 0))] * 2,
         out_specs=pl.BlockSpec((pairs, 4 * capacity, width), lambda i: (i, 0, 0)),
         out_shape=jax.ShapeDtypeStruct((chips // 2, 4 * capacity, width), jnp.bfloat16),
@@ -392,7 +409,7 @@
             transcendentals=0,
         ),
         name="place_rows",
-    )(target, first, second)
+    )(*targets, first, second)
 
 
 def shift(value, axis, step):
@@ -420,10 +437,10 @@
     here = lax.axis_index("x")
     dest_index, labels = route_rows(list_ids, owner_map, capacity, line, plane)
 
+    spots = jnp.stack([core, here, jnp.int32(line)])
+
     def chunks_at(*steps):
-        places = [(here + step) % line for step in steps]
-        spot = jnp.stack([core, here, jnp.int32(line)] + places)
-        pairs = cross_chunks(spot, embeddings, sketch, labels, line, len(steps))
+        pairs = cross_chunks(spots, embeddings, sketch, labels, line, steps)
         return [(pairs[2 * i + 1], shift(pairs[2 * i], "narrow", 1)) for i in range(len(steps))]
 
     (far,) = chunks_at(2)
@@ -434,20 +451,21 @@
     from_below = shift(join_chunk(*up, from_below, 0), "x", 1)
     from_above = shift(join_chunk(*down, from_above, 1), "x", line - 1)
 
-    both_dest = jnp.concatenate([dest_index, shift(dest_index, "narrow", 1)])
-    both_owner = both_dest // capacity
-    target = (both_owner % chips) * capacity + both_dest % capacity
-    target = jnp.where(both_owner // chips == core, target, -1)
-    target = jnp.where(core == 0, target, target[::-1])
+    def target_of(dest):
+        owner = dest // capacity
+        return jnp.where(owner // chips == core, (owner % chips) * capacity + dest % capacity, -1)
+
+    def by_core(own, other):
+        return jnp.where(core == 0, own, other), jnp.where(core == 0, other, own)
+
+    targets = by_core(target_of(dest_index), target_of(shift(dest_index, "narrow", 1)))
 
     packed = line_total([*near, from_below, from_above], plane, gram_piece)
+    packed, targets = lax.optimization_barrier((packed, targets))
     packed = lax.all_to_all(packed, PLANE, 0, 0, tiled=True)
-    packed, target = lax.optimization_barrier((packed, target))
     packed, arrived_labels = plane_total(packed, 2 * (piece + gram_piece))
     packed = lax.all_to_all(packed, PLANE, 0, 0, tiled=True)
-    gram_line = packed[:, 2 * piece : 2 * (piece + gram_piece)]
-    gram_line = jnp.concatenate([gram_line[:, :gram_piece], gram_line[:, gram_piece:]], axis=2)
-    gram_line = gram_line.reshape(-1, rank)
+    gram_line = gram_rows(packed, piece, gram_piece)
     gram_parts = [gram_line] + [shift(gram_line, "x", step) for step in range(1, line)]
     packed, gram_parts[1] = lax.optimization_barrier((packed, gram_parts[1]))
     cross_line = packed[:, : 2 * piece]
@@ -462,14 +480,8 @@
     other_basis = shift(basis, "narrow", 1)
     begun = product_of_half(own_half, embeddings, basis, None, jnp.float32)
     reduced = product_of_half(other_half, embeddings, other_basis, begun, jnp.bfloat16)
-    other = shift(reduced, "narrow", 1)
-    send_rows = place_rows(
-        target,
-        jnp.where(core == 0, reduced, other),
-        jnp.where(core == 0, other, reduced),
-        chips,
-        capacity,
-    )
+    rows = by_core(reduced, shift(reduced, "narrow", 1))
+    send_rows = place_rows(targets, *rows, chips, capacity)
     send_rows = send_rows.reshape(chips, cores * capacity, rank)
     arrived = lax.all_to_all(send_rows, ("y", "z", "x"), 0, 0, tiled=True)
     arrived = arrived.reshape(chips, cores, capacity, rank).transpose(1, 0, 2, 3)

time: 203 us -> 201 us (level)
  blocking collectives: 22.7 us -> 53.3 us
  waiting for transfers between devices: 98.5 us -> 80.3 us
  starting transfers between devices: 35.3 us -> 23.4 us
  local copies, waits for them, and re-layouts: 10.8 us -> 7.71 us
    all_to_all x1 -> x2, blocking collectives: 22.7 us -> 53.3 us  [local(): packed = lax.all_to_all(packed, PLANE, 0, 0, tiled=True)]
    all_to_all x1 -> x0, waiting for transfers between devices: 17.3 us -> none  [local(): packed = lax.all_to_all(packed, PLANE, 0, 0, tiled=True)]
    all_to_all x1 -> x0, starting transfers between devices: 11.4 us -> none  [local(): packed = lax.all_to_all(packed, PLANE, 0, 0, tiled=True)]
    unnamed x9, local copies, waits for them, and re-layouts: 7.82 us -> 5.77 us
  transfers between devices with their start and end apart: 20 -> 19, of which waited for: 12 -> 11; matrix products, arithmetic and copies ran while one was open for 1% -> 1% of each run, Pallas kernels for 7% -> 8%
where the time goes in v5:
time: 201 us
  waiting for transfers between devices  80.3 us (40%)
  blocking collectives  53.3 us (27%)
  Pallas kernels  31.1 us (15%)
  starting transfers between devices  23.4 us (12%)
  local copies, waits for them, and re-layouts  7.71 us (4%)
  matrix products  4.03 us (2%)
    all_to_all x2, blocking collectives, local(): packed = lax.all_to_all(packed, PLANE, 0, 0, tiled=True)  53.3 us
    all_to_all x1, waiting for transfers between devices, local(): arrived = lax.all_to_all(send_rows, ('y', 'z', 'x'), 0, 0, tiled=True)  40.8 us
    ppermute x18, waiting for transfers between devices, shift(): lax.ppermute(value, axis, [(i, (i + step) % size) for i in range(size)])  39.4 us
    ppermute x18, starting transfers between devices, shift(): lax.ppermute(value, axis, [(i, (i + step) % size) for i in range(size)])  15.1 us
    pallas_call x1, Pallas kernels, invert_factor(): pl.pallas_call(invert_kernel, in_specs=[pl.BlockSpec(memory_space=pltpu.S...  10.8 us
    all_to_all x1, starting transfers between devices, local(): arrived = lax.all_to_all(send_rows, ('y', 'z', 'x'), 0, 0, tiled=True)  8.37 us
    pallas_call x1, Pallas kernels, project_half(): pl.pallas_call(whiten_kernel, in_specs=[pl.BlockSpec(memory_space=pltpu.S...  6.32 us
    unnamed x9, local copies, waits for them, and re-layouts  5.77 us
  transfers between devices with their start and end apart: 19, of which 11 were waited for; matrix products, arithmetic and copies ran while one was open for 1% of the time, Pallas kernels for 8%

profile of v5, /device:TPU:32, one launch (start us, length us, event | category | flops | bytes accessed | tf_op | source)
XLA Modules:
  0.0 201.0 jit_solution(13634487109062835050)
XLA Ops:
  0.7 1.4 copy-done.2
  3.0 1.6 route_rows.1
  4.5 4.0 %fusion.2.sketch_ref = bf16[768,256]{1,0:T(8,128)(2,1)S(1)} fusion(bf16[768,4096]{1,0:T(8,128)(2,1)S(1)} %copy-done, s32[4096,256]{1,0:T(8,128)} %param.5), kind=kOutput, calls=%fused_computation.2 | convolution fusion | flops 1611857920 | bytes 10878976 | tf_op jit(solution)/shard_map/dot_general | solution.py:432
  10.0 2.7 %cross_chunks.2 = (f32[256,640]{1,0:T(8,128)S(1)}, f32[256,640]{1,0:T(8,128)S(1)}, f32[256,640]{1,0:T(8,128)S(1)}, f32[256,640]{1,0:T(8,128)S(1)}, f32[256,640]{1,0:T(8,128)}, /*index=5*/f32[256,640]{1,0:T(8,128)S(1)}) custom-call(s32[3]{0:T(128)S(1)} %pad_add_fusion.spot_ref, bf16[768,4096]{1,0:T(8,128)(2,1)S(1)} %copy-done, ...), custom_call_target="tpu_custom_call" | custom-call | flops 1207959552 | bytes 3000000 | tf_op jit(solution)/shard_map/cross_chunks/pallas_call | solution.py:192
  13.4 2.8 %collective-permute-start.6 = (f32[128,640]{1,0:T(8,128)S(1)}, f32[128,640]{1,0:T(8,128)S(1)}, u32[]{:S(2)}, u32[]{:S(2)}) collective-permute-start(f32[128,640]{1,0:T(8,128)S(1)} %get-tuple-element.57), channel_id=1, source_target_pairs={{0,3},{1,0},{2,1},{3,2},{4,7},{5,4},{6,5},{7,6},{8,11},{9,8},{10,9... | collective-permute-start | bytes 983048 | tf_op jit(solution)/shard_map/ppermute | solution.py:417
  16.5 7.4 %collective-permute-done.6.extra_ref = f32[128,640]{1,0:T(8,128)S(1)} collective-permute-done((f32[128,640]{1,0:T(8,128)S(1)}, f32[128,640]{1,0:T(8,128)S(1)}, u32[]{:S(2)}, u32[]{:S(2)}) %collective-permute-start.6) | collective-permute-done | bytes 327712 | tf_op jit(solution)/shard_map/ppermute | solution.py:417
  24.0 3.8 %collective-permute-start.7 = (f32[256,640]{1,0:T(8,128)S(1)}, f32[256,640]{1,0:T(8,128)S(1)}, u32[]{:S(2)}, u32[]{:S(2)}) collective-permute-start(f32[256,640]{1,0:T(8,128)S(1)} %join_chunk.3), channel_id=1, source_target_pairs={{0,3},{1,0},{2,1},{3,2},{4,7},{5,4},{6,5},{7,6},{8,11},{9,8},{10,9... | collective-permute-start | bytes 1966088 | tf_op jit(solution)/shard_map/ppermute | solution.py:417
  30.0 11.6 %collective-permute-done.7.refs_3_ = f32[256,640]{1,0:T(8,128)S(1)} collective-permute-done((f32[256,640]{1,0:T(8,128)S(1)}, f32[256,640]{1,0:T(8,128)S(1)}, u32[]{:S(2)}, u32[]{:S(2)}) %collective-permute-start.7) | collective-permute-done | bytes 655392 | tf_op jit(solution)/shard_map/ppermute | solution.py:417
  41.6 4.6 %collective-permute-done.4.refs_2_ = f32[256,640]{1,0:T(8,128)S(1)} collective-permute-done((f32[256,640]{1,0:T(8,128)}, f32[256,640]{1,0:T(8,128)S(1)}, u32[]{:S(2)}, u32[]{:S(2)}) %collective-permute-start.4) | collective-permute-done | bytes 655392 | tf_op jit(solution)/shard_map/ppermute | solution.py:417
  46.4 30.3 %all_to_all.15.parts_ref = f32[32,40,128]{2,1,0:T(8,128)S(1)} all-to-all(f32[32,40,128]{2,1,0:T(8,128)S(1)} %line_total.1), channel_id=1, replica_groups=mesh['narrow'=2,'y'=4,'z'=8,'x'=4] {'y','z'}, dimensions={0} | all-to-all | bytes 1310720 | tf_op jit(solution)/shard_map/all_to_all | solution.py:465
  76.8 23.0 %all_to_all.16.parts_ref = f32[32,40,128]{2,1,0:T(8,128)S(1)} all-to-all(f32[32,40,128]{2,1,0:T(8,128)S(1)} %get-tuple-element.37), channel_id=1, replica_groups=mesh['narrow'=2,'y'=4,'z'=8,'x'=4] {'y','z'}, dimensions={0} | all-to-all | bytes 1310720 | tf_op jit(solution)/shard_map/all_to_all | solution.py:467
  101.0 2.1 %collective-permute-start.11 = (f32[64,256]{1,0:T(8,128)S(1)}, f32[64,256]{1,0:T(8,128)S(1)}, u32[]{:S(2)}, u32[]{:S(2)}) collective-permute-start(f32[64,256]{1,0:T(8,128)S(1)} %gram_rows.1.refs_0_), channel_id=1, source_target_pairs={{0,3},{1,0},{2,1},{3,2},{4,7},{5,4},{6,5},{7,6},{8,11},{9,8},{10,9... | collective-permute-start | bytes 196616 | tf_op jit(solution)/shard_map/ppermute | solution.py:417
  103.1 3.6 %collective-permute-done.9.refs_1_ = f32[64,256]{1,0:T(8,128)S(1)} collective-permute-done((f32[64,256]{1,0:T(8,128)S(1)}, f32[64,256]{1,0:T(8,128)S(1)}, u32[]{:S(2)}, u32[]{:S(2)}) %collective-permute-start.9) | collective-permute-done | bytes 65568 | tf_op jit(solution)/shard_map/ppermute | solution.py:417
  107.4 2.7 %collective-permute-start.14 = (f32[32,32,128]{2,1,0:T(8,128)S(1)}, f32[32,32,128]{2,1,0:T(8,128)S(1)}, u32[]{:S(2)}, u32[]{:S(2)}) collective-permute-start(f32[32,32,128]{2,1,0:T(8,128)S(1)} %slice.14.refs_0_), channel_id=1, source_target_pairs={{0,3},{1,0},{2,1},{3,2},{4,7},{5,4},{6,5},{7,6},{8,11},{9,8},{10,9... | collective-permute-start | bytes 1572872 | tf_op jit(solution)/shard_map/ppermute | solution.py:417
  110.1 1.6 collective-permute-done.11.refs_3_
  111.8 10.8 %invert_factor.1.inverse_ref = f32[256,256]{1,0:T(8,128)S(1)} custom-call(s32[1]{0:T(128)} %bitcast.1.spot_ref, f32[64,256]{1,0:T(8,128)S(1)} %gram_rows.1.refs_0_, f32[64,256]{1,0:T(8,128)S(1)} %collective-permute-done.9.refs_1_, f32[64,256]{1,0:T(8,128)S(1)} %collective-permute-done.10.refs_2_, f32[64,256]{1,0:T(8,128)S(1)} %collective-permute-done.11.refs_3_), custom_call_target="tpu_custom_call" | custom-call | flops 20000000000 | bytes 524288 | tf_op jit(solution)/shard_map/invert_factor/pallas_call | solution.py:88
  122.5 5.9 %collective-permute-done.12.refs_1_ = f32[32,32,128]{2,1,0:T(8,128)S(1)} collective-permute-done((f32[32,32,128]{2,1,0:T(8,128)S(1)}, f32[32,32,128]{2,1,0:T(8,128)S(1)}, u32[]{:S(2)}, u32[]{:S(2)}) %collective-permute-start.12) | collective-permute-done | bytes 524320 | tf_op jit(solution)/shard_map/ppermute | solution.py:417
  129.1 2.1 %moment_of.1.moment_ref = f32[256,256]{1,0:T(8,128)S(1)} custom-call(f32[32,32,128]{2,1,0:T(8,128)S(1)} %slice.14.refs_0_, f32[32,32,128]{2,1,0:T(8,128)S(1)} %collective-permute-done.12.refs_1_, f32[32,32,128]{2,1,0:T(8,128)S(1)} %collective-permute-done.13.refs_2_, f32[32,32,128]{2,1,0:T(8,128)S(1)} %collective-permute-done.14.refs_3_), custom_call_target="tpu_custom_call" | custom-call | flops 4000000000 | bytes 2359296 | tf_op jit(solution)/shard_map/moment_of/pallas_call | solution.py:111
  131.5 1.5 collective-permute-done.15.other_ref
  133.0 6.3 %project_half.1.basis_ref = bf16[2048,256]{1,0:T(8,128)(2,1)S(1)} custom-call(s32[1]{0:T(128)} %bitcast.1.spot_ref, f32[256,256]{1,0:T(8,128)S(1)} %invert_factor.1.inverse_ref, f32[256,256]{1,0:T(8,128)S(1)} %moment_of.1.moment_ref, f32[256,256]{1,0:T(8,128)S(1)} %collective-permute-done.15.other_ref, f32[32,32,128]{2,1,0:T(8,128)S(1)} %slice.14.refs_0_, ...), custom_call_target="tpu_custom_call" | custom-call | flops 12000000000 | bytes 4194304 | tf_op jit(solution)/shard_map/project_half/pallas_call | solution.py:151
  139.6 2.8 %copy-done.1 = bf16[768,4096]{1,0:T(8,128)(2,1)S(1)} copy-done((bf16[768,4096]{1,0:T(8,128)(2,1)S(1)}, bf16[768,4096]{1,0:T(8,128)(2,1)}, u32[]{:S(2)}) %copy-start.1) | copy-done | bytes 6291480
  146.3 2.9 %place_rows.1 = bf16[64,48,256]{2,1,0:T(8,128)(2,1)} custom-call(s32[1,768]{1,0:T(1,128)S(1)} %broadcast_select_fusion.3.first_target, s32[1,768]{1,0:T(1,128)S(1)} %get-tuple-element.35.second_target, bf16[768,256]{1,0:T(8,128)(2,1)S(1)} %get-tuple-element.56.first_ref, bf16[768,256]{1,0:T(8,128)(2,1)S(1)} %get-tuple-element.55.second_ref), custom_call_target="tpu_custom_call" | custom-call | flops 1207959552 | bytes 3145728 | tf_op jit(solution)/shard_map/place_rows/pallas_call | solution.py:398
  149.2 8.4 %all-to-all-start.2 = ((bf16[128,24,256]{2,1,0:T(8,128)(2,1)}), bf16[128,24,256]{2,1,0:T(8,128)(2,1)S(1)}, u32[]{:S(2)}, u32[]{:S(2)}) async-start(bf16[128,24,256]{2,1,0:T(8,128)(2,1)} %bitcast.5), calls=%async_computation.2 | async-start | bytes 3145728 | tf_op jit(solution)/shard_map/all_to_all | solution.py:486
  158.5 40.8 %all-to-all-done.2 = bf16[128,24,256]{2,1,0:T(8,128)(2,1)S(1)} async-done(((bf16[128,24,256]{2,1,0:T(8,128)(2,1)}), bf16[128,24,256]{2,1,0:T(8,128)(2,1)S(1)}, u32[]{:S(2)}, u32[]{:S(2)}) %all-to-all-start.2) | async-done | bytes 1572896 | tf_op jit(solution)/shard_map/all_to_all | solution.py:486
  (52 shorter events, 15.3 us)
Async XLA Ops:
  0.6 3.9 %copy-start = (bf16[768,4096]{1,0:T(8,128)(2,1)S(1)}, bf16[768,4096]{1,0:T(8,128)(2,1)}, u32[]{:S(2)}) copy-start(bf16[768,4096]{1,0:T(8,128)(2,1)} %rows_ref.7) | copy-start | bytes 18874372
  0.6 1.4 copy-start.2
  2.0 0.9 copy-start.3
  9.9 3.3 %collective-permute-start.2 = (f32[256,640]{1,0:T(8,128)S(1)}, f32[256,640]{1,0:T(8,128)S(1)}, u32[]{:S(2)}, u32[]{:S(2)}) collective-permute-start(f32[256,640]{1,0:T(8,128)S(1)} %get-tuple-element.30), channel_id=1, source_target_pairs={{0,128},{128,0},{1,129},{129,1},{2,130},{130,2},{3,131},{131,3},{4... | collective-permute-start | bytes 1966088 | tf_op jit(solution)/shard_map/ppermute | solution.py:417
  12.8 3.7 %collective-permute-start.5 = (f32[256,640]{1,0:T(8,128)S(1)}, f32[256,640]{1,0:T(8,128)S(1)}, u32[]{:S(2)}, u32[]{:S(2)}) collective-permute-start(f32[256,640]{1,0:T(8,128)S(1)} %get-tuple-element.32), channel_id=1, source_target_pairs={{0,128},{128,0},{1,129},{129,1},{2,130},{130,2},{3,131},{131,3},{4... | collective-permute-start | bytes 1966088 | tf_op jit(solution)/shard_map/ppermute | solution.py:417
  13.3 14.5 %collective-permute-start.1 = (f32[256,640]{1,0:T(8,128)S(1)}, f32[256,640]{1,0:T(8,128)S(1)}, u32[]{:S(2)}, u32[]{:S(2)}) collective-permute-start(f32[256,640]{1,0:T(8,128)S(1)} %get-tuple-element.28), channel_id=1, source_target_pairs={{0,128},{128,0},{1,129},{129,1},{2,130},{130,2},{3,131},{131,3},{4... | collective-permute-start | bytes 1966088 | tf_op jit(solution)/shard_map/ppermute | solution.py:417
  13.4 10.5 %collective-permute-start.6 = (f32[128,640]{1,0:T(8,128)S(1)}, f32[128,640]{1,0:T(8,128)S(1)}, u32[]{:S(2)}, u32[]{:S(2)}) collective-permute-start(f32[128,640]{1,0:T(8,128)S(1)} %get-tuple-element.57), channel_id=1, source_target_pairs={{0,3},{1,0},{2,1},{3,2},{4,7},{5,4},{6,5},{7,6},{8,11},{9,8},{10,9... | collective-permute-start | bytes 983048 | tf_op jit(solution)/shard_map/ppermute | solution.py:417
  16.2 11.5 %collective-permute-start.3 = (f32[128,640]{1,0:T(8,128)S(1)}, f32[128,640]{1,0:T(8,128)S(1)}, u32[]{:S(2)}, u32[]{:S(2)}) collective-permute-start(f32[128,640]{1,0:T(8,128)S(1)} %get-tuple-element.58), channel_id=1, source_target_pairs={{0,1},{1,2},{2,3},{3,0},{4,5},{5,6},{6,7},{7,4},{8,9},{9,10},{10,1... | collective-permute-start | bytes 983048 | tf_op jit(solution)/shard_map/ppermute | solution.py:417
  16.2 13.7 %collective-permute-start = (f32[256,640]{1,0:T(8,128)}, f32[256,640]{1,0:T(8,128)S(1)}, u32[]{:S(2)}, u32[]{:S(2)}) collective-permute-start(f32[256,640]{1,0:T(8,128)} %get-tuple-element.26), channel_id=1, source_target_pairs={{0,128},{128,0},{1,129},{129,1},{2,130},{130,2},{3,131},{131,3},{4... | collective-permute-start | bytes 1966088 | tf_op jit(solution)/shard_map/ppermute | solution.py:417
  24.0 17.6 %collective-permute-start.7 = (f32[256,640]{1,0:T(8,128)S(1)}, f32[256,640]{1,0:T(8,128)S(1)}, u32[]{:S(2)}, u32[]{:S(2)}) collective-permute-start(f32[256,640]{1,0:T(8,128)S(1)} %join_chunk.3), channel_id=1, source_target_pairs={{0,3},{1,0},{2,1},{3,2},{4,7},{5,4},{6,5},{7,6},{8,11},{9,8},{10,9... | collective-permute-start | bytes 1966088 | tf_op jit(solution)/shard_map/ppermute | solution.py:417
  28.7 17.5 %collective-permute-start.4 = (f32[256,640]{1,0:T(8,128)}, f32[256,640]{1,0:T(8,128)S(1)}, u32[]{:S(2)}, u32[]{:S(2)}) collective-permute-start(f32[256,640]{1,0:T(8,128)} %join_chunk.2), channel_id=1, source_target_pairs={{0,1},{1,2},{2,3},{3,0},{4,5},{5,6},{6,7},{7,4},{8,9},{9,10},{10,1... | collective-permute-start | bytes 1966088 | tf_op jit(solution)/shard_map/ppermute | solution.py:417
  28.7 1.2 collective-permute-start.8
  99.8 7.0 %collective-permute-start.9 = (f32[64,256]{1,0:T(8,128)S(1)}, f32[64,256]{1,0:T(8,128)S(1)}, u32[]{:S(2)}, u32[]{:S(2)}) collective-permute-start(f32[64,256]{1,0:T(8,128)S(1)} %gram_rows.1.refs_0_), channel_id=1, source_target_pairs={{0,1},{1,2},{2,3},{3,0},{4,5},{5,6},{6,7},{7,4},{8,9},{9,10},{10,1... | collective-permute-start | bytes 196616 | tf_op jit(solution)/shard_map/ppermute | solution.py:417
  100.2 9.9 %collective-permute-start.10 = (f32[64,256]{1,0:T(8,128)S(1)}, f32[64,256]{1,0:T(8,128)S(1)}, u32[]{:S(2)}, u32[]{:S(2)}) collective-permute-start(f32[64,256]{1,0:T(8,128)S(1)} %gram_rows.1.refs_0_), channel_id=1, source_target_pairs={{0,2},{1,3},{2,0},{3,1},{4,6},{5,7},{6,4},{7,5},{8,10},{9,11},{10,... | collective-permute-start | bytes 196616 | tf_op jit(solution)/shard_map/ppermute | solution.py:417
  101.0 10.8 %collective-permute-start.11 = (f32[64,256]{1,0:T(8,128)S(1)}, f32[64,256]{1,0:T(8,128)S(1)}, u32[]{:S(2)}, u32[]{:S(2)}) collective-permute-start(f32[64,256]{1,0:T(8,128)S(1)} %gram_rows.1.refs_0_), channel_id=1, source_target_pairs={{0,3},{1,0},{2,1},{3,2},{4,7},{5,4},{6,5},{7,6},{8,11},{9,8},{10,9... | collective-permute-start | bytes 196616 | tf_op jit(solution)/shard_map/ppermute | solution.py:417
  106.8 21.6 %collective-permute-start.12 = (f32[32,32,128]{2,1,0:T(8,128)S(1)}, f32[32,32,128]{2,1,0:T(8,128)S(1)}, u32[]{:S(2)}, u32[]{:S(2)}) collective-permute-start(f32[32,32,128]{2,1,0:T(8,128)S(1)} %slice.14.refs_0_), channel_id=1, source_target_pairs={{0,1},{1,2},{2,3},{3,0},{4,5},{5,6},{6,7},{7,4},{8,9},{9,10},{10,1... | collective-permute-start | bytes 1572872 | tf_op jit(solution)/shard_map/ppermute | solution.py:417
  106.9 21.5 %collective-permute-start.13 = (f32[32,32,128]{2,1,0:T(8,128)S(1)}, f32[32,32,128]{2,1,0:T(8,128)S(1)}, u32[]{:S(2)}, u32[]{:S(2)}) collective-permute-start(f32[32,32,128]{2,1,0:T(8,128)S(1)} %slice.14.refs_0_), channel_id=1, source_target_pairs={{0,2},{1,3},{2,0},{3,1},{4,6},{5,7},{6,4},{7,5},{8,10},{9,11},{10,... | collective-permute-start | bytes 1572872 | tf_op jit(solution)/shard_map/ppermute | solution.py:417
  107.4 21.6 %collective-permute-start.14 = (f32[32,32,128]{2,1,0:T(8,128)S(1)}, f32[32,32,128]{2,1,0:T(8,128)S(1)}, u32[]{:S(2)}, u32[]{:S(2)}) collective-permute-start(f32[32,32,128]{2,1,0:T(8,128)S(1)} %slice.14.refs_0_), channel_id=1, source_target_pairs={{0,3},{1,0},{2,1},{3,2},{4,7},{5,4},{6,5},{7,6},{8,11},{9,8},{10,9... | collective-permute-start | bytes 1572872 | tf_op jit(solution)/shard_map/ppermute | solution.py:417
  131.2 1.8 collective-permute-start.15
  139.3 4.0 %collective-permute-start.16 = (bf16[2048,256]{1,0:T(8,128)(2,1)S(1)}, bf16[2048,256]{1,0:T(8,128)(2,1)S(1)}, u32[]{:S(2)}, u32[]{:S(2)}) collective-permute-start(bf16[2048,256]{1,0:T(8,128)(2,1)S(1)} %project_half.1.basis_ref), channel_id=1, source_target_pairs={{0,128},{128,0},{1,129},{129,1},{2,130},{130,2},{3,131},{131,3},{4... | collective-permute-start | bytes 3145736 | tf_op jit(solution)/shard_map/ppermute | solution.py:417
  139.6 2.8 %copy-start.1 = (bf16[768,4096]{1,0:T(8,128)(2,1)S(1)}, bf16[768,4096]{1,0:T(8,128)(2,1)}, u32[]{:S(2)}) copy-start(bf16[768,4096]{1,0:T(8,128)(2,1)} %rows_ref.7) | copy-start | bytes 18874372
  144.4 1.8 collective-permute-start.17
  149.2 50.2 %all-to-all-start.2 = ((bf16[128,24,256]{2,1,0:T(8,128)(2,1)}), bf16[128,24,256]{2,1,0:T(8,128)(2,1)S(1)}, u32[]{:S(2)}, u32[]{:S(2)}) async-start(bf16[128,24,256]{2,1,0:T(8,128)(2,1)} %bitcast.5), calls=%async_computation.2 | async-start | bytes 3145728 | tf_op jit(solution)/shard_map/all_to_all | solution.py:486

commit v6 on v5

--- a/solution.py
+++ b/solution.py
@@ -32,6 +32,32 @@
     (ah, al), (bh, bl) = a, b
     mul = functools.partial(jnp.dot, preferred_element_type=jnp.float32)
     return mul(ah, bh) + (mul(ah, bl) + mul(al, bh))
+
+
+POWERS = (64, 32, 16, 8, 4)
+
+
+def scaled(value):
+    top = jnp.max(jnp.abs(value), axis=(0, 1), keepdims=True)
+    factor, power = jnp.ones_like(top), jnp.zeros_like(top)
+    for p in POWERS:
+        large = top * factor >= 2.0 ** (11 + p)
+        factor = jnp.where(large, factor * 2.0**-p, factor)
+        power = jnp.where(large, power - p, power)
+    for p in POWERS:
+        small = top * factor < 2.0 ** (15 - p)
+        factor = jnp.where(small, factor * 2.0**p, factor)
+        power = jnp.where(small, power + p, power)
+    return value * factor, power
+
+
+def unscale_factor(power):
+    factor = jnp.ones_like(power)
+    for p in POWERS:
+        up, down = power >= p, power <= -p
+        factor = jnp.where(up, factor * 2.0**-p, jnp.where(down, factor * 2.0**p, factor))
+        power = jnp.where(up, power - p, jnp.where(down, power + p, power))
+    return factor
 
 
 def invert_kernel(spot_ref, *refs):
@@ -100,7 +126,7 @@
 def moment_kernel(*refs):
     total = None
     for part_ref in refs[:-1]:
-        part = whole_rows(part_ref[...])
+        part = plain_rows(part_ref)
         term = dot_f32(part, part, ROW_DIMS)
         total = term if total is None else total + term
     refs[-1][...] = total
@@ -143,11 +169,11 @@
     for step, part_ref in enumerate(parts):
         place = lax.rem(spot_ref[0] + len(parts) - step, len(parts))
         rows = pl.ds(pl.multiple_of(place * height, height), height)
-        out_ref[rows, :] = dot_split(split_two(whole_rows(part_ref[...])), weight).astype(jnp.bfloat16)
+        out_ref[rows, :] = dot_split(split_two(plain_rows(part_ref)), weight).astype(jnp.bfloat16)
 
 
 def project_half(spot, inverse, moment, other, parts):
-    chunk, rank = parts[0].shape[0] * parts[0].shape[1] // 2, inverse.shape[0]
+    chunk, rank = parts[0].shape[0] * (parts[0].shape[1] - 8) // 2, inverse.shape[0]
     return pl.pallas_call(
         whiten_kernel,
         in_specs=[pl.BlockSpec(memory_space=pltpu.SMEM)]
@@ -202,34 +228,51 @@
     )(spot, embeddings, sketch, labels)
 
 
-def join_kernel(side, keep_ref, got_ref, extra_ref, out_ref):
-    height = extra_ref.shape[0]
-    out_ref[...] = keep_ref[...] + got_ref[...]
-    out_ref[side * height : (side + 1) * height, :] += extra_ref[...]
+def join_kernel(side, keep_ref, got_ref, extra_ref, body_ref, tail_ref):
+    rank, width = body_ref.shape
+    total = keep_ref[...] + got_ref[...]
+    extra = jnp.concatenate(
+        [extra_ref[...], jnp.zeros_like(extra_ref)][:: 1 - 2 * side], axis=0
+    )
+    total = total + extra
+    body, power = scaled(total[:, :width])
+    body_ref[...] = body
+    tail = total[:, width:]
+    row = lax.broadcasted_iota(jnp.int32, tail.shape, 0)
+    lane = lax.broadcasted_iota(jnp.int32, tail.shape, 1)
+    tail_ref[...] = jnp.where((row == rank - 1) & (lane >= 64), power, tail)
 
 
 def join_chunk(keep, got, extra, side):
-    return pl.pallas_call(
+    rank, width = keep.shape
+    body, tail = pl.pallas_call(
         functools.partial(join_kernel, side),
-        out_shape=jax.ShapeDtypeStruct(keep.shape, jnp.float32),
+        out_shape=[
+            jax.ShapeDtypeStruct((rank, width - 128), jnp.float32),
+            jax.ShapeDtypeStruct((rank, 128), jnp.float32),
+        ],
         compiler_params=GRANT,
         cost_estimate=pl.CostEstimate(flops=400000, bytes_accessed=2000000, transcendentals=0),
         name="join_chunk",
     )(keep, got, extra)
+    return body.astype(jnp.float16), tail
 
 
 def line_kernel(gram_piece, *refs):
-    parts, out_ref = refs[:-1], refs[-1]
+    first, second, out_ref = refs[0], refs[1], refs[-1]
     plane = out_ref.shape[0]
-    total = parts[0][...] + parts[1][...]
-    for part_ref in parts[2:]:
-        total = total + part_ref[...]
+    total = first[...] + second[...]
     rank, width = total.shape[0], total.shape[1] - 128
+    body, tail = total[:, :width], total[:, width:]
+    for body_ref, tail_ref in zip(refs[2:-1:2], refs[3:-1:2]):
+        more = tail_ref[...]
+        body = body + body_ref[...] * unscale_factor(more[rank - 1 :, 127:])
+        tail = tail + more
     piece = width // plane
-    turned = total[:, :width].T.reshape(plane, piece, rank)
+    turned = body.T.reshape(plane, piece, rank)
     out_ref[:, :piece, :] = turned[:, :, :128]
     out_ref[:, piece : 2 * piece, :] = turned[:, :, 128:]
-    tail = total[:, width:].T.reshape(2, plane, gram_piece, rank)
+    tail = tail.T.reshape(2, plane, gram_piece, rank)
     gram, labels = tail[0], tail[1][:, :1, :128]
     fill = jnp.zeros((plane, out_ref.shape[1] - 2 * (piece + gram_piece) - 1, 128), jnp.float32)
     out_ref[:, 2 * piece :, :] = jnp.concatenate(
@@ -250,23 +293,44 @@
     )(*parts)
 
 
-def plane_kernel(label_row, parts_ref, out_ref, label_ref):
-    out_ref[...] = jnp.broadcast_to(jnp.sum(parts_ref[...], axis=0, keepdims=True), out_ref.shape)
-    label_ref[...] = parts_ref[:, label_row, :].astype(jnp.int32) - 1
-
-
-def plane_total(parts, label_row):
+def plane_kernel(piece, gram_piece, parts_ref, out_ref, label_ref):
+    cut, end = 2 * piece, 2 * (piece + gram_piece)
+    total = jnp.sum(parts_ref[:, :end, :], axis=0)
+    rows, power = scaled(total[:cut])
+    gram, gram_power = scaled(total[cut:])
+    lanes = total.shape[1]
+    pieces = [rows, jnp.broadcast_to(power, (1, lanes))]
+    for term in range(3):
+        short = gram.astype(jnp.bfloat16).astype(jnp.float32)
+        pieces.append(short)
+        gram = gram - short
+    pieces.append(jnp.broadcast_to(gram_power, (1, lanes)))
+    filled = sum(p.shape[0] for p in pieces)
+    pieces.append(jnp.zeros((out_ref.shape[0] - filled, lanes), jnp.float32))
+    out_ref[...] = jnp.concatenate(pieces, axis=0)
+    label_ref[...] = parts_ref[:, end, :].astype(jnp.int32) - 1
+
+
+def plane_total(parts, piece, gram_piece):
     plane, _, lanes = parts.shape
-    return pl.pallas_call(
-        functools.partial(plane_kernel, label_row),
+    rows = 2 * piece + 6 * gram_piece + 2
+    rows += -rows % 16
+    return pl.pallas_call(
+        functools.partial(plane_kernel, piece, gram_piece),
         out_shape=[
-            jax.ShapeDtypeStruct(parts.shape, jnp.float32),
+            jax.ShapeDtypeStruct((rows, lanes), jnp.float32),
             jax.ShapeDtypeStruct((plane, lanes), jnp.int32),
         ],
         compiler_params=GRANT,
         cost_estimate=pl.CostEstimate(flops=1000000, bytes_accessed=1600000, transcendentals=0),
         name="plane_total",
     )(parts)
+
+
+def plain_rows(part_ref):
+    part = part_ref[...]
+    cut = part.shape[1] - 8
+    return whole_rows(part[:, :cut] * unscale_factor(part[:, cut : cut + 1]))
 
 
 def whole_rows(part):
@@ -275,15 +339,17 @@
     return jnp.concatenate([t.reshape(plane * pair // 2, lanes) for t in sides], axis=1)
 
 
-def gram_kernel(piece, gram_piece, parts_ref, out_ref):
-    start = 2 * piece
-    out_ref[...] = whole_rows(parts_ref[:, start : start + 2 * gram_piece, :])
-
-
-def gram_rows(parts, piece, gram_piece):
+def gram_kernel(parts_ref, out_ref):
+    pair = 2 * out_ref.shape[0] // parts_ref.shape[0]
+    terms = [parts_ref[:, 1 + t * pair : 1 + (t + 1) * pair, :] for t in range(3)]
+    power = parts_ref[:, 1 + 3 * pair : 2 + 3 * pair, :]
+    out_ref[...] = whole_rows((terms[0] + (terms[1] + terms[2])) * unscale_factor(power))
+
+
+def gram_rows(parts, gram_piece):
     plane, _, lanes = parts.shape
     return pl.pallas_call(
-        functools.partial(gram_kernel, piece, gram_piece),
+        gram_kernel,
         out_shape=jax.ShapeDtypeStruct((plane * gram_piece, 2 * lanes), jnp.float32),
         compiler_params=GRANT,
         cost_estimate=pl.CostEstimate(flops=10000, bytes_accessed=200000, transcendentals=0),
@@ -448,8 +514,9 @@
     far = far[0] + far[1]
     from_below = shift(far[: rank // 2], "x", 1)
     from_above = shift(far[rank // 2 :], "x", line - 1)
-    from_below = shift(join_chunk(*up, from_below, 0), "x", 1)
-    from_above = shift(join_chunk(*down, from_above, 1), "x", line - 1)
+    from_below = [shift(part, "x", 1) for part in join_chunk(*up, from_below, 0)]
+    from_above = [shift(part, "x", line - 1) for part in join_chunk(*down, from_above, 1)]
+    arrived = [part.astype(jnp.float32) for part in from_below + from_above]
 
     def target_of(dest):
         owner = dest // capacity
@@ -460,16 +527,18 @@
 
     targets = by_core(target_of(dest_index), target_of(shift(dest_index, "narrow", 1)))
 
-    packed = line_total([*near, from_below, from_above], plane, gram_piece)
+    packed = line_total([*near, *arrived], plane, gram_piece)
     packed, targets = lax.optimization_barrier((packed, targets))
     packed = lax.all_to_all(packed, PLANE, 0, 0, tiled=True)
-    packed, arrived_labels = plane_total(packed, 2 * (piece + gram_piece))
+    packed, arrived_labels = plane_total(packed, piece, gram_piece)
+    packed = jnp.broadcast_to(packed.astype(jnp.float16)[None], (plane,) + packed.shape)
     packed = lax.all_to_all(packed, PLANE, 0, 0, tiled=True)
-    gram_line = gram_rows(packed, piece, gram_piece)
+    gram_line = gram_rows(packed[:, 2 * piece :].astype(jnp.float32), gram_piece)
     gram_parts = [gram_line] + [shift(gram_line, "x", step) for step in range(1, line)]
     packed, gram_parts[1] = lax.optimization_barrier((packed, gram_parts[1]))
-    cross_line = packed[:, : 2 * piece]
+    cross_line = packed[:, : 2 * piece + 8]
     cross_parts = [cross_line] + [shift(cross_line, "x", step) for step in range(1, line)]
+    cross_parts = [part.astype(jnp.float32) for part in cross_parts]
     arrived_labels = arrived_labels[:, : cores * line * SLOTS].reshape(plane, cores, line, SLOTS)
     arrived_labels = arrived_labels[..., :capacity].transpose(1, 0, 2, 3)
 

time: 201 us -> 188 us (0.935)
  waiting for transfers between devices: 80.3 us -> 62.7 us
  blocking collectives: 53.3 us -> 48 us
  Pallas kernels: 31.1 us -> 35.3 us
  starting transfers between devices: 23.4 us -> 27.3 us
    ppermute x18 -> x20, waiting for transfers between devices: 39.4 us -> 21.9 us  [shift(): lax.ppermute(value, axis, [(i, (i + step) % size) for i in range(size)])]
    all_to_all x2, blocking collectives: 53.3 us -> 48 us  [local(): packed = lax.all_to_all(packed, PLANE, 0, 0, tiled=True)]
    ppermute x18 -> x20, starting transfers between devices: 15.1 us -> 18.8 us  [shift(): lax.ppermute(value, axis, [(i, (i + step) % size) for i in range(size)])]
  transfers between devices with their start and end apart: 19 -> 21, of which waited for: 11 -> 8; matrix products, arithmetic and copies ran while one was open for 1% -> 1% of each run, Pallas kernels for 8% -> 9%
where the time goes in v6:
time: 188 us
  waiting for transfers between devices  62.7 us (33%)
  blocking collectives  48 us (26%)
  Pallas kernels  35.3 us (19%)
  starting transfers between devices  27.3 us (15%)
  local copies, waits for them, and re-layouts  8.55 us (5%)
  matrix products  4.03 us (2%)
    all_to_all x2, blocking collectives, local(): packed = lax.all_to_all(packed, PLANE, 0, 0, tiled=True)  48 us
    all_to_all x1, waiting for transfers between devices, local(): arrived = lax.all_to_all(send_rows, ('y', 'z', 'x'), 0, 0, tiled=True)  40.8 us
    ppermute x20, waiting for transfers between devices, shift(): lax.ppermute(value, axis, [(i, (i + step) % size) for i in range(size)])  21.9 us
    ppermute x20, starting transfers between devices, shift(): lax.ppermute(value, axis, [(i, (i + step) % size) for i in range(size)])  18.8 us
    pallas_call x1, Pallas kernels, invert_factor(): pl.pallas_call(invert_kernel, in_specs=[pl.BlockSpec(memory_space=pltpu.S...  10.8 us
    all_to_all x1, starting transfers between devices, local(): arrived = lax.all_to_all(send_rows, ('y', 'z', 'x'), 0, 0, tiled=True)  8.43 us
    pallas_call x1, Pallas kernels, project_half(): pl.pallas_call(whiten_kernel, in_specs=[pl.BlockSpec(memory_space=pltpu.S...  6.99 us
    unnamed x9, local copies, waits for them, and re-layouts  5.77 us
  transfers between devices with their start and end apart: 21, of which 8 were waited for; matrix products, arithmetic and copies ran while one was open for 1% of the time, Pallas kernels for 9%

profile of v6, /device:TPU:32, one launch (start us, length us, event | category | flops | bytes accessed | tf_op | source)
XLA Modules:
  0.0 187.6 jit_solution(4843654618177245131)
XLA Ops:
  0.7 1.4 copy-done.2
  3.0 1.6 route_rows.1
  4.5 4.0 %fusion.2.sketch_ref = bf16[768,256]{1,0:T(8,128)(2,1)S(1)} fusion(bf16[768,4096]{1,0:T(8,128)(2,1)S(1)} %copy-done, s32[4096,256]{1,0:T(8,128)} %param.5), kind=kOutput, calls=%fused_computation.2 | convolution fusion | flops 1611857920 | bytes 10878976 | tf_op jit(solution)/shard_map/dot_general | solution.py:498
  10.0 2.7 %cross_chunks.2 = (f32[256,640]{1,0:T(8,128)}, f32[256,640]{1,0:T(8,128)S(1)}, f32[256,640]{1,0:T(8,128)S(1)}, f32[256,640]{1,0:T(8,128)S(1)}, f32[256,640]{1,0:T(8,128)}, /*index=5*/f32[256,640]{1,0:T(8,128)S(1)}) custom-call(s32[3]{0:T(128)S(1)} %pad_add_fusion.spot_ref, bf16[768,4096]{1,0:T(8,128)(2,1)S(1)} %copy-done, ...), custom_call_target="tpu_custom_call" | custom-call | flops 1207959552 | bytes 3000000 | tf_op jit(solution)/shard_map/cross_chunks/pallas_call | solution.py:218
  14.2 2.8 %collective-permute-start.7 = (f32[128,640]{1,0:T(8,128)}, f32[128,640]{1,0:T(8,128)}, u32[]{:S(2)}, u32[]{:S(2)}) collective-permute-start(f32[128,640]{1,0:T(8,128)} %get-tuple-element.65), channel_id=1, source_target_pairs={{0,3},{1,0},{2,1},{3,2},{4,7},{5,4},{6,5},{7,6},{8,11},{9,8},{10,9... | collective-permute-start | bytes 983048 | tf_op jit(solution)/shard_map/ppermute | solution.py:483
  17.5 7.4 %collective-permute-done.7.extra_ref = f32[128,640]{1,0:T(8,128)} collective-permute-done((f32[128,640]{1,0:T(8,128)}, f32[128,640]{1,0:T(8,128)}, u32[]{:S(2)}, u32[]{:S(2)}) %collective-permute-start.7) | collective-permute-done | bytes 327712 | tf_op jit(solution)/shard_map/ppermute | solution.py:483
  26.2 3.8 %collective-permute-start.8 = (f16[256,512]{1,0:T(8,128)(2,1)S(1)}, f16[256,512]{1,0:T(8,128)(2,1)S(1)}, u32[]{:S(2)}, u32[]{:S(2)}) collective-permute-start(f16[256,512]{1,0:T(8,128)(2,1)S(1)} %convert_element_type.40), channel_id=1, source_target_pairs={{0,3},{1,0},{2,1},{3,2},{4,7},{5,4},{6,5},{7,6},{8,11},{9,8},{10,9... | collective-permute-start | bytes 786440 | tf_op jit(solution)/shard_map/ppermute | solution.py:483
  31.5 3.5 %collective-permute-start.9 = (f32[256,128]{1,0:T(8,128)S(1)}, f32[256,128]{1,0:T(8,128)S(1)}, u32[]{:S(2)}, u32[]{:S(2)}) collective-permute-start(f32[256,128]{1,0:T(8,128)S(1)} %get-tuple-element.40), channel_id=1, source_target_pairs={{0,3},{1,0},{2,1},{3,2},{4,7},{5,4},{6,5},{7,6},{8,11},{9,8},{10,9... | collective-permute-start | bytes 393224 | tf_op jit(solution)/shard_map/ppermute | solution.py:483
  35.0 1.6 collective-permute-done.8
  36.6 5.0 %collective-permute-done.4 = f16[256,512]{1,0:T(8,128)(2,1)S(1)} collective-permute-done((f16[256,512]{1,0:T(8,128)(2,1)S(1)}, f16[256,512]{1,0:T(8,128)(2,1)S(1)}, u32[]{:S(2)}, u32[]{:S(2)}) %collective-permute-start.4) | collective-permute-done | bytes 262176 | tf_op jit(solution)/shard_map/ppermute | solution.py:483
  43.0 1.4 line_total.1
  44.5 30.3 %all_to_all.15.parts_ref = f32[32,40,128]{2,1,0:T(8,128)S(1)} all-to-all(f32[32,40,128]{2,1,0:T(8,128)S(1)} %line_total.1), channel_id=1, replica_groups=mesh['narrow'=2,'y'=4,'z'=8,'x'=4] {'y','z'}, dimensions={0} | all-to-all | bytes 1310720 | tf_op jit(solution)/shard_map/all_to_all | solution.py:532
  75.0 17.7 %all_to_all.16 = f16[32,48,128]{2,1,0:T(8,128)(2,1)S(1)} all-to-all(f16[32,48,128]{2,1,0:T(8,128)(2,1)S(1)} %broadcast_in_dim.5), channel_id=1, replica_groups=mesh['narrow'=2,'y'=4,'z'=8,'x'=4] {'y','z'}, dimensions={0} | all-to-all | bytes 786432 | tf_op jit(solution)/shard_map/all_to_all | solution.py:535
  94.1 2.2 %collective-permute-start.13 = (f32[64,256]{1,0:T(8,128)S(1)}, f32[64,256]{1,0:T(8,128)S(1)}, u32[]{:S(2)}, u32[]{:S(2)}) collective-permute-start(f32[64,256]{1,0:T(8,128)S(1)} %gram_rows.1.refs_0_), channel_id=1, source_target_pairs={{0,3},{1,0},{2,1},{3,2},{4,7},{5,4},{6,5},{7,6},{8,11},{9,8},{10,9... | collective-permute-start | bytes 196616 | tf_op jit(solution)/shard_map/ppermute | solution.py:483
  96.3 3.6 %collective-permute-done.11.refs_1_ = f32[64,256]{1,0:T(8,128)S(1)} collective-permute-done((f32[64,256]{1,0:T(8,128)S(1)}, f32[64,256]{1,0:T(8,128)S(1)}, u32[]{:S(2)}, u32[]{:S(2)}) %collective-permute-start.11) | collective-permute-done | bytes 65568 | tf_op jit(solution)/shard_map/ppermute | solution.py:483
  100.6 2.7 %collective-permute-start.16 = (f16[32,40,128]{2,1,0:T(8,128)(2,1)S(1)}, f16[32,40,128]{2,1,0:T(8,128)(2,1)S(1)}, u32[]{:S(2)}, u32[]{:S(2)}) collective-permute-start(f16[32,40,128]{2,1,0:T(8,128)(2,1)S(1)} %get-tuple-element.67), channel_id=1, source_target_pairs={{0,3},{1,0},{2,1},{3,2},{4,7},{5,4},{6,5},{7,6},{8,11},{9,8},{10,9... | collective-permute-start | bytes 983048 | tf_op jit(solution)/shard_map/ppermute | solution.py:483
  103.4 10.8 %invert_factor.1.inverse_ref = f32[256,256]{1,0:T(8,128)S(1)} custom-call(s32[1]{0:T(128)} %bitcast.1.spot_ref, f32[64,256]{1,0:T(8,128)S(1)} %gram_rows.1.refs_0_, f32[64,256]{1,0:T(8,128)S(1)} %collective-permute-done.11.refs_1_, f32[64,256]{1,0:T(8,128)S(1)} %collective-permute-done.12.refs_2_, f32[64,256]{1,0:T(8,128)S(1)} %collective-permute-done.13.refs_3_), custom_call_target="tpu_custom_call" | custom-call | flops 20000000000 | bytes 524288 | tf_op jit(solution)/shard_map/invert_factor/pallas_call | solution.py:114
  114.3 2.7 %moment_of.1.moment_ref = f32[256,256]{1,0:T(8,128)S(1)} custom-call(f32[32,40,128]{2,1,0:T(8,128)S(1)} %get-tuple-element.49.refs_0_, f32[32,40,128]{2,1,0:T(8,128)S(1)} %convert_element_type.45.refs_1_, f32[32,40,128]{2,1,0:T(8,128)S(1)} %convert_element_type.46.refs_2_, f32[32,40,128]{2,1,0:T(8,128)S(1)} %convert_element_type.47.refs_3_), custom_call_target="tpu_custom_call" | custom-call | flops 4000000000 | bytes 2359296 | tf_op jit(solution)/shard_map/moment_of/pallas_call | solution.py:137
  117.4 1.5 collective-permute-done.17.other_ref
  118.9 7.0 %project_half.1.basis_ref = bf16[2048,256]{1,0:T(8,128)(2,1)S(1)} custom-call(s32[1]{0:T(128)} %bitcast.1.spot_ref, f32[256,256]{1,0:T(8,128)S(1)} %invert_factor.1.inverse_ref, f32[256,256]{1,0:T(8,128)S(1)} %moment_of.1.moment_ref, f32[256,256]{1,0:T(8,128)S(1)} %collective-permute-done.17.other_ref, f32[32,40,128]{2,1,0:T(8,128)S(1)} %get-tuple-element.49.refs_0_, ...), custom_call_target="tpu_custom_call" | custom-call | flops 12000000000 | bytes 4194304 | tf_op jit(solution)/shard_map/project_half/pallas_call | solution.py:177
  126.1 2.8 %copy-done.1 = bf16[768,4096]{1,0:T(8,128)(2,1)S(1)} copy-done((bf16[768,4096]{1,0:T(8,128)(2,1)S(1)}, bf16[768,4096]{1,0:T(8,128)(2,1)}, u32[]{:S(2)}) %copy-start.1) | copy-done | bytes 6291480
  132.8 2.9 %place_rows.1 = bf16[64,48,256]{2,1,0:T(8,128)(2,1)} custom-call(s32[1,768]{1,0:T(1,128)S(1)} %broadcast_select_fusion.3.first_target, s32[1,768]{1,0:T(1,128)S(1)} %get-tuple-element.43.second_target, bf16[768,256]{1,0:T(8,128)(2,1)S(1)} %get-tuple-element.64.first_ref, bf16[768,256]{1,0:T(8,128)(2,1)S(1)} %get-tuple-element.63.second_ref), custom_call_target="tpu_custom_call" | custom-call | flops 1207959552 | bytes 3145728 | tf_op jit(solution)/shard_map/place_rows/pallas_call | solution.py:464
  135.7 8.4 %all-to-all-start.2 = ((bf16[128,24,256]{2,1,0:T(8,128)(2,1)}), bf16[128,24,256]{2,1,0:T(8,128)(2,1)S(1)}, u32[]{:S(2)}, u32[]{:S(2)}) async-start(bf16[128,24,256]{2,1,0:T(8,128)(2,1)} %bitcast.5), calls=%async_computation.2 | async-start | bytes 3145728 | tf_op jit(solution)/shard_map/all_to_all | solution.py:555
  145.1 40.8 %all-to-all-done.2 = bf16[128,24,256]{2,1,0:T(8,128)(2,1)S(1)} async-done(((bf16[128,24,256]{2,1,0:T(8,128)(2,1)}), bf16[128,24,256]{2,1,0:T(8,128)(2,1)S(1)}, u32[]{:S(2)}, u32[]{:S(2)}) %all-to-all-start.2) | async-done | bytes 1572896 | tf_op jit(solution)/shard_map/all_to_all | solution.py:555
  (66 shorter events, 17.9 us)
Async XLA Ops:
  0.6 3.9 %copy-start = (bf16[768,4096]{1,0:T(8,128)(2,1)S(1)}, bf16[768,4096]{1,0:T(8,128)(2,1)}, u32[]{:S(2)}) copy-start(bf16[768,4096]{1,0:T(8,128)(2,1)} %rows_ref.7) | copy-start | bytes 18874372
  0.6 1.4 copy-start.2
  9.9 3.4 %collective-permute-start.2 = (f32[256,640]{1,0:T(8,128)S(1)}, f32[256,640]{1,0:T(8,128)S(1)}, u32[]{:S(2)}, u32[]{:S(2)}) collective-permute-start(f32[256,640]{1,0:T(8,128)S(1)} %get-tuple-element.34), channel_id=1, source_target_pairs={{0,128},{128,0},{1,129},{129,1},{2,130},{130,2},{3,131},{131,3},{4... | collective-permute-start | bytes 1966088 | tf_op jit(solution)/shard_map/ppermute | solution.py:483
  12.8 4.5 %collective-permute-start.6 = (f32[256,640]{1,0:T(8,128)S(1)}, f32[256,640]{1,0:T(8,128)S(1)}, u32[]{:S(2)}, u32[]{:S(2)}) collective-permute-start(f32[256,640]{1,0:T(8,128)S(1)} %get-tuple-element.38), channel_id=1, source_target_pairs={{0,128},{128,0},{1,129},{129,1},{2,130},{130,2},{3,131},{131,3},{4... | collective-permute-start | bytes 1966088 | tf_op jit(solution)/shard_map/ppermute | solution.py:483
  13.3 16.7 %collective-permute-start.1 = (f32[256,640]{1,0:T(8,128)}, f32[256,640]{1,0:T(8,128)S(1)}, u32[]{:S(2)}, u32[]{:S(2)}) collective-permute-start(f32[256,640]{1,0:T(8,128)} %get-tuple-element.32), channel_id=1, source_target_pairs={{0,128},{128,0},{1,129},{129,1},{2,130},{130,2},{3,131},{131,3},{4... | collective-permute-start | bytes 1966088 | tf_op jit(solution)/shard_map/ppermute | solution.py:483
  14.2 10.7 %collective-permute-start.7 = (f32[128,640]{1,0:T(8,128)}, f32[128,640]{1,0:T(8,128)}, u32[]{:S(2)}, u32[]{:S(2)}) collective-permute-start(f32[128,640]{1,0:T(8,128)} %get-tuple-element.65), channel_id=1, source_target_pairs={{0,3},{1,0},{2,1},{3,2},{4,7},{5,4},{6,5},{7,6},{8,11},{9,8},{10,9... | collective-permute-start | bytes 983048 | tf_op jit(solution)/shard_map/ppermute | solution.py:483
  17.0 13.0 %collective-permute-start.3 = (f32[128,640]{1,0:T(8,128)}, f32[128,640]{1,0:T(8,128)}, u32[]{:S(2)}, u32[]{:S(2)}) collective-permute-start(f32[128,640]{1,0:T(8,128)} %get-tuple-element.66), channel_id=1, source_target_pairs={{0,1},{1,2},{2,3},{3,0},{4,5},{5,6},{6,7},{7,4},{8,9},{9,10},{10,1... | collective-permute-start | bytes 983048 | tf_op jit(solution)/shard_map/ppermute | solution.py:483
  17.0 24.7 %collective-permute-start = (f32[256,640]{1,0:T(8,128)}, f32[256,640]{1,0:T(8,128)}, u32[]{:S(2)}, u32[]{:S(2)}) collective-permute-start(f32[256,640]{1,0:T(8,128)} %get-tuple-element.30), channel_id=1, source_target_pairs={{0,128},{128,0},{1,129},{129,1},{2,130},{130,2},{3,131},{131,3},{4... | collective-permute-start | bytes 1966088 | tf_op jit(solution)/shard_map/ppermute | solution.py:483
  17.2 14.1 %collective-permute-start.10 = (s32[1,768]{1,0:T(1,128)S(1)}, s32[1,768]{1,0:T(1,128)S(1)}, u32[]{:S(2)}, u32[]{:S(2)}) collective-permute-start(s32[1,768]{1,0:T(1,128)S(1)} %get-tuple-element.41), channel_id=1, source_target_pairs={{0,128},{128,0},{1,129},{129,1},{2,130},{130,2},{3,131},{131,3},{4... | collective-permute-start | bytes 9224 | tf_op jit(solution)/shard_map/ppermute | solution.py:483
  26.2 10.4 %collective-permute-start.8 = (f16[256,512]{1,0:T(8,128)(2,1)S(1)}, f16[256,512]{1,0:T(8,128)(2,1)S(1)}, u32[]{:S(2)}, u32[]{:S(2)}) collective-permute-start(f16[256,512]{1,0:T(8,128)(2,1)S(1)} %convert_element_type.40), channel_id=1, source_target_pairs={{0,3},{1,0},{2,1},{3,2},{4,7},{5,4},{6,5},{7,6},{8,11},{9,8},{10,9... | collective-permute-start | bytes 786440 | tf_op jit(solution)/shard_map/ppermute | solution.py:483
  31.3 10.3 %collective-permute-start.4 = (f16[256,512]{1,0:T(8,128)(2,1)S(1)}, f16[256,512]{1,0:T(8,128)(2,1)S(1)}, u32[]{:S(2)}, u32[]{:S(2)}) collective-permute-start(f16[256,512]{1,0:T(8,128)(2,1)S(1)} %convert_element_type.38), channel_id=1, source_target_pairs={{0,1},{1,2},{2,3},{3,0},{4,5},{5,6},{6,7},{7,4},{8,9},{9,10},{10,1... | collective-permute-start | bytes 786440 | tf_op jit(solution)/shard_map/ppermute | solution.py:483
  31.5 10.2 %collective-permute-start.9 = (f32[256,128]{1,0:T(8,128)S(1)}, f32[256,128]{1,0:T(8,128)S(1)}, u32[]{:S(2)}, u32[]{:S(2)}) collective-permute-start(f32[256,128]{1,0:T(8,128)S(1)} %get-tuple-element.40), channel_id=1, source_target_pairs={{0,3},{1,0},{2,1},{3,2},{4,7},{5,4},{6,5},{7,6},{8,11},{9,8},{10,9... | collective-permute-start | bytes 393224 | tf_op jit(solution)/shard_map/ppermute | solution.py:483
  34.9 8.1 %collective-permute-start.5 = (f32[256,128]{1,0:T(8,128)S(1)}, f32[256,128]{1,0:T(8,128)S(1)}, u32[]{:S(2)}, u32[]{:S(2)}) collective-permute-start(f32[256,128]{1,0:T(8,128)S(1)} %get-tuple-element.36), channel_id=1, source_target_pairs={{0,1},{1,2},{2,3},{3,0},{4,5},{5,6},{6,7},{7,4},{8,9},{9,10},{10,1... | collective-permute-start | bytes 393224 | tf_op jit(solution)/shard_map/ppermute | solution.py:483
  93.0 7.0 %collective-permute-start.11 = (f32[64,256]{1,0:T(8,128)S(1)}, f32[64,256]{1,0:T(8,128)S(1)}, u32[]{:S(2)}, u32[]{:S(2)}) collective-permute-start(f32[64,256]{1,0:T(8,128)S(1)} %gram_rows.1.refs_0_), channel_id=1, source_target_pairs={{0,1},{1,2},{2,3},{3,0},{4,5},{5,6},{6,7},{7,4},{8,9},{9,10},{10,1... | collective-permute-start | bytes 196616 | tf_op jit(solution)/shard_map/ppermute | solution.py:483
  93.4 9.9 %collective-permute-start.12 = (f32[64,256]{1,0:T(8,128)S(1)}, f32[64,256]{1,0:T(8,128)S(1)}, u32[]{:S(2)}, u32[]{:S(2)}) collective-permute-start(f32[64,256]{1,0:T(8,128)S(1)} %gram_rows.1.refs_0_), channel_id=1, source_target_pairs={{0,2},{1,3},{2,0},{3,1},{4,6},{5,7},{6,4},{7,5},{8,10},{9,11},{10,... | collective-permute-start | bytes 196616 | tf_op jit(solution)/shard_map/ppermute | solution.py:483
  94.1 9.3 %collective-permute-start.13 = (f32[64,256]{1,0:T(8,128)S(1)}, f32[64,256]{1,0:T(8,128)S(1)}, u32[]{:S(2)}, u32[]{:S(2)}) collective-permute-start(f32[64,256]{1,0:T(8,128)S(1)} %gram_rows.1.refs_0_), channel_id=1, source_target_pairs={{0,3},{1,0},{2,1},{3,2},{4,7},{5,4},{6,5},{7,6},{8,11},{9,8},{10,9... | collective-permute-start | bytes 196616 | tf_op jit(solution)/shard_map/ppermute | solution.py:483
  100.0 14.1 %collective-permute-start.14 = (f16[32,40,128]{2,1,0:T(8,128)(2,1)S(1)}, f16[32,40,128]{2,1,0:T(8,128)(2,1)S(1)}, u32[]{:S(2)}, u32[]{:S(2)}) collective-permute-start(f16[32,40,128]{2,1,0:T(8,128)(2,1)S(1)} %get-tuple-element.67), channel_id=1, source_target_pairs={{0,1},{1,2},{2,3},{3,0},{4,5},{5,6},{6,7},{7,4},{8,9},{9,10},{10,1... | collective-permute-start | bytes 983048 | tf_op jit(solution)/shard_map/ppermute | solution.py:483
  100.1 14.1 %collective-permute-start.15 = (f16[32,40,128]{2,1,0:T(8,128)(2,1)S(1)}, f16[32,40,128]{2,1,0:T(8,128)(2,1)S(1)}, u32[]{:S(2)}, u32[]{:S(2)}) collective-permute-start(f16[32,40,128]{2,1,0:T(8,128)(2,1)S(1)} %get-tuple-element.67), channel_id=1, source_target_pairs={{0,2},{1,3},{2,0},{3,1},{4,6},{5,7},{6,4},{7,5},{8,10},{9,11},{10,... | collective-permute-start | bytes 983048 | tf_op jit(solution)/shard_map/ppermute | solution.py:483
  100.6 13.6 %collective-permute-start.16 = (f16[32,40,128]{2,1,0:T(8,128)(2,1)S(1)}, f16[32,40,128]{2,1,0:T(8,128)(2,1)S(1)}, u32[]{:S(2)}, u32[]{:S(2)}) collective-permute-start(f16[32,40,128]{2,1,0:T(8,128)(2,1)S(1)} %get-tuple-element.67), channel_id=1, source_target_pairs={{0,3},{1,0},{2,1},{3,2},{4,7},{5,4},{6,5},{7,6},{8,11},{9,8},{10,9... | collective-permute-start | bytes 983048 | tf_op jit(solution)/shard_map/ppermute | solution.py:483
  117.0 1.8 collective-permute-start.17
  125.9 4.0 %collective-permute-start.18 = (bf16[2048,256]{1,0:T(8,128)(2,1)S(1)}, bf16[2048,256]{1,0:T(8,128)(2,1)S(1)}, u32[]{:S(2)}, u32[]{:S(2)}) collective-permute-start(bf16[2048,256]{1,0:T(8,128)(2,1)S(1)} %project_half.1.basis_ref), channel_id=1, source_target_pairs={{0,128},{128,0},{1,129},{129,1},{2,130},{130,2},{3,131},{131,3},{4... | collective-permute-start | bytes 3145736 | tf_op jit(solution)/shard_map/ppermute | solution.py:483
  126.1 2.8 %copy-start.1 = (bf16[768,4096]{1,0:T(8,128)(2,1)S(1)}, bf16[768,4096]{1,0:T(8,128)(2,1)}, u32[]{:S(2)}) copy-start(bf16[768,4096]{1,0:T(8,128)(2,1)} %rows_ref.7) | copy-start | bytes 18874372
  130.9 1.8 collective-permute-start.19
  135.7 50.2 %all-to-all-start.2 = ((bf16[128,24,256]{2,1,0:T(8,128)(2,1)}), bf16[128,24,256]{2,1,0:T(8,128)(2,1)S(1)}, u32[]{:S(2)}, u32[]{:S(2)}) async-start(bf16[128,24,256]{2,1,0:T(8,128)(2,1)} %bitcast.5), calls=%async_computation.2 | async-start | bytes 3145728 | tf_op jit(solution)/shard_map/all_to_all | solution.py:555
  (1 other events, 0.9 us)

commit v7 on v6

--- a/solution.py
+++ b/solution.py
@@ -58,6 +58,32 @@
         factor = jnp.where(up, factor * 2.0**-p, jnp.where(down, factor * 2.0**p, factor))
         power = jnp.where(up, power - p, jnp.where(down, power + p, power))
     return factor
+
+
+def spread_rows(rows, gram, extra, count):
+    def leaf(value):
+        flat, power = scaled(value.reshape(-1, value.shape[2]))
+        shape = (value.shape[0], 1, value.shape[2])
+        return flat.reshape(value.shape), jnp.broadcast_to(power[None], shape)
+
+    pieces = list(leaf(rows))
+    gram, gram_power = leaf(gram)
+    for term in range(3):
+        short = gram.astype(jnp.bfloat16).astype(jnp.float32)
+        pieces.append(short)
+        gram = gram - short
+    pieces += [gram_power] + extra
+    filled = sum(p.shape[1] for p in pieces)
+    if filled < count:
+        shape = (rows.shape[0], count - filled, rows.shape[2])
+        pieces.append(jnp.zeros(shape, jnp.float32))
+    return jnp.concatenate(pieces, axis=1)
+
+
+def joined_gram(parts, start, pair):
+    terms = [parts[:, start + t * pair : start + (t + 1) * pair, :] for t in range(3)]
+    power = parts[:, start + 3 * pair : start + 3 * pair + 1, :]
+    return (terms[0] + (terms[1] + terms[2])) * unscale_factor(power)
 
 
 def invert_kernel(spot_ref, *refs):
@@ -270,20 +296,21 @@
         tail = tail + more
     piece = width // plane
     turned = body.T.reshape(plane, piece, rank)
-    out_ref[:, :piece, :] = turned[:, :, :128]
-    out_ref[:, piece : 2 * piece, :] = turned[:, :, 128:]
     tail = tail.T.reshape(2, plane, gram_piece, rank)
-    gram, labels = tail[0], tail[1][:, :1, :128]
-    fill = jnp.zeros((plane, out_ref.shape[1] - 2 * (piece + gram_piece) - 1, 128), jnp.float32)
-    out_ref[:, 2 * piece :, :] = jnp.concatenate(
-        [gram[:, :, :128], gram[:, :, 128:], labels, fill], axis=1
+    gram, labels = tail[0], tail[1][:, :1, :128].astype(jnp.int32)
+    digits = [(labels % 1024).astype(jnp.float32), (labels // 1024).astype(jnp.float32)]
+    out_ref[...] = spread_rows(
+        jnp.concatenate([turned[:, :, :128], turned[:, :, 128:]], axis=1),
+        jnp.concatenate([gram[:, :, :128], gram[:, :, 128:]], axis=1),
+        digits,
+        out_ref.shape[1],
     )
 
 
 def line_total(parts, plane, gram_piece):
     width = parts[0].shape[1] - 128
-    rows = 2 * (width // plane + gram_piece) + 1
-    rows += -rows % 8
+    rows = 2 * (width // plane) + 6 * gram_piece + 4
+    rows += -rows % 16
     return pl.pallas_call(
         functools.partial(line_kernel, gram_piece),
         out_shape=jax.ShapeDtypeStruct((plane, rows, 128), jnp.float32),
@@ -294,21 +321,14 @@
 
 
 def plane_kernel(piece, gram_piece, parts_ref, out_ref, label_ref):
-    cut, end = 2 * piece, 2 * (piece + gram_piece)
-    total = jnp.sum(parts_ref[:, :end, :], axis=0)
-    rows, power = scaled(total[:cut])
-    gram, gram_power = scaled(total[cut:])
-    lanes = total.shape[1]
-    pieces = [rows, jnp.broadcast_to(power, (1, lanes))]
-    for term in range(3):
-        short = gram.astype(jnp.bfloat16).astype(jnp.float32)
-        pieces.append(short)
-        gram = gram - short
-    pieces.append(jnp.broadcast_to(gram_power, (1, lanes)))
-    filled = sum(p.shape[0] for p in pieces)
-    pieces.append(jnp.zeros((out_ref.shape[0] - filled, lanes), jnp.float32))
-    out_ref[...] = jnp.concatenate(pieces, axis=0)
-    label_ref[...] = parts_ref[:, end, :].astype(jnp.int32) - 1
+    cut, pair = 2 * piece, 2 * gram_piece
+    parts = parts_ref[...]
+    rows = jnp.sum(parts[:, :cut, :] * unscale_factor(parts[:, cut : cut + 1, :]), axis=0)
+    gram = jnp.sum(joined_gram(parts, cut + 1, pair), axis=0)
+    out_ref[...] = spread_rows(rows[None], gram[None], [], out_ref.shape[0])[0]
+    end = cut + 2 + 3 * pair
+    labels = parts[:, end, :] + 1024.0 * parts[:, end + 1, :]
+    label_ref[...] = labels.astype(jnp.int32) - 1
 
 
 def plane_total(parts, piece, gram_piece):
@@ -341,9 +361,7 @@
 
 def gram_kernel(parts_ref, out_ref):
     pair = 2 * out_ref.shape[0] // parts_ref.shape[0]
-    terms = [parts_ref[:, 1 + t * pair : 1 + (t + 1) * pair, :] for t in range(3)]
-    power = parts_ref[:, 1 + 3 * pair : 2 + 3 * pair, :]
-    out_ref[...] = whole_rows((terms[0] + (terms[1] + terms[2])) * unscale_factor(power))
+    out_ref[...] = whole_rows(joined_gram(parts_ref[...], 1, pair))
 
 
 def gram_rows(parts, gram_piece):
@@ -529,7 +547,8 @@
 
     packed = line_total([*near, *arrived], plane, gram_piece)
     packed, targets = lax.optimization_barrier((packed, targets))
-    packed = lax.all_to_all(packed, PLANE, 0, 0, tiled=True)
+    packed = lax.all_to_all(packed.astype(jnp.float16), PLANE, 0, 0, tiled=True)
+    packed = packed.astype(jnp.float32)
     packed, arrived_labels = plane_total(packed, piece, gram_piece)
     packed = jnp.broadcast_to(packed.astype(jnp.float16)[None], (plane,) + packed.shape)
     packed = lax.all_to_all(packed, PLANE, 0, 0, tiled=True)

time: 188 us -> 185 us (0.984)
  blocking collectives: 48 us -> 42.5 us
    all_to_all x2 -> x1, blocking collectives: 48 us -> 17.7 us  [local(): packed = lax.all_to_all(packed, PLANE, 0, 0, tiled=True)]
    all_to_all x0 -> x1, blocking collectives: none -> 24.8 us  [local(): packed = lax.all_to_all(packed.astype(jnp.float16), PLANE, 0, 0, tiled=True)]
  transfers between devices with their start and end apart: 21 -> 21, of which waited for: 8 -> 9; matrix products, arithmetic and copies ran while one was open for 1% -> 1% of each run, Pallas kernels for 9% -> 9%
where the time goes in v7:
time: 185 us; the launch traced here: 184 us
  waiting for transfers between devices  62.7 us (34%)
  blocking collectives  42.5 us (23%)
  Pallas kernels  36.1 us (20%)
  starting transfers between devices  28.4 us (15%)
  local copies, waits for them, and re-layouts  8.55 us (5%)
  matrix products  4.03 us (2%)
    all_to_all x1, waiting for transfers between devices, local(): arrived = lax.all_to_all(send_rows, ('y', 'z', 'x'), 0, 0, tiled=True)  40.8 us
    all_to_all x1, blocking collectives, local(): packed = lax.all_to_all(packed.astype(jnp.float16), PLANE, 0, 0, tiled=True)  24.8 us
    ppermute x20, waiting for transfers between devices, shift(): lax.ppermute(value, axis, [(i, (i + step) % size) for i in range(size)])  21.8 us
    ppermute x20, starting transfers between devices, shift(): lax.ppermute(value, axis, [(i, (i + step) % size) for i in range(size)])  18.9 us
    all_to_all x1, blocking collectives, local(): packed = lax.all_to_all(packed, PLANE, 0, 0, tiled=True)  17.7 us
    pallas_call x1, Pallas kernels, invert_factor(): pl.pallas_call(invert_kernel, in_specs=[pl.BlockSpec(memory_space=pltpu.S...  10.8 us
    all_to_all x1, starting transfers between devices, local(): arrived = lax.all_to_all(send_rows, ('y', 'z', 'x'), 0, 0, tiled=True)  9.57 us
    pallas_call x1, Pallas kernels, project_half(): pl.pallas_call(whiten_kernel, in_specs=[pl.BlockSpec(memory_space=pltpu.S...  6.99 us
  transfers between devices with their start and end apart: 21, of which 9 were waited for; matrix products, arithmetic and copies ran while one was open for 1% of the time, Pallas kernels for 9%

profile of v7, /device:TPU:32, one launch (start us, length us, event | category | flops | bytes accessed | tf_op | source)
XLA Modules:
  0.0 184.2 jit_solution(11533296663683167532)
XLA Ops:
  0.7 1.4 copy-done.2
  3.0 1.6 route_rows.1
  4.5 4.0 %fusion.2.sketch_ref = bf16[768,256]{1,0:T(8,128)(2,1)S(1)} fusion(bf16[768,4096]{1,0:T(8,128)(2,1)S(1)} %copy-done, s32[4096,256]{1,0:T(8,128)} %param.5), kind=kOutput, calls=%fused_computation.2 | convolution fusion | flops 1611857920 | bytes 10878976 | tf_op jit(solution)/shard_map/dot_general | solution.py:516
  10.0 2.7 %cross_chunks.2 = (f32[256,640]{1,0:T(8,128)}, f32[256,640]{1,0:T(8,128)S(1)}, f32[256,640]{1,0:T(8,128)S(1)}, f32[256,640]{1,0:T(8,128)S(1)}, f32[256,640]{1,0:T(8,128)}, /*index=5*/f32[256,640]{1,0:T(8,128)S(1)}) custom-call(s32[3]{0:T(128)S(1)} %pad_add_fusion.spot_ref, bf16[768,4096]{1,0:T(8,128)(2,1)S(1)} %copy-done, ...), custom_call_target="tpu_custom_call" | custom-call | flops 1207959552 | bytes 3000000 | tf_op jit(solution)/shard_map/cross_chunks/pallas_call | solution.py:244
  14.2 2.8 %collective-permute-start.7 = (f32[128,640]{1,0:T(8,128)}, f32[128,640]{1,0:T(8,128)}, u32[]{:S(2)}, u32[]{:S(2)}) collective-permute-start(f32[128,640]{1,0:T(8,128)} %get-tuple-element.65), channel_id=1, source_target_pairs={{0,3},{1,0},{2,1},{3,2},{4,7},{5,4},{6,5},{7,6},{8,11},{9,8},{10,9... | collective-permute-start | bytes 983048 | tf_op jit(solution)/shard_map/ppermute | solution.py:501
  17.5 7.4 %collective-permute-done.7.extra_ref = f32[128,640]{1,0:T(8,128)} collective-permute-done((f32[128,640]{1,0:T(8,128)}, f32[128,640]{1,0:T(8,128)}, u32[]{:S(2)}, u32[]{:S(2)}) %collective-permute-start.7) | collective-permute-done | bytes 327712 | tf_op jit(solution)/shard_map/ppermute | solution.py:501
  26.2 3.8 %collective-permute-start.8 = (f16[256,512]{1,0:T(8,128)(2,1)S(1)}, f16[256,512]{1,0:T(8,128)(2,1)S(1)}, u32[]{:S(2)}, u32[]{:S(2)}) collective-permute-start(f16[256,512]{1,0:T(8,128)(2,1)S(1)} %convert_element_type.46), channel_id=1, source_target_pairs={{0,3},{1,0},{2,1},{3,2},{4,7},{5,4},{6,5},{7,6},{8,11},{9,8},{10,9... | collective-permute-start | bytes 786440 | tf_op jit(solution)/shard_map/ppermute | solution.py:501
  31.5 3.5 %collective-permute-start.9 = (f32[256,128]{1,0:T(8,128)S(1)}, f32[256,128]{1,0:T(8,128)S(1)}, u32[]{:S(2)}, u32[]{:S(2)}) collective-permute-start(f32[256,128]{1,0:T(8,128)S(1)} %get-tuple-element.40), channel_id=1, source_target_pairs={{0,3},{1,0},{2,1},{3,2},{4,7},{5,4},{6,5},{7,6},{8,11},{9,8},{10,9... | collective-permute-start | bytes 393224 | tf_op jit(solution)/shard_map/ppermute | solution.py:501
  35.0 1.6 collective-permute-done.8
  36.6 5.0 %collective-permute-done.4 = f16[256,512]{1,0:T(8,128)(2,1)S(1)} collective-permute-done((f16[256,512]{1,0:T(8,128)(2,1)S(1)}, f16[256,512]{1,0:T(8,128)(2,1)S(1)}, u32[]{:S(2)}, u32[]{:S(2)}) %collective-permute-start.4) | collective-permute-done | bytes 262176 | tf_op jit(solution)/shard_map/ppermute | solution.py:501
  43.0 1.7 line_total.1
  44.8 24.8 %all_to_all.15 = f16[32,48,128]{2,1,0:T(8,128)(2,1)S(1)} all-to-all(f16[32,48,128]{2,1,0:T(8,128)(2,1)S(1)} %convert_element_type.48), channel_id=1, replica_groups=mesh['narrow'=2,'y'=4,'z'=8,'x'=4] {'y','z'}, dimensions={0} | all-to-all | bytes 786432 | tf_op jit(solution)/shard_map/all_to_all | solution.py:550
  70.5 17.7 %all_to_all.16 = f16[32,48,128]{2,1,0:T(8,128)(2,1)S(1)} all-to-all(f16[32,48,128]{2,1,0:T(8,128)(2,1)S(1)} %broadcast_in_dim.5), channel_id=1, replica_groups=mesh['narrow'=2,'y'=4,'z'=8,'x'=4] {'y','z'}, dimensions={0} | all-to-all | bytes 786432 | tf_op jit(solution)/shard_map/all_to_all | solution.py:554
  89.6 2.2 %collective-permute-start.13 = (f32[64,256]{1,0:T(8,128)S(1)}, f32[64,256]{1,0:T(8,128)S(1)}, u32[]{:S(2)}, u32[]{:S(2)}) collective-permute-start(f32[64,256]{1,0:T(8,128)S(1)} %gram_rows.1.refs_0_), channel_id=1, source_target_pairs={{0,3},{1,0},{2,1},{3,2},{4,7},{5,4},{6,5},{7,6},{8,11},{9,8},{10,9... | collective-permute-start | bytes 196616 | tf_op jit(solution)/shard_map/ppermute | solution.py:501
  91.8 3.0 %collective-permute-done.11.refs_1_ = f32[64,256]{1,0:T(8,128)S(1)} collective-permute-done((f32[64,256]{1,0:T(8,128)S(1)}, f32[64,256]{1,0:T(8,128)S(1)}, u32[]{:S(2)}, u32[]{:S(2)}) %collective-permute-start.11) | collective-permute-done | bytes 65568 | tf_op jit(solution)/shard_map/ppermute | solution.py:501
  95.4 2.7 %collective-permute-start.16 = (f16[32,40,128]{2,1,0:T(8,128)(2,1)S(1)}, f16[32,40,128]{2,1,0:T(8,128)(2,1)S(1)}, u32[]{:S(2)}, u32[]{:S(2)}) collective-permute-start(f16[32,40,128]{2,1,0:T(8,128)(2,1)S(1)} %get-tuple-element.67), channel_id=1, source_target_pairs={{0,3},{1,0},{2,1},{3,2},{4,7},{5,4},{6,5},{7,6},{8,11},{9,8},{10,9... | collective-permute-start | bytes 983048 | tf_op jit(solution)/shard_map/ppermute | solution.py:501
  98.2 10.8 %invert_factor.1.inverse_ref = f32[256,256]{1,0:T(8,128)S(1)} custom-call(s32[1]{0:T(128)} %bitcast.1.spot_ref, f32[64,256]{1,0:T(8,128)S(1)} %gram_rows.1.refs_0_, f32[64,256]{1,0:T(8,128)S(1)} %collective-permute-done.11.refs_1_, f32[64,256]{1,0:T(8,128)S(1)} %collective-permute-done.12.refs_2_, f32[64,256]{1,0:T(8,128)S(1)} %collective-permute-done.13.refs_3_), custom_call_target="tpu_custom_call" | custom-call | flops 20000000000 | bytes 524288 | tf_op jit(solution)/shard_map/invert_factor/pallas_call | solution.py:140
  109.8 2.7 %moment_of.1.moment_ref = f32[256,256]{1,0:T(8,128)S(1)} custom-call(f32[32,40,128]{2,1,0:T(8,128)S(1)} %get-tuple-element.49.refs_0_, f32[32,40,128]{2,1,0:T(8,128)S(1)} %convert_element_type.53.refs_1_, f32[32,40,128]{2,1,0:T(8,128)S(1)} %convert_element_type.54.refs_2_, f32[32,40,128]{2,1,0:T(8,128)S(1)} %convert_element_type.55.refs_3_), custom_call_target="tpu_custom_call" | custom-call | flops 4000000000 | bytes 2359296 | tf_op jit(solution)/shard_map/moment_of/pallas_call | solution.py:163
  112.6 1.5 collective-permute-done.17.other_ref
  114.1 7.0 %project_half.1.basis_ref = bf16[2048,256]{1,0:T(8,128)(2,1)S(1)} custom-call(s32[1]{0:T(128)} %bitcast.1.spot_ref, f32[256,256]{1,0:T(8,128)S(1)} %invert_factor.1.inverse_ref, f32[256,256]{1,0:T(8,128)S(1)} %moment_of.1.moment_ref, f32[256,256]{1,0:T(8,128)S(1)} %collective-permute-done.17.other_ref, f32[32,40,128]{2,1,0:T(8,128)S(1)} %get-tuple-element.49.refs_0_, ...), custom_call_target="tpu_custom_call" | custom-call | flops 12000000000 | bytes 4194304 | tf_op jit(solution)/shard_map/project_half/pallas_call | solution.py:203
  121.6 2.8 %copy-done.1 = bf16[768,4096]{1,0:T(8,128)(2,1)S(1)} copy-done((bf16[768,4096]{1,0:T(8,128)(2,1)S(1)}, bf16[768,4096]{1,0:T(8,128)(2,1)}, u32[]{:S(2)}) %copy-start.1) | copy-done | bytes 6291480
  128.3 2.9 %place_rows.1 = bf16[64,48,256]{2,1,0:T(8,128)(2,1)} custom-call(s32[1,768]{1,0:T(1,128)S(1)} %broadcast_select_fusion.3.first_target, s32[1,768]{1,0:T(1,128)S(1)} %get-tuple-element.43.second_target, bf16[768,256]{1,0:T(8,128)(2,1)S(1)} %get-tuple-element.64.first_ref, bf16[768,256]{1,0:T(8,128)(2,1)S(1)} %get-tuple-element.63.second_ref), custom_call_target="tpu_custom_call" | custom-call | flops 1207959552 | bytes 3145728 | tf_op jit(solution)/shard_map/place_rows/pallas_call | solution.py:482
  131.2 9.6 %all-to-all-start.2 = ((bf16[128,24,256]{2,1,0:T(8,128)(2,1)}), bf16[128,24,256]{2,1,0:T(8,128)(2,1)S(1)}, u32[]{:S(2)}, u32[]{:S(2)}) async-start(bf16[128,24,256]{2,1,0:T(8,128)(2,1)} %bitcast.5), calls=%async_computation.2 | async-start | bytes 3145728 | tf_op jit(solution)/shard_map/all_to_all | solution.py:574
  141.7 40.8 %all-to-all-done.2 = bf16[128,24,256]{2,1,0:T(8,128)(2,1)S(1)} async-done(((bf16[128,24,256]{2,1,0:T(8,128)(2,1)}), bf16[128,24,256]{2,1,0:T(8,128)(2,1)S(1)}, u32[]{:S(2)}, u32[]{:S(2)}) %all-to-all-start.2) | async-done | bytes 1572896 | tf_op jit(solution)/shard_map/all_to_all | solution.py:574
  (68 shorter events, 19.2 us)
Async XLA Ops:
  0.6 3.9 %copy-start = (bf16[768,4096]{1,0:T(8,128)(2,1)S(1)}, bf16[768,4096]{1,0:T(8,128)(2,1)}, u32[]{:S(2)}) copy-start(bf16[768,4096]{1,0:T(8,128)(2,1)} %rows_ref.7) | copy-start | bytes 18874372
  0.6 1.4 copy-start.2
  9.9 3.4 %collective-permute-start.2 = (f32[256,640]{1,0:T(8,128)S(1)}, f32[256,640]{1,0:T(8,128)S(1)}, u32[]{:S(2)}, u32[]{:S(2)}) collective-permute-start(f32[256,640]{1,0:T(8,128)S(1)} %get-tuple-element.34), channel_id=1, source_target_pairs={{0,128},{128,0},{1,129},{129,1},{2,130},{130,2},{3,131},{131,3},{4... | collective-permute-start | bytes 1966088 | tf_op jit(solution)/shard_map/ppermute | solution.py:501
  12.8 4.5 %collective-permute-start.6 = (f32[256,640]{1,0:T(8,128)S(1)}, f32[256,640]{1,0:T(8,128)S(1)}, u32[]{:S(2)}, u32[]{:S(2)}) collective-permute-start(f32[256,640]{1,0:T(8,128)S(1)} %get-tuple-element.38), channel_id=1, source_target_pairs={{0,128},{128,0},{1,129},{129,1},{2,130},{130,2},{3,131},{131,3},{4... | collective-permute-start | bytes 1966088 | tf_op jit(solution)/shard_map/ppermute | solution.py:501
  13.3 16.7 %collective-permute-start.1 = (f32[256,640]{1,0:T(8,128)}, f32[256,640]{1,0:T(8,128)S(1)}, u32[]{:S(2)}, u32[]{:S(2)}) collective-permute-start(f32[256,640]{1,0:T(8,128)} %get-tuple-element.32), channel_id=1, source_target_pairs={{0,128},{128,0},{1,129},{129,1},{2,130},{130,2},{3,131},{131,3},{4... | collective-permute-start | bytes 1966088 | tf_op jit(solution)/shard_map/ppermute | solution.py:501
  14.2 10.7 %collective-permute-start.7 = (f32[128,640]{1,0:T(8,128)}, f32[128,640]{1,0:T(8,128)}, u32[]{:S(2)}, u32[]{:S(2)}) collective-permute-start(f32[128,640]{1,0:T(8,128)} %get-tuple-element.65), channel_id=1, source_target_pairs={{0,3},{1,0},{2,1},{3,2},{4,7},{5,4},{6,5},{7,6},{8,11},{9,8},{10,9... | collective-permute-start | bytes 983048 | tf_op jit(solution)/shard_map/ppermute | solution.py:501
  17.0 13.0 %collective-permute-start.3 = (f32[128,640]{1,0:T(8,128)}, f32[128,640]{1,0:T(8,128)}, u32[]{:S(2)}, u32[]{:S(2)}) collective-permute-start(f32[128,640]{1,0:T(8,128)} %get-tuple-element.66), channel_id=1, source_target_pairs={{0,1},{1,2},{2,3},{3,0},{4,5},{5,6},{6,7},{7,4},{8,9},{9,10},{10,1... | collective-permute-start | bytes 983048 | tf_op jit(solution)/shard_map/ppermute | solution.py:501
  17.0 24.7 %collective-permute-start = (f32[256,640]{1,0:T(8,128)}, f32[256,640]{1,0:T(8,128)}, u32[]{:S(2)}, u32[]{:S(2)}) collective-permute-start(f32[256,640]{1,0:T(8,128)} %get-tuple-element.30), channel_id=1, source_target_pairs={{0,128},{128,0},{1,129},{129,1},{2,130},{130,2},{3,131},{131,3},{4... | collective-permute-start | bytes 1966088 | tf_op jit(solution)/shard_map/ppermute | solution.py:501
  17.2 14.1 %collective-permute-start.10 = (s32[1,768]{1,0:T(1,128)S(1)}, s32[1,768]{1,0:T(1,128)S(1)}, u32[]{:S(2)}, u32[]{:S(2)}) collective-permute-start(s32[1,768]{1,0:T(1,128)S(1)} %get-tuple-element.41), channel_id=1, source_target_pairs={{0,128},{128,0},{1,129},{129,1},{2,130},{130,2},{3,131},{131,3},{4... | collective-permute-start | bytes 9224 | tf_op jit(solution)/shard_map/ppermute | solution.py:501
  26.2 10.4 %collective-permute-start.8 = (f16[256,512]{1,0:T(8,128)(2,1)S(1)}, f16[256,512]{1,0:T(8,128)(2,1)S(1)}, u32[]{:S(2)}, u32[]{:S(2)}) collective-permute-start(f16[256,512]{1,0:T(8,128)(2,1)S(1)} %convert_element_type.46), channel_id=1, source_target_pairs={{0,3},{1,0},{2,1},{3,2},{4,7},{5,4},{6,5},{7,6},{8,11},{9,8},{10,9... | collective-permute-start | bytes 786440 | tf_op jit(solution)/shard_map/ppermute | solution.py:501
  31.3 10.3 %collective-permute-start.4 = (f16[256,512]{1,0:T(8,128)(2,1)S(1)}, f16[256,512]{1,0:T(8,128)(2,1)S(1)}, u32[]{:S(2)}, u32[]{:S(2)}) collective-permute-start(f16[256,512]{1,0:T(8,128)(2,1)S(1)} %convert_element_type.44), channel_id=1, source_target_pairs={{0,1},{1,2},{2,3},{3,0},{4,5},{5,6},{6,7},{7,4},{8,9},{9,10},{10,1... | collective-permute-start | bytes 786440 | tf_op jit(solution)/shard_map/ppermute | solution.py:501
  31.5 10.2 %collective-permute-start.9 = (f32[256,128]{1,0:T(8,128)S(1)}, f32[256,128]{1,0:T(8,128)S(1)}, u32[]{:S(2)}, u32[]{:S(2)}) collective-permute-start(f32[256,128]{1,0:T(8,128)S(1)} %get-tuple-element.40), channel_id=1, source_target_pairs={{0,3},{1,0},{2,1},{3,2},{4,7},{5,4},{6,5},{7,6},{8,11},{9,8},{10,9... | collective-permute-start | bytes 393224 | tf_op jit(solution)/shard_map/ppermute | solution.py:501
  34.9 8.1 %collective-permute-start.5 = (f32[256,128]{1,0:T(8,128)S(1)}, f32[256,128]{1,0:T(8,128)S(1)}, u32[]{:S(2)}, u32[]{:S(2)}) collective-permute-start(f32[256,128]{1,0:T(8,128)S(1)} %get-tuple-element.36), channel_id=1, source_target_pairs={{0,1},{1,2},{2,3},{3,0},{4,5},{5,6},{6,7},{7,4},{8,9},{9,10},{10,1... | collective-permute-start | bytes 393224 | tf_op jit(solution)/shard_map/ppermute | solution.py:501
  88.5 6.3 %collective-permute-start.11 = (f32[64,256]{1,0:T(8,128)S(1)}, f32[64,256]{1,0:T(8,128)S(1)}, u32[]{:S(2)}, u32[]{:S(2)}) collective-permute-start(f32[64,256]{1,0:T(8,128)S(1)} %gram_rows.1.refs_0_), channel_id=1, source_target_pairs={{0,1},{1,2},{2,3},{3,0},{4,5},{5,6},{6,7},{7,4},{8,9},{9,10},{10,1... | collective-permute-start | bytes 196616 | tf_op jit(solution)/shard_map/ppermute | solution.py:501
  88.6 9.6 %collective-permute-start.12 = (f32[64,256]{1,0:T(8,128)S(1)}, f32[64,256]{1,0:T(8,128)S(1)}, u32[]{:S(2)}, u32[]{:S(2)}) collective-permute-start(f32[64,256]{1,0:T(8,128)S(1)} %gram_rows.1.refs_0_), channel_id=1, source_target_pairs={{0,2},{1,3},{2,0},{3,1},{4,6},{5,7},{6,4},{7,5},{8,10},{9,11},{10,... | collective-permute-start | bytes 196616 | tf_op jit(solution)/shard_map/ppermute | solution.py:501
  89.6 8.6 %collective-permute-start.13 = (f32[64,256]{1,0:T(8,128)S(1)}, f32[64,256]{1,0:T(8,128)S(1)}, u32[]{:S(2)}, u32[]{:S(2)}) collective-permute-start(f32[64,256]{1,0:T(8,128)S(1)} %gram_rows.1.refs_0_), channel_id=1, source_target_pairs={{0,3},{1,0},{2,1},{3,2},{4,7},{5,4},{6,5},{7,6},{8,11},{9,8},{10,9... | collective-permute-start | bytes 196616 | tf_op jit(solution)/shard_map/ppermute | solution.py:501
  94.9 14.1 %collective-permute-start.14 = (f16[32,40,128]{2,1,0:T(8,128)(2,1)S(1)}, f16[32,40,128]{2,1,0:T(8,128)(2,1)S(1)}, u32[]{:S(2)}, u32[]{:S(2)}) collective-permute-start(f16[32,40,128]{2,1,0:T(8,128)(2,1)S(1)} %get-tuple-element.67), channel_id=1, source_target_pairs={{0,1},{1,2},{2,3},{3,0},{4,5},{5,6},{6,7},{7,4},{8,9},{9,10},{10,1... | collective-permute-start | bytes 983048 | tf_op jit(solution)/shard_map/ppermute | solution.py:501
  94.9 14.1 %collective-permute-start.15 = (f16[32,40,128]{2,1,0:T(8,128)(2,1)S(1)}, f16[32,40,128]{2,1,0:T(8,128)(2,1)S(1)}, u32[]{:S(2)}, u32[]{:S(2)}) collective-permute-start(f16[32,40,128]{2,1,0:T(8,128)(2,1)S(1)} %get-tuple-element.67), channel_id=1, source_target_pairs={{0,2},{1,3},{2,0},{3,1},{4,6},{5,7},{6,4},{7,5},{8,10},{9,11},{10,... | collective-permute-start | bytes 983048 | tf_op jit(solution)/shard_map/ppermute | solution.py:501
  95.4 14.3 %collective-permute-start.16 = (f16[32,40,128]{2,1,0:T(8,128)(2,1)S(1)}, f16[32,40,128]{2,1,0:T(8,128)(2,1)S(1)}, u32[]{:S(2)}, u32[]{:S(2)}) collective-permute-start(f16[32,40,128]{2,1,0:T(8,128)(2,1)S(1)} %get-tuple-element.67), channel_id=1, source_target_pairs={{0,3},{1,0},{2,1},{3,2},{4,7},{5,4},{6,5},{7,6},{8,11},{9,8},{10,9... | collective-permute-start | bytes 983048 | tf_op jit(solution)/shard_map/ppermute | solution.py:501
  112.5 1.6 collective-permute-start.17
  121.1 4.3 %collective-permute-start.18 = (bf16[2048,256]{1,0:T(8,128)(2,1)S(1)}, bf16[2048,256]{1,0:T(8,128)(2,1)S(1)}, u32[]{:S(2)}, u32[]{:S(2)}) collective-permute-start(bf16[2048,256]{1,0:T(8,128)(2,1)S(1)} %project_half.1.basis_ref), channel_id=1, source_target_pairs={{0,128},{128,0},{1,129},{129,1},{2,130},{130,2},{3,131},{131,3},{4... | collective-permute-start | bytes 3145736 | tf_op jit(solution)/shard_map/ppermute | solution.py:501
  121.6 2.8 %copy-start.1 = (bf16[768,4096]{1,0:T(8,128)(2,1)S(1)}, bf16[768,4096]{1,0:T(8,128)(2,1)}, u32[]{:S(2)}) copy-start(bf16[768,4096]{1,0:T(8,128)(2,1)} %rows_ref.7) | copy-start | bytes 18874372
  126.3 1.8 collective-permute-start.19
  131.2 51.4 %all-to-all-start.2 = ((bf16[128,24,256]{2,1,0:T(8,128)(2,1)}), bf16[128,24,256]{2,1,0:T(8,128)(2,1)S(1)}, u32[]{:S(2)}, u32[]{:S(2)}) async-start(bf16[128,24,256]{2,1,0:T(8,128)(2,1)} %bitcast.5), calls=%async_computation.2 | async-start | bytes 3145728 | tf_op jit(solution)/shard_map/all_to_all | solution.py:574
  (1 other events, 0.9 us)

commit v8 on v7

--- a/solution.py
+++ b/solution.py
@@ -375,23 +375,24 @@
     )(parts)
 
 
-def product_kernel(core_ref, rows_ref, basis_ref, *refs):
+def product_kernel(own, core_ref, rows_ref, basis_ref, *refs):
+    place = core_ref[0] if own else 1 - core_ref[0]
     half, width = basis_ref.shape[0], 512
     total = None if len(refs) == 1 else refs[0][...]
     for step in range(half // width):
-        columns = pl.ds(pl.multiple_of(core_ref[0] * half + step * width, width), width)
+        columns = pl.ds(pl.multiple_of(place * half + step * width, width), width)
         basis = basis_ref[step * width : (step + 1) * width, :]
         term = jnp.dot(rows_ref[:, columns], basis, preferred_element_type=jnp.float32)
         total = term if total is None else total + term
     refs[-1][...] = total.astype(refs[-1].dtype)
 
 
-def product_of_half(half, embeddings, basis, begin, out_type):
+def product_of_half(core, own, embeddings, basis, begin, out_type):
     depth, dim = embeddings.shape
     rank = basis.shape[1]
     extra = [] if begin is None else [begin]
     return pl.pallas_call(
-        product_kernel,
+        functools.partial(product_kernel, own),
         in_specs=[pl.BlockSpec(memory_space=pltpu.SMEM)]
         + [pl.BlockSpec(memory_space=pltpu.VMEM)] * (2 + len(extra)),
         out_shape=jax.ShapeDtypeStruct((depth, rank), out_type),
@@ -400,7 +401,7 @@
             flops=depth * dim * rank, bytes_accessed=depth * dim + dim * rank, transcendentals=0
         ),
         name="product_of_half",
-    )(half, embeddings, basis, *extra)
+    )(core, embeddings, basis, *extra)
 
 
 def route_kernel(capacity, line, plane, ids_ref, map_ref, dest_ref, label_ref):
@@ -459,30 +460,33 @@
     )(list_ids.reshape(-1, 128), owner_map.reshape(-1, 128))
 
 
-def place_kernel(capacity, first_target, second_target, first_ref, second_ref, out_ref):
+def place_kernel(capacity, core_ref, own_target, other_target, own_ref, other_ref, out_ref):
     pairs, _, width = out_ref.shape
     count = pairs * 2 * capacity
     slots = pl.program_id(0) * count + lax.broadcasted_iota(
-        jnp.int32, (count, first_ref.shape[0]), 0
+        jnp.int32, (count, own_ref.shape[0]), 0
     )
     found = []
-    for target_ref, rows_ref in ((first_target, first_ref), (second_target, second_ref)):
+    for target_ref, rows_ref in ((own_target, own_ref), (other_target, other_ref)):
         onehot = (slots == target_ref[...]).astype(jnp.bfloat16)
         term = jnp.dot(onehot, rows_ref[...], preferred_element_type=jnp.float32)
         found.append(term.reshape(pairs, 2 * capacity, width))
-    a, b = found
+    first = core_ref[0] == 0
+    a = jnp.where(first, found[0], found[1])
+    b = jnp.where(first, found[1], found[0])
     out_ref[...] = jnp.concatenate(
         [a[:, :capacity], b[:, :capacity], a[:, capacity:], b[:, capacity:]], axis=1
     ).astype(jnp.bfloat16)
 
 
-def place_rows(targets, first, second, chips, capacity):
+def place_rows(core, targets, own, other, chips, capacity):
     pairs = 16
-    depth, width = first.shape
+    depth, width = own.shape
     return pl.pallas_call(
         functools.partial(place_kernel, capacity),
         grid=(chips // 2 // pairs,),
-        in_specs=[pl.BlockSpec((1, depth), lambda i: (0, 0))] * 2
+        in_specs=[pl.BlockSpec(memory_space=pltpu.SMEM)]
+        + [pl.BlockSpec((1, depth), lambda i: (0, 0))] * 2
         + [pl.BlockSpec((depth, width), lambda i: (0, 0))] * 2,
         out_specs=pl.BlockSpec((pairs, 4 * capacity, width), lambda i: (i, 0, 0)),
         out_shape=jax.ShapeDtypeStruct((chips // 2, 4 * capacity, width), jnp.bfloat16),
@@ -493,7 +497,7 @@
             transcendentals=0,
         ),
         name="place_rows",
-    )(*targets, first, second)
+    )(core, *targets, own, other)
 
 
 def shift(value, axis, step):
@@ -510,7 +514,6 @@
     dev_count = cores * chips
     core = lax.axis_index("narrow")
     spot = lax.axis_index("x").reshape(1)
-    own_half, other_half = core.reshape(1), (1 - core).reshape(1)
     piece, gram_piece = dim // dev_count, rank // chips
     seed_matrix = sketch_seed.astype(jnp.bfloat16)
     sketch = jnp.dot(embeddings, seed_matrix, preferred_element_type=jnp.float32).astype(
@@ -540,10 +543,7 @@
         owner = dest // capacity
         return jnp.where(owner // chips == core, (owner % chips) * capacity + dest % capacity, -1)
 
-    def by_core(own, other):
-        return jnp.where(core == 0, own, other), jnp.where(core == 0, other, own)
-
-    targets = by_core(target_of(dest_index), target_of(shift(dest_index, "narrow", 1)))
+    targets = target_of(dest_index), target_of(shift(dest_index, "narrow", 1))
 
     packed = line_total([*near, *arrived], plane, gram_piece)
     packed, targets = lax.optimization_barrier((packed, targets))
@@ -566,10 +566,10 @@
     moment = moment_of(cross_parts)
     basis = project_half(spot, inverse, moment, shift(moment, "narrow", 1), cross_parts)
     other_basis = shift(basis, "narrow", 1)
-    begun = product_of_half(own_half, embeddings, basis, None, jnp.float32)
-    reduced = product_of_half(other_half, embeddings, other_basis, begun, jnp.bfloat16)
-    rows = by_core(reduced, shift(reduced, "narrow", 1))
-    send_rows = place_rows(targets, *rows, chips, capacity)
+    begun = product_of_half(spots, True, embeddings, basis, None, jnp.float32)
+    reduced = product_of_half(spots, False, embeddings, other_basis, begun, jnp.bfloat16)
+    other = shift(reduced, "narrow", 1)
+    send_rows = place_rows(spots, targets, reduced, other, chips, capacity)
     send_rows = send_rows.reshape(chips, cores * capacity, rank)
     arrived = lax.all_to_all(send_rows, ("y", "z", "x"), 0, 0, tiled=True)
     arrived = arrived.reshape(chips, cores, capacity, rank).transpose(1, 0, 2, 3)

time: 185 us -> 178 us (0.962)
  local copies, waits for them, and re-layouts: 8.55 us -> 4.92 us
  Pallas kernels: 36.1 us -> 34.1 us
    unnamed x9 -> x7, local copies, waits for them, and re-layouts: 5.77 us -> 2.98 us
    pallas_call x2, Pallas kernels: 2.44 us -> 0.5 us  [join_chunk(): pl.pallas_call(functools.partial(join_kernel, side), out_shape=[jax.Shape...]
  transfers between devices with their start and end apart: 21 -> 21, of which waited for: 9 -> 10; matrix products, arithmetic and copies ran while one was open for 1% -> 1% of each run, Pallas kernels for 9% -> 8%
where the time goes in v8:
time: 178 us
  waiting for transfers between devices  63.3 us (36%)
  blocking collectives  42.3 us (24%)
  Pallas kernels  34.1 us (19%)
  starting transfers between devices  27.4 us (15%)
  local copies, waits for them, and re-layouts  4.92 us (3%)
  matrix products  4.03 us (2%)
    all_to_all x1, waiting for transfers between devices, local(): arrived = lax.all_to_all(send_rows, ('y', 'z', 'x'), 0, 0, tiled=True)  40.7 us
    all_to_all x1, blocking collectives, local(): packed = lax.all_to_all(packed.astype(jnp.float16), PLANE, 0, 0, tiled=True)  24.8 us
    ppermute x20, waiting for transfers between devices, shift(): lax.ppermute(value, axis, [(i, (i + step) % size) for i in range(size)])  22.6 us
    ppermute x20, starting transfers between devices, shift(): lax.ppermute(value, axis, [(i, (i + step) % size) for i in range(size)])  18.9 us
    all_to_all x1, blocking collectives, local(): packed = lax.all_to_all(packed, PLANE, 0, 0, tiled=True)  17.6 us
    pallas_call x1, Pallas kernels, invert_factor(): pl.pallas_call(invert_kernel, in_specs=[pl.BlockSpec(memory_space=pltpu.S...  10.8 us
    all_to_all x1, starting transfers between devices, local(): arrived = lax.all_to_all(send_rows, ('y', 'z', 'x'), 0, 0, tiled=True)  8.54 us
    pallas_call x1, Pallas kernels, project_half(): pl.pallas_call(whiten_kernel, in_specs=[pl.BlockSpec(memory_space=pltpu.S...  6.98 us
  transfers between devices with their start and end apart: 21, of which 10 were waited for; matrix products, arithmetic and copies ran while one was open for 1% of the time, Pallas kernels for 8%

profile of v8, /device:TPU:32, one launch (start us, length us, event | category | flops | bytes accessed | tf_op | source)
XLA Modules:
  0.0 177.9 jit_solution(7825013166900880946)
XLA Ops:
  3.0 1.6 route_rows.1
  4.5 4.0 %fusion.2.sketch_ref = bf16[768,256]{1,0:T(8,128)(2,1)S(1)} fusion(bf16[768,4096]{1,0:T(8,128)(2,1)S(1)} %copy-done, s32[4096,256]{1,0:T(8,128)} %param.5), kind=kOutput, calls=%fused_computation.2 | convolution fusion | flops 1611857920 | bytes 10878976 | tf_op jit(solution)/shard_map/dot_general | solution.py:519
  10.0 2.1 %cross_chunks.2 = (f32[256,640]{1,0:T(8,128)S(1)}, f32[256,640]{1,0:T(8,128)S(1)}, f32[256,640]{1,0:T(8,128)S(1)}, f32[256,640]{1,0:T(8,128)S(1)}, f32[256,640]{1,0:T(8,128)S(1)}, /*index=5*/f32[256,640]{1,0:T(8,128)S(1)}) custom-call(s32[3]{0:T(128)S(1)} %pad_add_fusion.spot_ref.core_ref, bf16[768,4096]{1,0:T(8,128)(2,1)S(1)} %copy-done, ...), custom_call_target="tpu_custom_call" | custom-call | flops 1207959552 | bytes 3000000 | tf_op jit(solution)/shard_map/cross_chunks/pallas_call | solution.py:244
  13.0 2.8 %collective-permute-start.7 = (f32[128,640]{1,0:T(8,128)S(1)}, f32[128,640]{1,0:T(8,128)S(1)}, u32[]{:S(2)}, u32[]{:S(2)}) collective-permute-start(f32[128,640]{1,0:T(8,128)S(1)} %get-tuple-element.60), channel_id=1, source_target_pairs={{0,3},{1,0},{2,1},{3,2},{4,7},{5,4},{6,5},{7,6},{8,11},{9,8},{10,9... | collective-permute-start | bytes 983048 | tf_op jit(solution)/shard_map/ppermute | solution.py:505
  16.3 7.0 %collective-permute-done.7.extra_ref = f32[128,640]{1,0:T(8,128)S(1)} collective-permute-done((f32[128,640]{1,0:T(8,128)S(1)}, f32[128,640]{1,0:T(8,128)S(1)}, u32[]{:S(2)}, u32[]{:S(2)}) %collective-permute-start.7) | collective-permute-done | bytes 327712 | tf_op jit(solution)/shard_map/ppermute | solution.py:505
  23.7 3.8 %collective-permute-start.8 = (f16[256,512]{1,0:T(8,128)(2,1)S(1)}, f16[256,512]{1,0:T(8,128)(2,1)S(1)}, u32[]{:S(2)}, u32[]{:S(2)}) collective-permute-start(f16[256,512]{1,0:T(8,128)(2,1)S(1)} %convert_element_type.46), channel_id=1, source_target_pairs={{0,3},{1,0},{2,1},{3,2},{4,7},{5,4},{6,5},{7,6},{8,11},{9,8},{10,9... | collective-permute-start | bytes 786440 | tf_op jit(solution)/shard_map/ppermute | solution.py:505
  27.9 3.5 %collective-permute-start.9 = (f32[256,128]{1,0:T(8,128)S(1)}, f32[256,128]{1,0:T(8,128)S(1)}, u32[]{:S(2)}, u32[]{:S(2)}) collective-permute-start(f32[256,128]{1,0:T(8,128)S(1)} %get-tuple-element.40), channel_id=1, source_target_pairs={{0,3},{1,0},{2,1},{3,2},{4,7},{5,4},{6,5},{7,6},{8,11},{9,8},{10,9... | collective-permute-start | bytes 393224 | tf_op jit(solution)/shard_map/ppermute | solution.py:505
  31.4 2.7 %collective-permute-done.8 = f16[256,512]{1,0:T(8,128)(2,1)S(1)} collective-permute-done((f16[256,512]{1,0:T(8,128)(2,1)S(1)}, f16[256,512]{1,0:T(8,128)(2,1)S(1)}, u32[]{:S(2)}, u32[]{:S(2)}) %collective-permute-start.8) | collective-permute-done | bytes 262176 | tf_op jit(solution)/shard_map/ppermute | solution.py:505
  34.2 3.8 %collective-permute-done.4 = f16[256,512]{1,0:T(8,128)(2,1)S(1)} collective-permute-done((f16[256,512]{1,0:T(8,128)(2,1)S(1)}, f16[256,512]{1,0:T(8,128)(2,1)S(1)}, u32[]{:S(2)}, u32[]{:S(2)}) %collective-permute-start.4) | collective-permute-done | bytes 262176 | tf_op jit(solution)/shard_map/ppermute | solution.py:505
  40.1 24.8 %all_to_all.15 = f16[32,48,128]{2,1,0:T(8,128)(2,1)S(1)} all-to-all(f16[32,48,128]{2,1,0:T(8,128)(2,1)S(1)} %convert_element_type.48), channel_id=1, replica_groups=mesh['narrow'=2,'y'=4,'z'=8,'x'=4] {'y','z'}, dimensions={0} | all-to-all | bytes 786432 | tf_op jit(solution)/shard_map/all_to_all | solution.py:550
  65.7 17.6 %all_to_all.16 = f16[32,48,128]{2,1,0:T(8,128)(2,1)S(1)} all-to-all(f16[32,48,128]{2,1,0:T(8,128)(2,1)S(1)} %broadcast_in_dim.5), channel_id=1, replica_groups=mesh['narrow'=2,'y'=4,'z'=8,'x'=4] {'y','z'}, dimensions={0} | all-to-all | bytes 786432 | tf_op jit(solution)/shard_map/all_to_all | solution.py:554
  83.7 1.8 collective-permute-start.12
  86.9 2.9 %collective-permute-done.11.refs_1_ = f32[64,256]{1,0:T(8,128)S(1)} collective-permute-done((f32[64,256]{1,0:T(8,128)S(1)}, f32[64,256]{1,0:T(8,128)S(1)}, u32[]{:S(2)}, u32[]{:S(2)}) %collective-permute-start.11) | collective-permute-done | bytes 65568 | tf_op jit(solution)/shard_map/ppermute | solution.py:505
  90.5 2.7 %collective-permute-start.16 = (f16[32,40,128]{2,1,0:T(8,128)(2,1)S(1)}, f16[32,40,128]{2,1,0:T(8,128)(2,1)S(1)}, u32[]{:S(2)}, u32[]{:S(2)}) collective-permute-start(f16[32,40,128]{2,1,0:T(8,128)(2,1)S(1)} %get-tuple-element.62), channel_id=1, source_target_pairs={{0,3},{1,0},{2,1},{3,2},{4,7},{5,4},{6,5},{7,6},{8,11},{9,8},{10,9... | collective-permute-start | bytes 983048 | tf_op jit(solution)/shard_map/ppermute | solution.py:505
  93.3 10.8 %invert_factor.1.inverse_ref = f32[256,256]{1,0:T(8,128)S(1)} custom-call(s32[1]{0:T(128)} %bitcast.1.spot_ref, f32[64,256]{1,0:T(8,128)S(1)} %gram_rows.1.refs_0_, f32[64,256]{1,0:T(8,128)S(1)} %collective-permute-done.11.refs_1_, f32[64,256]{1,0:T(8,128)S(1)} %collective-permute-done.12.refs_2_, f32[64,256]{1,0:T(8,128)S(1)} %collective-permute-done.13.refs_3_), custom_call_target="tpu_custom_call" | custom-call | flops 20000000000 | bytes 524288 | tf_op jit(solution)/shard_map/invert_factor/pallas_call | solution.py:140
  104.9 2.7 %moment_of.1.moment_ref = f32[256,256]{1,0:T(8,128)S(1)} custom-call(f32[32,40,128]{2,1,0:T(8,128)S(1)} %get-tuple-element.49.refs_0_, f32[32,40,128]{2,1,0:T(8,128)S(1)} %convert_element_type.53.refs_1_, f32[32,40,128]{2,1,0:T(8,128)S(1)} %convert_element_type.54.refs_2_, f32[32,40,128]{2,1,0:T(8,128)S(1)} %convert_element_type.55.refs_3_), custom_call_target="tpu_custom_call" | custom-call | flops 4000000000 | bytes 2359296 | tf_op jit(solution)/shard_map/moment_of/pallas_call | solution.py:163
  107.7 1.5 collective-permute-done.17.other_ref
  109.2 7.0 %project_half.1.basis_ref = bf16[2048,256]{1,0:T(8,128)(2,1)S(1)} custom-call(s32[1]{0:T(128)} %bitcast.1.spot_ref, f32[256,256]{1,0:T(8,128)S(1)} %invert_factor.1.inverse_ref, f32[256,256]{1,0:T(8,128)S(1)} %moment_of.1.moment_ref, f32[256,256]{1,0:T(8,128)S(1)} %collective-permute-done.17.other_ref, f32[32,40,128]{2,1,0:T(8,128)S(1)} %get-tuple-element.49.refs_0_, ...), custom_call_target="tpu_custom_call" | custom-call | flops 12000000000 | bytes 4194304 | tf_op jit(solution)/shard_map/project_half/pallas_call | solution.py:203
  116.7 1.5 product_of_half.2.refs_0_
  119.2 1.5 product_of_half.3.own_ref
  121.0 1.6 collective-permute-done.19.other_ref
  122.6 3.5 %place_rows.1 = bf16[64,48,256]{2,1,0:T(8,128)(2,1)} custom-call(s32[3]{0:T(128)S(1)} %pad_add_fusion.spot_ref.core_ref, s32[1,768]{1,0:T(1,128)S(1)} %compare_select_fusion.1.own_target, s32[1,768]{1,0:T(1,128)S(1)} %compare_select_fusion.other_target, bf16[768,256]{1,0:T(8,128)(2,1)S(1)} %product_of_half.3.own_ref, ...), custom_call_target="tpu_custom_call" | custom-call | flops 1207959552 | bytes 3145728 | tf_op jit(solution)/shard_map/place_rows/pallas_call | solution.py:485
  126.1 8.5 %all-to-all-start.2 = ((bf16[128,24,256]{2,1,0:T(8,128)(2,1)}), bf16[128,24,256]{2,1,0:T(8,128)(2,1)S(1)}, u32[]{:S(2)}, u32[]{:S(2)}) async-start(bf16[128,24,256]{2,1,0:T(8,128)(2,1)} %bitcast.4), calls=%async_computation.2 | async-start | bytes 3145728 | tf_op jit(solution)/shard_map/all_to_all | solution.py:574
  135.6 40.7 %all-to-all-done.2 = bf16[128,24,256]{2,1,0:T(8,128)(2,1)S(1)} async-done(((bf16[128,24,256]{2,1,0:T(8,128)(2,1)}), bf16[128,24,256]{2,1,0:T(8,128)(2,1)S(1)}, u32[]{:S(2)}, u32[]{:S(2)}) %all-to-all-start.2) | async-done | bytes 1572896 | tf_op jit(solution)/shard_map/all_to_all | solution.py:574
  (65 shorter events, 16.5 us)
Async XLA Ops:
  0.6 3.9 %copy-start = (bf16[768,4096]{1,0:T(8,128)(2,1)S(1)}, bf16[768,4096]{1,0:T(8,128)(2,1)}, u32[]{:S(2)}) copy-start(bf16[768,4096]{1,0:T(8,128)(2,1)} %rows_ref.7) | copy-start | bytes 18874372
  0.6 1.4 copy-start.1
  2.0 0.9 copy-start.2
  9.9 2.9 %collective-permute-start.2 = (f32[256,640]{1,0:T(8,128)S(1)}, f32[256,640]{1,0:T(8,128)S(1)}, u32[]{:S(2)}, u32[]{:S(2)}) collective-permute-start(f32[256,640]{1,0:T(8,128)S(1)} %get-tuple-element.34), channel_id=1, source_target_pairs={{0,128},{128,0},{1,129},{129,1},{2,130},{130,2},{3,131},{131,3},{4... | collective-permute-start | bytes 1966088 | tf_op jit(solution)/shard_map/ppermute | solution.py:505
  12.1 3.8 %collective-permute-start.6 = (f32[256,640]{1,0:T(8,128)S(1)}, f32[256,640]{1,0:T(8,128)S(1)}, u32[]{:S(2)}, u32[]{:S(2)}) collective-permute-start(f32[256,640]{1,0:T(8,128)S(1)} %get-tuple-element.38), channel_id=1, source_target_pairs={{0,128},{128,0},{1,129},{129,1},{2,130},{130,2},{3,131},{131,3},{4... | collective-permute-start | bytes 1966088 | tf_op jit(solution)/shard_map/ppermute | solution.py:505
  12.7 14.7 %collective-permute-start.1 = (f32[256,640]{1,0:T(8,128)S(1)}, f32[256,640]{1,0:T(8,128)S(1)}, u32[]{:S(2)}, u32[]{:S(2)}) collective-permute-start(f32[256,640]{1,0:T(8,128)S(1)} %get-tuple-element.32), channel_id=1, source_target_pairs={{0,128},{128,0},{1,129},{129,1},{2,130},{130,2},{3,131},{131,3},{4... | collective-permute-start | bytes 1966088 | tf_op jit(solution)/shard_map/ppermute | solution.py:505
  13.0 10.4 %collective-permute-start.7 = (f32[128,640]{1,0:T(8,128)S(1)}, f32[128,640]{1,0:T(8,128)S(1)}, u32[]{:S(2)}, u32[]{:S(2)}) collective-permute-start(f32[128,640]{1,0:T(8,128)S(1)} %get-tuple-element.60), channel_id=1, source_target_pairs={{0,3},{1,0},{2,1},{3,2},{4,7},{5,4},{6,5},{7,6},{8,11},{9,8},{10,9... | collective-permute-start | bytes 983048 | tf_op jit(solution)/shard_map/ppermute | solution.py:505
  15.8 11.6 %collective-permute-start.3 = (f32[128,640]{1,0:T(8,128)S(1)}, f32[128,640]{1,0:T(8,128)S(1)}, u32[]{:S(2)}, u32[]{:S(2)}) collective-permute-start(f32[128,640]{1,0:T(8,128)S(1)} %get-tuple-element.61), channel_id=1, source_target_pairs={{0,1},{1,2},{2,3},{3,0},{4,5},{5,6},{6,7},{7,4},{8,9},{9,10},{10,1... | collective-permute-start | bytes 983048 | tf_op jit(solution)/shard_map/ppermute | solution.py:505
  15.8 22.3 %collective-permute-start = (f32[256,640]{1,0:T(8,128)S(1)}, f32[256,640]{1,0:T(8,128)S(1)}, u32[]{:S(2)}, u32[]{:S(2)}) collective-permute-start(f32[256,640]{1,0:T(8,128)S(1)} %get-tuple-element.30), channel_id=1, source_target_pairs={{0,128},{128,0},{1,129},{129,1},{2,130},{130,2},{3,131},{131,3},{4... | collective-permute-start | bytes 1966088 | tf_op jit(solution)/shard_map/ppermute | solution.py:505
  16.0 15.4 %collective-permute-start.10 = (s32[1,768]{1,0:T(1,128)S(1)}, s32[1,768]{1,0:T(1,128)S(1)}, u32[]{:S(2)}, u32[]{:S(2)}) collective-permute-start(s32[1,768]{1,0:T(1,128)S(1)} %get-tuple-element.41), channel_id=1, source_target_pairs={{0,128},{128,0},{1,129},{129,1},{2,130},{130,2},{3,131},{131,3},{4... | collective-permute-start | bytes 9224 | tf_op jit(solution)/shard_map/ppermute | solution.py:505
  23.7 10.5 %collective-permute-start.8 = (f16[256,512]{1,0:T(8,128)(2,1)S(1)}, f16[256,512]{1,0:T(8,128)(2,1)S(1)}, u32[]{:S(2)}, u32[]{:S(2)}) collective-permute-start(f16[256,512]{1,0:T(8,128)(2,1)S(1)} %convert_element_type.46), channel_id=1, source_target_pairs={{0,3},{1,0},{2,1},{3,2},{4,7},{5,4},{6,5},{7,6},{8,11},{9,8},{10,9... | collective-permute-start | bytes 786440 | tf_op jit(solution)/shard_map/ppermute | solution.py:505
  27.7 10.3 %collective-permute-start.4 = (f16[256,512]{1,0:T(8,128)(2,1)S(1)}, f16[256,512]{1,0:T(8,128)(2,1)S(1)}, u32[]{:S(2)}, u32[]{:S(2)}) collective-permute-start(f16[256,512]{1,0:T(8,128)(2,1)S(1)} %convert_element_type.44), channel_id=1, source_target_pairs={{0,1},{1,2},{2,3},{3,0},{4,5},{5,6},{6,7},{7,4},{8,9},{9,10},{10,1... | collective-permute-start | bytes 786440 | tf_op jit(solution)/shard_map/ppermute | solution.py:505
  27.9 10.2 %collective-permute-start.9 = (f32[256,128]{1,0:T(8,128)S(1)}, f32[256,128]{1,0:T(8,128)S(1)}, u32[]{:S(2)}, u32[]{:S(2)}) collective-permute-start(f32[256,128]{1,0:T(8,128)S(1)} %get-tuple-element.40), channel_id=1, source_target_pairs={{0,3},{1,0},{2,1},{3,2},{4,7},{5,4},{6,5},{7,6},{8,11},{9,8},{10,9... | collective-permute-start | bytes 393224 | tf_op jit(solution)/shard_map/ppermute | solution.py:505
  31.4 8.0 %collective-permute-start.5 = (f32[256,128]{1,0:T(8,128)S(1)}, f32[256,128]{1,0:T(8,128)S(1)}, u32[]{:S(2)}, u32[]{:S(2)}) collective-permute-start(f32[256,128]{1,0:T(8,128)S(1)} %get-tuple-element.36), channel_id=1, source_target_pairs={{0,1},{1,2},{2,3},{3,0},{4,5},{5,6},{6,7},{7,4},{8,9},{9,10},{10,1... | collective-permute-start | bytes 393224 | tf_op jit(solution)/shard_map/ppermute | solution.py:505
  83.6 6.2 %collective-permute-start.11 = (f32[64,256]{1,0:T(8,128)S(1)}, f32[64,256]{1,0:T(8,128)S(1)}, u32[]{:S(2)}, u32[]{:S(2)}) collective-permute-start(f32[64,256]{1,0:T(8,128)S(1)} %gram_rows.1.refs_0_), channel_id=1, source_target_pairs={{0,1},{1,2},{2,3},{3,0},{4,5},{5,6},{6,7},{7,4},{8,9},{9,10},{10,1... | collective-permute-start | bytes 196616 | tf_op jit(solution)/shard_map/ppermute | solution.py:505
  83.7 9.6 %collective-permute-start.12 = (f32[64,256]{1,0:T(8,128)S(1)}, f32[64,256]{1,0:T(8,128)S(1)}, u32[]{:S(2)}, u32[]{:S(2)}) collective-permute-start(f32[64,256]{1,0:T(8,128)S(1)} %gram_rows.1.refs_0_), channel_id=1, source_target_pairs={{0,2},{1,3},{2,0},{3,1},{4,6},{5,7},{6,4},{7,5},{8,10},{9,11},{10,... | collective-permute-start | bytes 196616 | tf_op jit(solution)/shard_map/ppermute | solution.py:505
  85.5 7.8 %collective-permute-start.13 = (f32[64,256]{1,0:T(8,128)S(1)}, f32[64,256]{1,0:T(8,128)S(1)}, u32[]{:S(2)}, u32[]{:S(2)}) collective-permute-start(f32[64,256]{1,0:T(8,128)S(1)} %gram_rows.1.refs_0_), channel_id=1, source_target_pairs={{0,3},{1,0},{2,1},{3,2},{4,7},{5,4},{6,5},{7,6},{8,11},{9,8},{10,9... | collective-permute-start | bytes 196616 | tf_op jit(solution)/shard_map/ppermute | solution.py:505
  90.0 14.1 %collective-permute-start.14 = (f16[32,40,128]{2,1,0:T(8,128)(2,1)S(1)}, f16[32,40,128]{2,1,0:T(8,128)(2,1)S(1)}, u32[]{:S(2)}, u32[]{:S(2)}) collective-permute-start(f16[32,40,128]{2,1,0:T(8,128)(2,1)S(1)} %get-tuple-element.62), channel_id=1, source_target_pairs={{0,1},{1,2},{2,3},{3,0},{4,5},{5,6},{6,7},{7,4},{8,9},{9,10},{10,1... | collective-permute-start | bytes 983048 | tf_op jit(solution)/shard_map/ppermute | solution.py:505
  90.0 14.1 %collective-permute-start.15 = (f16[32,40,128]{2,1,0:T(8,128)(2,1)S(1)}, f16[32,40,128]{2,1,0:T(8,128)(2,1)S(1)}, u32[]{:S(2)}, u32[]{:S(2)}) collective-permute-start(f16[32,40,128]{2,1,0:T(8,128)(2,1)S(1)} %get-tuple-element.62), channel_id=1, source_target_pairs={{0,2},{1,3},{2,0},{3,1},{4,6},{5,7},{6,4},{7,5},{8,10},{9,11},{10,... | collective-permute-start | bytes 983048 | tf_op jit(solution)/shard_map/ppermute | solution.py:505
  90.5 14.3 %collective-permute-start.16 = (f16[32,40,128]{2,1,0:T(8,128)(2,1)S(1)}, f16[32,40,128]{2,1,0:T(8,128)(2,1)S(1)}, u32[]{:S(2)}, u32[]{:S(2)}) collective-permute-start(f16[32,40,128]{2,1,0:T(8,128)(2,1)S(1)} %get-tuple-element.62), channel_id=1, source_target_pairs={{0,3},{1,0},{2,1},{3,2},{4,7},{5,4},{6,5},{7,6},{8,11},{9,8},{10,9... | collective-permute-start | bytes 983048 | tf_op jit(solution)/shard_map/ppermute | solution.py:505
  107.6 1.6 collective-permute-start.17
  116.2 3.0 %collective-permute-start.18 = (bf16[2048,256]{1,0:T(8,128)(2,1)S(1)}, bf16[2048,256]{1,0:T(8,128)(2,1)S(1)}, u32[]{:S(2)}, u32[]{:S(2)}) collective-permute-start(bf16[2048,256]{1,0:T(8,128)(2,1)S(1)} %project_half.1.basis_ref), channel_id=1, source_target_pairs={{0,128},{128,0},{1,129},{129,1},{2,130},{130,2},{3,131},{131,3},{4... | collective-permute-start | bytes 3145736 | tf_op jit(solution)/shard_map/ppermute | solution.py:505
  120.8 1.8 %collective-permute-start.19 = (bf16[768,256]{1,0:T(8,128)(2,1)S(1)}, bf16[768,256]{1,0:T(8,128)(2,1)S(1)}, u32[]{:S(2)}, u32[]{:S(2)}) collective-permute-start(bf16[768,256]{1,0:T(8,128)(2,1)S(1)} %product_of_half.3.own_ref), channel_id=1, source_target_pairs={{0,128},{128,0},{1,129},{129,1},{2,130},{130,2},{3,131},{131,3},{4... | collective-permute-start | bytes 1179656 | tf_op jit(solution)/shard_map/ppermute | solution.py:505
  126.1 50.2 %all-to-all-start.2 = ((bf16[128,24,256]{2,1,0:T(8,128)(2,1)}), bf16[128,24,256]{2,1,0:T(8,128)(2,1)S(1)}, u32[]{:S(2)}, u32[]{:S(2)}) async-start(bf16[128,24,256]{2,1,0:T(8,128)(2,1)} %bitcast.4), calls=%async_computation.2 | async-start | bytes 3145728 | tf_op jit(solution)/shard_map/all_to_all | solution.py:574

commit v9 on v8

--- a/solution.py
+++ b/solution.py
@@ -553,8 +553,8 @@
     packed = jnp.broadcast_to(packed.astype(jnp.float16)[None], (plane,) + packed.shape)
     packed = lax.all_to_all(packed, PLANE, 0, 0, tiled=True)
     gram_line = gram_rows(packed[:, 2 * piece :].astype(jnp.float32), gram_piece)
+    packed, gram_line = lax.optimization_barrier((packed, gram_line))
     gram_parts = [gram_line] + [shift(gram_line, "x", step) for step in range(1, line)]
-    packed, gram_parts[1] = lax.optimization_barrier((packed, gram_parts[1]))
     cross_line = packed[:, : 2 * piece + 8]
     cross_parts = [cross_line] + [shift(cross_line, "x", step) for step in range(1, line)]
     cross_parts = [part.astype(jnp.float32) for part in cross_parts]

time: 178 us -> 178 us (level)
  waiting for transfers between devices: 63.3 us -> 60.3 us
  starting transfers between devices: 27.4 us -> 30.1 us
    ppermute x20, waiting for transfers between devices: 22.6 us -> 19.5 us  [shift(): lax.ppermute(value, axis, [(i, (i + step) % size) for i in range(size)])]
    ppermute x20, starting transfers between devices: 18.9 us -> 20.7 us  [shift(): lax.ppermute(value, axis, [(i, (i + step) % size) for i in range(size)])]
  transfers between devices with their start and end apart: 21 -> 21, of which waited for: 10 -> 9; matrix products, arithmetic and copies ran while one was open for 1% -> 1% of each run, Pallas kernels for 8% -> 8%
where the time goes in v9:
time: 178 us; the launch traced here: 177 us
  waiting for transfers between devices  60.3 us (34%)
  blocking collectives  42.3 us (24%)
  Pallas kernels  34.1 us (19%)
  starting transfers between devices  30.1 us (17%)
  local copies, waits for them, and re-layouts  4.92 us (3%)
  matrix products  4.03 us (2%)
    all_to_all x1, waiting for transfers between devices, local(): arrived = lax.all_to_all(send_rows, ('y', 'z', 'x'), 0, 0, tiled=True)  40.7 us
    all_to_all x1, blocking collectives, local(): packed = lax.all_to_all(packed.astype(jnp.float16), PLANE, 0, 0, tiled=True)  24.8 us
    ppermute x20, starting transfers between devices, shift(): lax.ppermute(value, axis, [(i, (i + step) % size) for i in range(size)])  20.7 us
    ppermute x20, waiting for transfers between devices, shift(): lax.ppermute(value, axis, [(i, (i + step) % size) for i in range(size)])  19.5 us
    all_to_all x1, blocking collectives, local(): packed = lax.all_to_all(packed, PLANE, 0, 0, tiled=True)  17.6 us
    pallas_call x1, Pallas kernels, invert_factor(): pl.pallas_call(invert_kernel, in_specs=[pl.BlockSpec(memory_space=pltpu.S...  10.8 us
    all_to_all x1, starting transfers between devices, local(): arrived = lax.all_to_all(send_rows, ('y', 'z', 'x'), 0, 0, tiled=True)  9.4 us
    pallas_call x1, Pallas kernels, project_half(): pl.pallas_call(whiten_kernel, in_specs=[pl.BlockSpec(memory_space=pltpu.S...  6.99 us
  transfers between devices with their start and end apart: 21, of which 9 were waited for; matrix products, arithmetic and copies ran while one was open for 1% of the time, Pallas kernels for 8%

profile of v9, /device:TPU:32, one launch (start us, length us, event | category | flops | bytes accessed | tf_op | source)
XLA Modules:
  0.0 177.5 jit_solution(10867781784581620631)
XLA Ops:
  3.0 1.6 route_rows.1
  4.5 4.0 %fusion.2.sketch_ref = bf16[768,256]{1,0:T(8,128)(2,1)S(1)} fusion(bf16[768,4096]{1,0:T(8,128)(2,1)S(1)} %copy-done, s32[4096,256]{1,0:T(8,128)} %param.5), kind=kOutput, calls=%fused_computation.2 | convolution fusion | flops 1611857920 | bytes 10878976 | tf_op jit(solution)/shard_map/dot_general | solution.py:519
  10.0 2.1 %cross_chunks.2 = (f32[256,640]{1,0:T(8,128)S(1)}, f32[256,640]{1,0:T(8,128)S(1)}, f32[256,640]{1,0:T(8,128)S(1)}, f32[256,640]{1,0:T(8,128)S(1)}, f32[256,640]{1,0:T(8,128)S(1)}, /*index=5*/f32[256,640]{1,0:T(8,128)S(1)}) custom-call(s32[3]{0:T(128)S(1)} %pad_add_fusion.spot_ref.core_ref, bf16[768,4096]{1,0:T(8,128)(2,1)S(1)} %copy-done, ...), custom_call_target="tpu_custom_call" | custom-call | flops 1207959552 | bytes 3000000 | tf_op jit(solution)/shard_map/cross_chunks/pallas_call | solution.py:244
  13.0 2.8 %collective-permute-start.7 = (f32[128,640]{1,0:T(8,128)S(1)}, f32[128,640]{1,0:T(8,128)S(1)}, u32[]{:S(2)}, u32[]{:S(2)}) collective-permute-start(f32[128,640]{1,0:T(8,128)S(1)} %get-tuple-element.60), channel_id=1, source_target_pairs={{0,3},{1,0},{2,1},{3,2},{4,7},{5,4},{6,5},{7,6},{8,11},{9,8},{10,9... | collective-permute-start | bytes 983048 | tf_op jit(solution)/shard_map/ppermute | solution.py:505
  16.3 7.0 %collective-permute-done.7.extra_ref = f32[128,640]{1,0:T(8,128)S(1)} collective-permute-done((f32[128,640]{1,0:T(8,128)S(1)}, f32[128,640]{1,0:T(8,128)S(1)}, u32[]{:S(2)}, u32[]{:S(2)}) %collective-permute-start.7) | collective-permute-done | bytes 327712 | tf_op jit(solution)/shard_map/ppermute | solution.py:505
  23.7 3.8 %collective-permute-start.8 = (f16[256,512]{1,0:T(8,128)(2,1)S(1)}, f16[256,512]{1,0:T(8,128)(2,1)S(1)}, u32[]{:S(2)}, u32[]{:S(2)}) collective-permute-start(f16[256,512]{1,0:T(8,128)(2,1)S(1)} %convert_element_type.46), channel_id=1, source_target_pairs={{0,3},{1,0},{2,1},{3,2},{4,7},{5,4},{6,5},{7,6},{8,11},{9,8},{10,9... | collective-permute-start | bytes 786440 | tf_op jit(solution)/shard_map/ppermute | solution.py:505
  27.9 3.5 %collective-permute-start.9 = (f32[256,128]{1,0:T(8,128)S(1)}, f32[256,128]{1,0:T(8,128)S(1)}, u32[]{:S(2)}, u32[]{:S(2)}) collective-permute-start(f32[256,128]{1,0:T(8,128)S(1)} %get-tuple-element.40), channel_id=1, source_target_pairs={{0,3},{1,0},{2,1},{3,2},{4,7},{5,4},{6,5},{7,6},{8,11},{9,8},{10,9... | collective-permute-start | bytes 393224 | tf_op jit(solution)/shard_map/ppermute | solution.py:505
  31.4 2.7 %collective-permute-done.8 = f16[256,512]{1,0:T(8,128)(2,1)S(1)} collective-permute-done((f16[256,512]{1,0:T(8,128)(2,1)S(1)}, f16[256,512]{1,0:T(8,128)(2,1)S(1)}, u32[]{:S(2)}, u32[]{:S(2)}) %collective-permute-start.8) | collective-permute-done | bytes 262176 | tf_op jit(solution)/shard_map/ppermute | solution.py:505
  34.2 3.8 %collective-permute-done.4 = f16[256,512]{1,0:T(8,128)(2,1)S(1)} collective-permute-done((f16[256,512]{1,0:T(8,128)(2,1)S(1)}, f16[256,512]{1,0:T(8,128)(2,1)S(1)}, u32[]{:S(2)}, u32[]{:S(2)}) %collective-permute-start.4) | collective-permute-done | bytes 262176 | tf_op jit(solution)/shard_map/ppermute | solution.py:505
  40.1 24.8 %all_to_all.15 = f16[32,48,128]{2,1,0:T(8,128)(2,1)S(1)} all-to-all(f16[32,48,128]{2,1,0:T(8,128)(2,1)S(1)} %convert_element_type.48), channel_id=1, replica_groups=mesh['narrow'=2,'y'=4,'z'=8,'x'=4] {'y','z'}, dimensions={0} | all-to-all | bytes 786432 | tf_op jit(solution)/shard_map/all_to_all | solution.py:550
  65.7 17.6 %all_to_all.16 = f16[32,48,128]{2,1,0:T(8,128)(2,1)S(1)} all-to-all(f16[32,48,128]{2,1,0:T(8,128)(2,1)S(1)} %broadcast_in_dim.5), channel_id=1, replica_groups=mesh['narrow'=2,'y'=4,'z'=8,'x'=4] {'y','z'}, dimensions={0} | all-to-all | bytes 786432 | tf_op jit(solution)/shard_map/all_to_all | solution.py:554
  83.7 1.8 collective-permute-start.12
  88.0 2.2 %collective-permute-start.15 = (f16[32,40,128]{2,1,0:T(8,128)(2,1)S(1)}, f16[32,40,128]{2,1,0:T(8,128)(2,1)S(1)}, u32[]{:S(2)}, u32[]{:S(2)}) collective-permute-start(f16[32,40,128]{2,1,0:T(8,128)(2,1)S(1)} %get-tuple-element.62), channel_id=1, source_target_pairs={{0,2},{1,3},{2,0},{3,1},{4,6},{5,7},{6,4},{7,5},{8,10},{9,11},{10,... | collective-permute-start | bytes 983048 | tf_op jit(solution)/shard_map/ppermute | solution.py:505
  90.7 2.0 %collective-permute-start.16 = (f16[32,40,128]{2,1,0:T(8,128)(2,1)S(1)}, f16[32,40,128]{2,1,0:T(8,128)(2,1)S(1)}, u32[]{:S(2)}, u32[]{:S(2)}) collective-permute-start(f16[32,40,128]{2,1,0:T(8,128)(2,1)S(1)} %get-tuple-element.62), channel_id=1, source_target_pairs={{0,3},{1,0},{2,1},{3,2},{4,7},{5,4},{6,5},{7,6},{8,11},{9,8},{10,9... | collective-permute-start | bytes 983048 | tf_op jit(solution)/shard_map/ppermute | solution.py:505
  92.7 10.8 %invert_factor.1.inverse_ref = f32[256,256]{1,0:T(8,128)S(1)} custom-call(s32[1]{0:T(128)} %bitcast.1.spot_ref, f32[64,256]{1,0:T(8,128)S(1)} %gram_rows.1.refs_0_, f32[64,256]{1,0:T(8,128)S(1)} %collective-permute-done.11.refs_1_, f32[64,256]{1,0:T(8,128)S(1)} %collective-permute-done.12.refs_2_, f32[64,256]{1,0:T(8,128)S(1)} %collective-permute-done.13.refs_3_), custom_call_target="tpu_custom_call" | custom-call | flops 20000000000 | bytes 524288 | tf_op jit(solution)/shard_map/invert_factor/pallas_call | solution.py:140
  103.6 2.7 %moment_of.1.moment_ref = f32[256,256]{1,0:T(8,128)S(1)} custom-call(f32[32,40,128]{2,1,0:T(8,128)S(1)} %get-tuple-element.49.refs_0_, f32[32,40,128]{2,1,0:T(8,128)S(1)} %convert_element_type.53.refs_1_, f32[32,40,128]{2,1,0:T(8,128)S(1)} %convert_element_type.54.refs_2_, f32[32,40,128]{2,1,0:T(8,128)S(1)} %convert_element_type.55.refs_3_), custom_call_target="tpu_custom_call" | custom-call | flops 4000000000 | bytes 2359296 | tf_op jit(solution)/shard_map/moment_of/pallas_call | solution.py:163
  106.4 1.5 collective-permute-done.17.other_ref
  108.0 7.0 %project_half.1.basis_ref = bf16[2048,256]{1,0:T(8,128)(2,1)S(1)} custom-call(s32[1]{0:T(128)} %bitcast.1.spot_ref, f32[256,256]{1,0:T(8,128)S(1)} %invert_factor.1.inverse_ref, f32[256,256]{1,0:T(8,128)S(1)} %moment_of.1.moment_ref, f32[256,256]{1,0:T(8,128)S(1)} %collective-permute-done.17.other_ref, f32[32,40,128]{2,1,0:T(8,128)S(1)} %get-tuple-element.49.refs_0_, ...), custom_call_target="tpu_custom_call" | custom-call | flops 12000000000 | bytes 4194304 | tf_op jit(solution)/shard_map/project_half/pallas_call | solution.py:203
  115.4 1.5 product_of_half.2.refs_0_
  118.0 1.5 product_of_half.3.own_ref
  119.7 1.6 collective-permute-done.19.other_ref
  121.3 3.5 %place_rows.1 = bf16[64,48,256]{2,1,0:T(8,128)(2,1)} custom-call(s32[3]{0:T(128)S(1)} %pad_add_fusion.spot_ref.core_ref, s32[1,768]{1,0:T(1,128)S(1)} %compare_select_fusion.1.own_target, s32[1,768]{1,0:T(1,128)S(1)} %compare_select_fusion.other_target, bf16[768,256]{1,0:T(8,128)(2,1)S(1)} %product_of_half.3.own_ref, ...), custom_call_target="tpu_custom_call" | custom-call | flops 1207959552 | bytes 3145728 | tf_op jit(solution)/shard_map/place_rows/pallas_call | solution.py:485
  124.8 9.4 %all-to-all-start.2 = ((bf16[128,24,256]{2,1,0:T(8,128)(2,1)}), bf16[128,24,256]{2,1,0:T(8,128)(2,1)S(1)}, u32[]{:S(2)}, u32[]{:S(2)}) async-start(bf16[128,24,256]{2,1,0:T(8,128)(2,1)} %bitcast.4), calls=%async_computation.2 | async-start | bytes 3145728 | tf_op jit(solution)/shard_map/all_to_all | solution.py:574
  135.1 40.7 %all-to-all-done.2 = bf16[128,24,256]{2,1,0:T(8,128)(2,1)S(1)} async-done(((bf16[128,24,256]{2,1,0:T(8,128)(2,1)}), bf16[128,24,256]{2,1,0:T(8,128)(2,1)S(1)}, u32[]{:S(2)}, u32[]{:S(2)}) %all-to-all-start.2) | async-done | bytes 1572896 | tf_op jit(solution)/shard_map/all_to_all | solution.py:574
  (65 shorter events, 16.7 us)
Async XLA Ops:
  0.6 3.9 %copy-start = (bf16[768,4096]{1,0:T(8,128)(2,1)S(1)}, bf16[768,4096]{1,0:T(8,128)(2,1)}, u32[]{:S(2)}) copy-start(bf16[768,4096]{1,0:T(8,128)(2,1)} %rows_ref.7) | copy-start | bytes 18874372
  0.6 1.4 copy-start.1
  2.0 0.9 copy-start.2
  9.9 2.9 %collective-permute-start.2 = (f32[256,640]{1,0:T(8,128)S(1)}, f32[256,640]{1,0:T(8,128)S(1)}, u32[]{:S(2)}, u32[]{:S(2)}) collective-permute-start(f32[256,640]{1,0:T(8,128)S(1)} %get-tuple-element.34), channel_id=1, source_target_pairs={{0,128},{128,0},{1,129},{129,1},{2,130},{130,2},{3,131},{131,3},{4... | collective-permute-start | bytes 1966088 | tf_op jit(solution)/shard_map/ppermute | solution.py:505
  12.1 3.8 %collective-permute-start.6 = (f32[256,640]{1,0:T(8,128)S(1)}, f32[256,640]{1,0:T(8,128)S(1)}, u32[]{:S(2)}, u32[]{:S(2)}) collective-permute-start(f32[256,640]{1,0:T(8,128)S(1)} %get-tuple-element.38), channel_id=1, source_target_pairs={{0,128},{128,0},{1,129},{129,1},{2,130},{130,2},{3,131},{131,3},{4... | collective-permute-start | bytes 1966088 | tf_op jit(solution)/shard_map/ppermute | solution.py:505
  12.7 14.7 %collective-permute-start.1 = (f32[256,640]{1,0:T(8,128)S(1)}, f32[256,640]{1,0:T(8,128)S(1)}, u32[]{:S(2)}, u32[]{:S(2)}) collective-permute-start(f32[256,640]{1,0:T(8,128)S(1)} %get-tuple-element.32), channel_id=1, source_target_pairs={{0,128},{128,0},{1,129},{129,1},{2,130},{130,2},{3,131},{131,3},{4... | collective-permute-start | bytes 1966088 | tf_op jit(solution)/shard_map/ppermute | solution.py:505
  13.0 10.4 %collective-permute-start.7 = (f32[128,640]{1,0:T(8,128)S(1)}, f32[128,640]{1,0:T(8,128)S(1)}, u32[]{:S(2)}, u32[]{:S(2)}) collective-permute-start(f32[128,640]{1,0:T(8,128)S(1)} %get-tuple-element.60), channel_id=1, source_target_pairs={{0,3},{1,0},{2,1},{3,2},{4,7},{5,4},{6,5},{7,6},{8,11},{9,8},{10,9... | collective-permute-start | bytes 983048 | tf_op jit(solution)/shard_map/ppermute | solution.py:505
  15.8 11.6 %collective-permute-start.3 = (f32[128,640]{1,0:T(8,128)S(1)}, f32[128,640]{1,0:T(8,128)S(1)}, u32[]{:S(2)}, u32[]{:S(2)}) collective-permute-start(f32[128,640]{1,0:T(8,128)S(1)} %get-tuple-element.61), channel_id=1, source_target_pairs={{0,1},{1,2},{2,3},{3,0},{4,5},{5,6},{6,7},{7,4},{8,9},{9,10},{10,1... | collective-permute-start | bytes 983048 | tf_op jit(solution)/shard_map/ppermute | solution.py:505
  15.8 22.3 %collective-permute-start = (f32[256,640]{1,0:T(8,128)S(1)}, f32[256,640]{1,0:T(8,128)S(1)}, u32[]{:S(2)}, u32[]{:S(2)}) collective-permute-start(f32[256,640]{1,0:T(8,128)S(1)} %get-tuple-element.30), channel_id=1, source_target_pairs={{0,128},{128,0},{1,129},{129,1},{2,130},{130,2},{3,131},{131,3},{4... | collective-permute-start | bytes 1966088 | tf_op jit(solution)/shard_map/ppermute | solution.py:505
  16.0 15.4 %collective-permute-start.10 = (s32[1,768]{1,0:T(1,128)S(1)}, s32[1,768]{1,0:T(1,128)S(1)}, u32[]{:S(2)}, u32[]{:S(2)}) collective-permute-start(s32[1,768]{1,0:T(1,128)S(1)} %get-tuple-element.41), channel_id=1, source_target_pairs={{0,128},{128,0},{1,129},{129,1},{2,130},{130,2},{3,131},{131,3},{4... | collective-permute-start | bytes 9224 | tf_op jit(solution)/shard_map/ppermute | solution.py:505
  23.7 10.5 %collective-permute-start.8 = (f16[256,512]{1,0:T(8,128)(2,1)S(1)}, f16[256,512]{1,0:T(8,128)(2,1)S(1)}, u32[]{:S(2)}, u32[]{:S(2)}) collective-permute-start(f16[256,512]{1,0:T(8,128)(2,1)S(1)} %convert_element_type.46), channel_id=1, source_target_pairs={{0,3},{1,0},{2,1},{3,2},{4,7},{5,4},{6,5},{7,6},{8,11},{9,8},{10,9... | collective-permute-start | bytes 786440 | tf_op jit(solution)/shard_map/ppermute | solution.py:505
  27.7 10.3 %collective-permute-start.4 = (f16[256,512]{1,0:T(8,128)(2,1)S(1)}, f16[256,512]{1,0:T(8,128)(2,1)S(1)}, u32[]{:S(2)}, u32[]{:S(2)}) collective-permute-start(f16[256,512]{1,0:T(8,128)(2,1)S(1)} %convert_element_type.44), channel_id=1, source_target_pairs={{0,1},{1,2},{2,3},{3,0},{4,5},{5,6},{6,7},{7,4},{8,9},{9,10},{10,1... | collective-permute-start | bytes 786440 | tf_op jit(solution)/shard_map/ppermute | solution.py:505
  27.9 10.2 %collective-permute-start.9 = (f32[256,128]{1,0:T(8,128)S(1)}, f32[256,128]{1,0:T(8,128)S(1)}, u32[]{:S(2)}, u32[]{:S(2)}) collective-permute-start(f32[256,128]{1,0:T(8,128)S(1)} %get-tuple-element.40), channel_id=1, source_target_pairs={{0,3},{1,0},{2,1},{3,2},{4,7},{5,4},{6,5},{7,6},{8,11},{9,8},{10,9... | collective-permute-start | bytes 393224 | tf_op jit(solution)/shard_map/ppermute | solution.py:505
  31.4 8.0 %collective-permute-start.5 = (f32[256,128]{1,0:T(8,128)S(1)}, f32[256,128]{1,0:T(8,128)S(1)}, u32[]{:S(2)}, u32[]{:S(2)}) collective-permute-start(f32[256,128]{1,0:T(8,128)S(1)} %get-tuple-element.36), channel_id=1, source_target_pairs={{0,1},{1,2},{2,3},{3,0},{4,5},{5,6},{6,7},{7,4},{8,9},{9,10},{10,1... | collective-permute-start | bytes 393224 | tf_op jit(solution)/shard_map/ppermute | solution.py:505
  83.6 7.0 %collective-permute-start.11 = (f32[64,256]{1,0:T(8,128)S(1)}, f32[64,256]{1,0:T(8,128)S(1)}, u32[]{:S(2)}, u32[]{:S(2)}) collective-permute-start(f32[64,256]{1,0:T(8,128)S(1)} %gram_rows.1.refs_0_), channel_id=1, source_target_pairs={{0,1},{1,2},{2,3},{3,0},{4,5},{5,6},{6,7},{7,4},{8,9},{9,10},{10,1... | collective-permute-start | bytes 196616 | tf_op jit(solution)/shard_map/ppermute | solution.py:505
  83.7 9.0 %collective-permute-start.12 = (f32[64,256]{1,0:T(8,128)S(1)}, f32[64,256]{1,0:T(8,128)S(1)}, u32[]{:S(2)}, u32[]{:S(2)}) collective-permute-start(f32[64,256]{1,0:T(8,128)S(1)} %gram_rows.1.refs_0_), channel_id=1, source_target_pairs={{0,2},{1,3},{2,0},{3,1},{4,6},{5,7},{6,4},{7,5},{8,10},{9,11},{10,... | collective-permute-start | bytes 196616 | tf_op jit(solution)/shard_map/ppermute | solution.py:505
  85.5 7.2 %collective-permute-start.13 = (f32[64,256]{1,0:T(8,128)S(1)}, f32[64,256]{1,0:T(8,128)S(1)}, u32[]{:S(2)}, u32[]{:S(2)}) collective-permute-start(f32[64,256]{1,0:T(8,128)S(1)} %gram_rows.1.refs_0_), channel_id=1, source_target_pairs={{0,3},{1,0},{2,1},{3,2},{4,7},{5,4},{6,5},{7,6},{8,11},{9,8},{10,9... | collective-permute-start | bytes 196616 | tf_op jit(solution)/shard_map/ppermute | solution.py:505
  87.0 16.4 %collective-permute-start.14 = (f16[32,40,128]{2,1,0:T(8,128)(2,1)S(1)}, f16[32,40,128]{2,1,0:T(8,128)(2,1)S(1)}, u32[]{:S(2)}, u32[]{:S(2)}) collective-permute-start(f16[32,40,128]{2,1,0:T(8,128)(2,1)S(1)} %get-tuple-element.62), channel_id=1, source_target_pairs={{0,1},{1,2},{2,3},{3,0},{4,5},{5,6},{6,7},{7,4},{8,9},{9,10},{10,1... | collective-permute-start | bytes 983048 | tf_op jit(solution)/shard_map/ppermute | solution.py:505
  88.0 15.6 %collective-permute-start.15 = (f16[32,40,128]{2,1,0:T(8,128)(2,1)S(1)}, f16[32,40,128]{2,1,0:T(8,128)(2,1)S(1)}, u32[]{:S(2)}, u32[]{:S(2)}) collective-permute-start(f16[32,40,128]{2,1,0:T(8,128)(2,1)S(1)} %get-tuple-element.62), channel_id=1, source_target_pairs={{0,2},{1,3},{2,0},{3,1},{4,6},{5,7},{6,4},{7,5},{8,10},{9,11},{10,... | collective-permute-start | bytes 983048 | tf_op jit(solution)/shard_map/ppermute | solution.py:505
  90.7 12.9 %collective-permute-start.16 = (f16[32,40,128]{2,1,0:T(8,128)(2,1)S(1)}, f16[32,40,128]{2,1,0:T(8,128)(2,1)S(1)}, u32[]{:S(2)}, u32[]{:S(2)}) collective-permute-start(f16[32,40,128]{2,1,0:T(8,128)(2,1)S(1)} %get-tuple-element.62), channel_id=1, source_target_pairs={{0,3},{1,0},{2,1},{3,2},{4,7},{5,4},{6,5},{7,6},{8,11},{9,8},{10,9... | collective-permute-start | bytes 983048 | tf_op jit(solution)/shard_map/ppermute | solution.py:505
  106.3 1.6 collective-permute-start.17
  115.0 3.0 %collective-permute-start.18 = (bf16[2048,256]{1,0:T(8,128)(2,1)S(1)}, bf16[2048,256]{1,0:T(8,128)(2,1)S(1)}, u32[]{:S(2)}, u32[]{:S(2)}) collective-permute-start(bf16[2048,256]{1,0:T(8,128)(2,1)S(1)} %project_half.1.basis_ref), channel_id=1, source_target_pairs={{0,128},{128,0},{1,129},{129,1},{2,130},{130,2},{3,131},{131,3},{4... | collective-permute-start | bytes 3145736 | tf_op jit(solution)/shard_map/ppermute | solution.py:505
  119.5 1.8 %collective-permute-start.19 = (bf16[768,256]{1,0:T(8,128)(2,1)S(1)}, bf16[768,256]{1,0:T(8,128)(2,1)S(1)}, u32[]{:S(2)}, u32[]{:S(2)}) collective-permute-start(bf16[768,256]{1,0:T(8,128)(2,1)S(1)} %product_of_half.3.own_ref), channel_id=1, source_target_pairs={{0,128},{128,0},{1,129},{129,1},{2,130},{130,2},{3,131},{131,3},{4... | collective-permute-start | bytes 1179656 | tf_op jit(solution)/shard_map/ppermute | solution.py:505
  124.8 51.1 %all-to-all-start.2 = ((bf16[128,24,256]{2,1,0:T(8,128)(2,1)}), bf16[128,24,256]{2,1,0:T(8,128)(2,1)S(1)}, u32[]{:S(2)}, u32[]{:S(2)}) async-start(bf16[128,24,256]{2,1,0:T(8,128)(2,1)} %bitcast.4), calls=%async_computation.2 | async-start | bytes 3145728 | tf_op jit(solution)/shard_map/all_to_all | solution.py:574

commit v10 on v9

--- a/solution.py
+++ b/solution.py
@@ -152,8 +152,12 @@
 def moment_kernel(*refs):
     total = None
     for part_ref in refs[:-1]:
-        part = plain_rows(part_ref)
-        term = dot_f32(part, part, ROW_DIMS)
+        high, low = split_two(plain_rows(part_ref))
+        mul = functools.partial(
+            lax.dot_general, dimension_numbers=ROW_DIMS, preferred_element_type=jnp.float32
+        )
+        mixed = mul(high, low)
+        term = mul(high, high) + ((mixed + mixed.T) + mul(low, low))
         total = term if total is None else total + term
     refs[-1][...] = total
 
@@ -480,7 +484,7 @@
 
 
 def place_rows(core, targets, own, other, chips, capacity):
-    pairs = 16
+    pairs = 32
     depth, width = own.shape
     return pl.pallas_call(
         functools.partial(place_kernel, capacity),

time: 178 us -> 176 us (0.989)
  no operation moved by 1% of the time
where the time goes in v10:
time: 176 us
  waiting for transfers between devices  60.3 us (34%)
  blocking collectives  42.3 us (24%)
  Pallas kernels  32.5 us (18%)
  starting transfers between devices  30 us (17%)
  local copies, waits for them, and re-layouts  4.92 us (3%)
  matrix products  4.03 us (2%)
    all_to_all x1, waiting for transfers between devices, local(): arrived = lax.all_to_all(send_rows, ('y', 'z', 'x'), 0, 0, tiled=True)  40.7 us
    all_to_all x1, blocking collectives, local(): packed = lax.all_to_all(packed.astype(jnp.float16), PLANE, 0, 0, tiled=True)  24.8 us
    ppermute x20, starting transfers between devices, shift(): lax.ppermute(value, axis, [(i, (i + step) % size) for i in range(size)])  20.6 us
    ppermute x20, waiting for transfers between devices, shift(): lax.ppermute(value, axis, [(i, (i + step) % size) for i in range(size)])  19.5 us
    all_to_all x1, blocking collectives, local(): packed = lax.all_to_all(packed, PLANE, 0, 0, tiled=True)  17.6 us
    pallas_call x1, Pallas kernels, invert_factor(): pl.pallas_call(invert_kernel, in_specs=[pl.BlockSpec(memory_space=pltpu.S...  10.8 us
    all_to_all x1, starting transfers between devices, local(): arrived = lax.all_to_all(send_rows, ('y', 'z', 'x'), 0, 0, tiled=True)  9.39 us
    pallas_call x1, Pallas kernels, project_half(): pl.pallas_call(whiten_kernel, in_specs=[pl.BlockSpec(memory_space=pltpu.S...  6.99 us
  transfers between devices with their start and end apart: 21, of which 9 were waited for; matrix products, arithmetic and copies ran while one was open for 1% of the time, Pallas kernels for 8%

profile of v10, /device:TPU:32, one launch (start us, length us, event | category | flops | bytes accessed | tf_op | source)
XLA Modules:
  0.0 175.9 jit_solution(6039664832541762398)
XLA Ops:
  3.0 1.6 route_rows.1
  4.5 4.0 %fusion.2.sketch_ref = bf16[768,256]{1,0:T(8,128)(2,1)S(1)} fusion(bf16[768,4096]{1,0:T(8,128)(2,1)S(1)} %copy-done, s32[4096,256]{1,0:T(8,128)} %param.5), kind=kOutput, calls=%fused_computation.2 | convolution fusion | flops 1611857920 | bytes 10878976 | tf_op jit(solution)/shard_map/dot_general | solution.py:523
  10.0 2.1 %cross_chunks.2 = (f32[256,640]{1,0:T(8,128)S(1)}, f32[256,640]{1,0:T(8,128)S(1)}, f32[256,640]{1,0:T(8,128)S(1)}, f32[256,640]{1,0:T(8,128)S(1)}, f32[256,640]{1,0:T(8,128)S(1)}, /*index=5*/f32[256,640]{1,0:T(8,128)S(1)}) custom-call(s32[3]{0:T(128)S(1)} %pad_add_fusion.spot_ref.core_ref, bf16[768,4096]{1,0:T(8,128)(2,1)S(1)} %copy-done, ...), custom_call_target="tpu_custom_call" | custom-call | flops 1207959552 | bytes 3000000 | tf_op jit(solution)/shard_map/cross_chunks/pallas_call | solution.py:248
  13.0 2.8 %collective-permute-start.7 = (f32[128,640]{1,0:T(8,128)S(1)}, f32[128,640]{1,0:T(8,128)S(1)}, u32[]{:S(2)}, u32[]{:S(2)}) collective-permute-start(f32[128,640]{1,0:T(8,128)S(1)} %get-tuple-element.60), channel_id=1, source_target_pairs={{0,3},{1,0},{2,1},{3,2},{4,7},{5,4},{6,5},{7,6},{8,11},{9,8},{10,9... | collective-permute-start | bytes 983048 | tf_op jit(solution)/shard_map/ppermute | solution.py:509
  16.3 7.0 %collective-permute-done.7.extra_ref = f32[128,640]{1,0:T(8,128)S(1)} collective-permute-done((f32[128,640]{1,0:T(8,128)S(1)}, f32[128,640]{1,0:T(8,128)S(1)}, u32[]{:S(2)}, u32[]{:S(2)}) %collective-permute-start.7) | collective-permute-done | bytes 327712 | tf_op jit(solution)/shard_map/ppermute | solution.py:509
  23.7 3.8 %collective-permute-start.8 = (f16[256,512]{1,0:T(8,128)(2,1)S(1)}, f16[256,512]{1,0:T(8,128)(2,1)S(1)}, u32[]{:S(2)}, u32[]{:S(2)}) collective-permute-start(f16[256,512]{1,0:T(8,128)(2,1)S(1)} %convert_element_type.46), channel_id=1, source_target_pairs={{0,3},{1,0},{2,1},{3,2},{4,7},{5,4},{6,5},{7,6},{8,11},{9,8},{10,9... | collective-permute-start | bytes 786440 | tf_op jit(solution)/shard_map/ppermute | solution.py:509
  27.9 3.5 %collective-permute-start.9 = (f32[256,128]{1,0:T(8,128)S(1)}, f32[256,128]{1,0:T(8,128)S(1)}, u32[]{:S(2)}, u32[]{:S(2)}) collective-permute-start(f32[256,128]{1,0:T(8,128)S(1)} %get-tuple-element.40), channel_id=1, source_target_pairs={{0,3},{1,0},{2,1},{3,2},{4,7},{5,4},{6,5},{7,6},{8,11},{9,8},{10,9... | collective-permute-start | bytes 393224 | tf_op jit(solution)/shard_map/ppermute | solution.py:509
  31.4 2.7 %collective-permute-done.8 = f16[256,512]{1,0:T(8,128)(2,1)S(1)} collective-permute-done((f16[256,512]{1,0:T(8,128)(2,1)S(1)}, f16[256,512]{1,0:T(8,128)(2,1)S(1)}, u32[]{:S(2)}, u32[]{:S(2)}) %collective-permute-start.8) | collective-permute-done | bytes 262176 | tf_op jit(solution)/shard_map/ppermute | solution.py:509
  34.2 3.8 %collective-permute-done.4 = f16[256,512]{1,0:T(8,128)(2,1)S(1)} collective-permute-done((f16[256,512]{1,0:T(8,128)(2,1)S(1)}, f16[256,512]{1,0:T(8,128)(2,1)S(1)}, u32[]{:S(2)}, u32[]{:S(2)}) %collective-permute-start.4) | collective-permute-done | bytes 262176 | tf_op jit(solution)/shard_map/ppermute | solution.py:509
  40.1 24.8 %all_to_all.15 = f16[32,48,128]{2,1,0:T(8,128)(2,1)S(1)} all-to-all(f16[32,48,128]{2,1,0:T(8,128)(2,1)S(1)} %convert_element_type.48), channel_id=1, replica_groups=mesh['narrow'=2,'y'=4,'z'=8,'x'=4] {'y','z'}, dimensions={0} | all-to-all | bytes 786432 | tf_op jit(solution)/shard_map/all_to_all | solution.py:554
  65.7 17.6 %all_to_all.16 = f16[32,48,128]{2,1,0:T(8,128)(2,1)S(1)} all-to-all(f16[32,48,128]{2,1,0:T(8,128)(2,1)S(1)} %broadcast_in_dim.5), channel_id=1, replica_groups=mesh['narrow'=2,'y'=4,'z'=8,'x'=4] {'y','z'}, dimensions={0} | all-to-all | bytes 786432 | tf_op jit(solution)/shard_map/all_to_all | solution.py:558
  83.7 1.8 collective-permute-start.12
  88.0 2.2 %collective-permute-start.15 = (f16[32,40,128]{2,1,0:T(8,128)(2,1)S(1)}, f16[32,40,128]{2,1,0:T(8,128)(2,1)S(1)}, u32[]{:S(2)}, u32[]{:S(2)}) collective-permute-start(f16[32,40,128]{2,1,0:T(8,128)(2,1)S(1)} %get-tuple-element.62), channel_id=1, source_target_pairs={{0,2},{1,3},{2,0},{3,1},{4,6},{5,7},{6,4},{7,5},{8,10},{9,11},{10,... | collective-permute-start | bytes 983048 | tf_op jit(solution)/shard_map/ppermute | solution.py:509
  90.7 2.0 %collective-permute-start.16 = (f16[32,40,128]{2,1,0:T(8,128)(2,1)S(1)}, f16[32,40,128]{2,1,0:T(8,128)(2,1)S(1)}, u32[]{:S(2)}, u32[]{:S(2)}) collective-permute-start(f16[32,40,128]{2,1,0:T(8,128)(2,1)S(1)} %get-tuple-element.62), channel_id=1, source_target_pairs={{0,3},{1,0},{2,1},{3,2},{4,7},{5,4},{6,5},{7,6},{8,11},{9,8},{10,9... | collective-permute-start | bytes 983048 | tf_op jit(solution)/shard_map/ppermute | solution.py:509
  92.7 10.8 %invert_factor.1.inverse_ref = f32[256,256]{1,0:T(8,128)S(1)} custom-call(s32[1]{0:T(128)} %bitcast.1.spot_ref, f32[64,256]{1,0:T(8,128)S(1)} %gram_rows.1.refs_0_, f32[64,256]{1,0:T(8,128)S(1)} %collective-permute-done.11.refs_1_, f32[64,256]{1,0:T(8,128)S(1)} %collective-permute-done.12.refs_2_, f32[64,256]{1,0:T(8,128)S(1)} %collective-permute-done.13.refs_3_), custom_call_target="tpu_custom_call" | custom-call | flops 20000000000 | bytes 524288 | tf_op jit(solution)/shard_map/invert_factor/pallas_call | solution.py:140
  103.6 1.6 moment_of.1.moment_ref
  105.6 1.5 collective-permute-done.17.other_ref
  107.1 7.0 %project_half.1.basis_ref = bf16[2048,256]{1,0:T(8,128)(2,1)S(1)} custom-call(s32[1]{0:T(128)} %bitcast.1.spot_ref, f32[256,256]{1,0:T(8,128)S(1)} %invert_factor.1.inverse_ref, f32[256,256]{1,0:T(8,128)S(1)} %moment_of.1.moment_ref, f32[256,256]{1,0:T(8,128)S(1)} %collective-permute-done.17.other_ref, f32[32,40,128]{2,1,0:T(8,128)S(1)} %get-tuple-element.49.refs_0_, ...), custom_call_target="tpu_custom_call" | custom-call | flops 12000000000 | bytes 4194304 | tf_op jit(solution)/shard_map/project_half/pallas_call | solution.py:207
  114.3 1.5 product_of_half.2.refs_0_
  116.8 1.5 product_of_half.3.own_ref
  118.6 1.6 collective-permute-done.19.other_ref
  120.2 3.0 %place_rows.1 = bf16[64,48,256]{2,1,0:T(8,128)(2,1)} custom-call(s32[3]{0:T(128)S(1)} %pad_add_fusion.spot_ref.core_ref, s32[1,768]{1,0:T(1,128)S(1)} %compare_select_fusion.1.own_target, s32[1,768]{1,0:T(1,128)S(1)} %compare_select_fusion.other_target, bf16[768,256]{1,0:T(8,128)(2,1)S(1)} %product_of_half.3.own_ref, ...), custom_call_target="tpu_custom_call" | custom-call | flops 1207959552 | bytes 3145728 | tf_op jit(solution)/shard_map/place_rows/pallas_call | solution.py:489
  123.2 9.4 %all-to-all-start.2 = ((bf16[128,24,256]{2,1,0:T(8,128)(2,1)}), bf16[128,24,256]{2,1,0:T(8,128)(2,1)S(1)}, u32[]{:S(2)}, u32[]{:S(2)}) async-start(bf16[128,24,256]{2,1,0:T(8,128)(2,1)} %bitcast.4), calls=%async_computation.2 | async-start | bytes 3145728 | tf_op jit(solution)/shard_map/all_to_all | solution.py:578
  133.5 40.7 %all-to-all-done.2 = bf16[128,24,256]{2,1,0:T(8,128)(2,1)S(1)} async-done(((bf16[128,24,256]{2,1,0:T(8,128)(2,1)}), bf16[128,24,256]{2,1,0:T(8,128)(2,1)S(1)}, u32[]{:S(2)}, u32[]{:S(2)}) %all-to-all-start.2) | async-done | bytes 1572896 | tf_op jit(solution)/shard_map/all_to_all | solution.py:578
  (65 shorter events, 16.7 us)
Async XLA Ops:
  0.6 3.9 %copy-start = (bf16[768,4096]{1,0:T(8,128)(2,1)S(1)}, bf16[768,4096]{1,0:T(8,128)(2,1)}, u32[]{:S(2)}) copy-start(bf16[768,4096]{1,0:T(8,128)(2,1)} %rows_ref.7) | copy-start | bytes 18874372
  0.6 1.4 copy-start.1
  2.0 0.9 copy-start.2
  9.9 2.9 %collective-permute-start.2 = (f32[256,640]{1,0:T(8,128)S(1)}, f32[256,640]{1,0:T(8,128)S(1)}, u32[]{:S(2)}, u32[]{:S(2)}) collective-permute-start(f32[256,640]{1,0:T(8,128)S(1)} %get-tuple-element.34), channel_id=1, source_target_pairs={{0,128},{128,0},{1,129},{129,1},{2,130},{130,2},{3,131},{131,3},{4... | collective-permute-start | bytes 1966088 | tf_op jit(solution)/shard_map/ppermute | solution.py:509
  12.1 3.8 %collective-permute-start.6 = (f32[256,640]{1,0:T(8,128)S(1)}, f32[256,640]{1,0:T(8,128)S(1)}, u32[]{:S(2)}, u32[]{:S(2)}) collective-permute-start(f32[256,640]{1,0:T(8,128)S(1)} %get-tuple-element.38), channel_id=1, source_target_pairs={{0,128},{128,0},{1,129},{129,1},{2,130},{130,2},{3,131},{131,3},{4... | collective-permute-start | bytes 1966088 | tf_op jit(solution)/shard_map/ppermute | solution.py:509
  12.7 14.7 %collective-permute-start.1 = (f32[256,640]{1,0:T(8,128)S(1)}, f32[256,640]{1,0:T(8,128)S(1)}, u32[]{:S(2)}, u32[]{:S(2)}) collective-permute-start(f32[256,640]{1,0:T(8,128)S(1)} %get-tuple-element.32), channel_id=1, source_target_pairs={{0,128},{128,0},{1,129},{129,1},{2,130},{130,2},{3,131},{131,3},{4... | collective-permute-start | bytes 1966088 | tf_op jit(solution)/shard_map/ppermute | solution.py:509
  13.0 10.4 %collective-permute-start.7 = (f32[128,640]{1,0:T(8,128)S(1)}, f32[128,640]{1,0:T(8,128)S(1)}, u32[]{:S(2)}, u32[]{:S(2)}) collective-permute-start(f32[128,640]{1,0:T(8,128)S(1)} %get-tuple-element.60), channel_id=1, source_target_pairs={{0,3},{1,0},{2,1},{3,2},{4,7},{5,4},{6,5},{7,6},{8,11},{9,8},{10,9... | collective-permute-start | bytes 983048 | tf_op jit(solution)/shard_map/ppermute | solution.py:509
  15.8 11.6 %collective-permute-start.3 = (f32[128,640]{1,0:T(8,128)S(1)}, f32[128,640]{1,0:T(8,128)S(1)}, u32[]{:S(2)}, u32[]{:S(2)}) collective-permute-start(f32[128,640]{1,0:T(8,128)S(1)} %get-tuple-element.61), channel_id=1, source_target_pairs={{0,1},{1,2},{2,3},{3,0},{4,5},{5,6},{6,7},{7,4},{8,9},{9,10},{10,1... | collective-permute-start | bytes 983048 | tf_op jit(solution)/shard_map/ppermute | solution.py:509
  15.8 22.3 %collective-permute-start = (f32[256,640]{1,0:T(8,128)S(1)}, f32[256,640]{1,0:T(8,128)S(1)}, u32[]{:S(2)}, u32[]{:S(2)}) collective-permute-start(f32[256,640]{1,0:T(8,128)S(1)} %get-tuple-element.30), channel_id=1, source_target_pairs={{0,128},{128,0},{1,129},{129,1},{2,130},{130,2},{3,131},{131,3},{4... | collective-permute-start | bytes 1966088 | tf_op jit(solution)/shard_map/ppermute | solution.py:509
  16.0 15.4 %collective-permute-start.10 = (s32[1,768]{1,0:T(1,128)S(1)}, s32[1,768]{1,0:T(1,128)S(1)}, u32[]{:S(2)}, u32[]{:S(2)}) collective-permute-start(s32[1,768]{1,0:T(1,128)S(1)} %get-tuple-element.41), channel_id=1, source_target_pairs={{0,128},{128,0},{1,129},{129,1},{2,130},{130,2},{3,131},{131,3},{4... | collective-permute-start | bytes 9224 | tf_op jit(solution)/shard_map/ppermute | solution.py:509
  23.7 10.5 %collective-permute-start.8 = (f16[256,512]{1,0:T(8,128)(2,1)S(1)}, f16[256,512]{1,0:T(8,128)(2,1)S(1)}, u32[]{:S(2)}, u32[]{:S(2)}) collective-permute-start(f16[256,512]{1,0:T(8,128)(2,1)S(1)} %convert_element_type.46), channel_id=1, source_target_pairs={{0,3},{1,0},{2,1},{3,2},{4,7},{5,4},{6,5},{7,6},{8,11},{9,8},{10,9... | collective-permute-start | bytes 786440 | tf_op jit(solution)/shard_map/ppermute | solution.py:509
  27.7 10.3 %collective-permute-start.4 = (f16[256,512]{1,0:T(8,128)(2,1)S(1)}, f16[256,512]{1,0:T(8,128)(2,1)S(1)}, u32[]{:S(2)}, u32[]{:S(2)}) collective-permute-start(f16[256,512]{1,0:T(8,128)(2,1)S(1)} %convert_element_type.44), channel_id=1, source_target_pairs={{0,1},{1,2},{2,3},{3,0},{4,5},{5,6},{6,7},{7,4},{8,9},{9,10},{10,1... | collective-permute-start | bytes 786440 | tf_op jit(solution)/shard_map/ppermute | solution.py:509
  27.9 10.2 %collective-permute-start.9 = (f32[256,128]{1,0:T(8,128)S(1)}, f32[256,128]{1,0:T(8,128)S(1)}, u32[]{:S(2)}, u32[]{:S(2)}) collective-permute-start(f32[256,128]{1,0:T(8,128)S(1)} %get-tuple-element.40), channel_id=1, source_target_pairs={{0,3},{1,0},{2,1},{3,2},{4,7},{5,4},{6,5},{7,6},{8,11},{9,8},{10,9... | collective-permute-start | bytes 393224 | tf_op jit(solution)/shard_map/ppermute | solution.py:509
  31.4 8.0 %collective-permute-start.5 = (f32[256,128]{1,0:T(8,128)S(1)}, f32[256,128]{1,0:T(8,128)S(1)}, u32[]{:S(2)}, u32[]{:S(2)}) collective-permute-start(f32[256,128]{1,0:T(8,128)S(1)} %get-tuple-element.36), channel_id=1, source_target_pairs={{0,1},{1,2},{2,3},{3,0},{4,5},{5,6},{6,7},{7,4},{8,9},{9,10},{10,1... | collective-permute-start | bytes 393224 | tf_op jit(solution)/shard_map/ppermute | solution.py:509
  83.6 7.0 %collective-permute-start.11 = (f32[64,256]{1,0:T(8,128)S(1)}, f32[64,256]{1,0:T(8,128)S(1)}, u32[]{:S(2)}, u32[]{:S(2)}) collective-permute-start(f32[64,256]{1,0:T(8,128)S(1)} %gram_rows.1.refs_0_), channel_id=1, source_target_pairs={{0,1},{1,2},{2,3},{3,0},{4,5},{5,6},{6,7},{7,4},{8,9},{9,10},{10,1... | collective-permute-start | bytes 196616 | tf_op jit(solution)/shard_map/ppermute | solution.py:509
  83.7 9.0 %collective-permute-start.12 = (f32[64,256]{1,0:T(8,128)S(1)}, f32[64,256]{1,0:T(8,128)S(1)}, u32[]{:S(2)}, u32[]{:S(2)}) collective-permute-start(f32[64,256]{1,0:T(8,128)S(1)} %gram_rows.1.refs_0_), channel_id=1, source_target_pairs={{0,2},{1,3},{2,0},{3,1},{4,6},{5,7},{6,4},{7,5},{8,10},{9,11},{10,... | collective-permute-start | bytes 196616 | tf_op jit(solution)/shard_map/ppermute | solution.py:509
  85.5 7.2 %collective-permute-start.13 = (f32[64,256]{1,0:T(8,128)S(1)}, f32[64,256]{1,0:T(8,128)S(1)}, u32[]{:S(2)}, u32[]{:S(2)}) collective-permute-start(f32[64,256]{1,0:T(8,128)S(1)} %gram_rows.1.refs_0_), channel_id=1, source_target_pairs={{0,3},{1,0},{2,1},{3,2},{4,7},{5,4},{6,5},{7,6},{8,11},{9,8},{10,9... | collective-permute-start | bytes 196616 | tf_op jit(solution)/shard_map/ppermute | solution.py:509
  87.0 16.4 %collective-permute-start.14 = (f16[32,40,128]{2,1,0:T(8,128)(2,1)S(1)}, f16[32,40,128]{2,1,0:T(8,128)(2,1)S(1)}, u32[]{:S(2)}, u32[]{:S(2)}) collective-permute-start(f16[32,40,128]{2,1,0:T(8,128)(2,1)S(1)} %get-tuple-element.62), channel_id=1, source_target_pairs={{0,1},{1,2},{2,3},{3,0},{4,5},{5,6},{6,7},{7,4},{8,9},{9,10},{10,1... | collective-permute-start | bytes 983048 | tf_op jit(solution)/shard_map/ppermute | solution.py:509
  88.0 15.6 %collective-permute-start.15 = (f16[32,40,128]{2,1,0:T(8,128)(2,1)S(1)}, f16[32,40,128]{2,1,0:T(8,128)(2,1)S(1)}, u32[]{:S(2)}, u32[]{:S(2)}) collective-permute-start(f16[32,40,128]{2,1,0:T(8,128)(2,1)S(1)} %get-tuple-element.62), channel_id=1, source_target_pairs={{0,2},{1,3},{2,0},{3,1},{4,6},{5,7},{6,4},{7,5},{8,10},{9,11},{10,... | collective-permute-start | bytes 983048 | tf_op jit(solution)/shard_map/ppermute | solution.py:509
  90.7 12.9 %collective-permute-start.16 = (f16[32,40,128]{2,1,0:T(8,128)(2,1)S(1)}, f16[32,40,128]{2,1,0:T(8,128)(2,1)S(1)}, u32[]{:S(2)}, u32[]{:S(2)}) collective-permute-start(f16[32,40,128]{2,1,0:T(8,128)(2,1)S(1)} %get-tuple-element.62), channel_id=1, source_target_pairs={{0,3},{1,0},{2,1},{3,2},{4,7},{5,4},{6,5},{7,6},{8,11},{9,8},{10,9... | collective-permute-start | bytes 983048 | tf_op jit(solution)/shard_map/ppermute | solution.py:509
  105.2 1.8 %collective-permute-start.17 = (f32[256,256]{1,0:T(8,128)S(1)}, f32[256,256]{1,0:T(8,128)S(1)}, u32[]{:S(2)}, u32[]{:S(2)}) collective-permute-start(f32[256,256]{1,0:T(8,128)S(1)} %moment_of.1.moment_ref), channel_id=1, source_target_pairs={{0,128},{128,0},{1,129},{129,1},{2,130},{130,2},{3,131},{131,3},{4... | collective-permute-start | bytes 786440 | tf_op jit(solution)/shard_map/ppermute | solution.py:509
  114.1 2.7 %collective-permute-start.18 = (bf16[2048,256]{1,0:T(8,128)(2,1)S(1)}, bf16[2048,256]{1,0:T(8,128)(2,1)S(1)}, u32[]{:S(2)}, u32[]{:S(2)}) collective-permute-start(bf16[2048,256]{1,0:T(8,128)(2,1)S(1)} %project_half.1.basis_ref), channel_id=1, source_target_pairs={{0,128},{128,0},{1,129},{129,1},{2,130},{130,2},{3,131},{131,3},{4... | collective-permute-start | bytes 3145736 | tf_op jit(solution)/shard_map/ppermute | solution.py:509
  118.4 1.8 %collective-permute-start.19 = (bf16[768,256]{1,0:T(8,128)(2,1)S(1)}, bf16[768,256]{1,0:T(8,128)(2,1)S(1)}, u32[]{:S(2)}, u32[]{:S(2)}) collective-permute-start(bf16[768,256]{1,0:T(8,128)(2,1)S(1)} %product_of_half.3.own_ref), channel_id=1, source_target_pairs={{0,128},{128,0},{1,129},{129,1},{2,130},{130,2},{3,131},{131,3},{4... | collective-permute-start | bytes 1179656 | tf_op jit(solution)/shard_map/ppermute | solution.py:509
  123.2 51.1 %all-to-all-start.2 = ((bf16[128,24,256]{2,1,0:T(8,128)(2,1)}), bf16[128,24,256]{2,1,0:T(8,128)(2,1)S(1)}, u32[]{:S(2)}, u32[]{:S(2)}) async-start(bf16[128,24,256]{2,1,0:T(8,128)(2,1)} %bitcast.4), calls=%async_computation.2 | async-start | bytes 3145728 | tf_op jit(solution)/shard_map/all_to_all | solution.py:578
